TPU v7x, 512 devices: a whole 4x4x16 slice. The times are simulated.
512 devices in a mesh: rows: 128 (over y_lo, z, x), cols: 4 (over y_hi, core).
Axes of the slice: x: 4, y: 4 (y_hi: 2, y_lo: 2; y = y_hi * 2 + y_lo), z: 16, core: 2. Of those that a mesh axis runs over, the one named last changes fastest.
Arguments:
- level1_basis: float32 [98304, 256], P('rows'), may hold values from -6 to 6
- level2_basis: float32 [256, 98304], P('cols', 'rows'), may hold values from -6 to 6
- probes: float32 [98304, 2048], P('rows', 'cols'), may hold values from -6 to 6
Outputs:
- solution: float32 [98304, 2048], P('rows', 'cols')
- updated_basis: float32 [256, 98304], P('cols', 'rows')
All inputs are finite; a program needn't handle non-finite values.
Results may differ from a plain program's by a relative error of at most 0.0003.
Values sent between devices are 32-bit elements; how exact they have to be, the bound alone decides.
No kernel may reach another device: no remote copies, remote signals or barrier semaphores. Data moves between devices by JAX's collectives and lax.ppermute only.
A program may use at most 64 MiB of HBM per device.

v0:
```python
import jax
import jax.numpy as jnp
from jax import lax
from jax.sharding import PartitionSpec as P

PRECISE = lax.Precision.HIGHEST


def partner(value, axis, bit):
    return lax.ppermute(value, axis, [(i, i ^ 1 << bit) for i in range(lax.axis_size(axis))])


def coupling_inverse(basis_rank, leaf_count):
    identity = jnp.eye(basis_rank, dtype=jnp.float32)
    upper_rows = jnp.concatenate([2.0 * identity, -identity], axis=1)
    lower_rows = jnp.concatenate([-identity, 2.0 * identity], axis=1)
    return jnp.concatenate([upper_rows, lower_rows], axis=0) * (leaf_count / 3.0)


def capacity_solve(gram_own, gram_other, rhs_own, rhs_other, upper_half, leaf_count):
    basis_rank = gram_own.shape[0]
    gram_low = jnp.where(upper_half == 1, gram_other, gram_own)
    gram_high = jnp.where(upper_half == 1, gram_own, gram_other)
    rhs_low = jnp.where(upper_half == 1, rhs_other, rhs_own)
    rhs_high = jnp.where(upper_half == 1, rhs_own, rhs_other)
    zero_block = jnp.zeros_like(gram_own)
    capacitance = coupling_inverse(basis_rank, leaf_count) + jnp.concatenate(
        [
            jnp.concatenate([gram_low, zero_block], axis=1),
            jnp.concatenate([zero_block, gram_high], axis=1),
        ],
        axis=0,
    )
    factor = jnp.linalg.cholesky(capacitance)
    stacked = jax.scipy.linalg.cho_solve(
        (factor, True), jnp.concatenate([rhs_low, rhs_high], axis=0)
    )
    return jnp.where(upper_half == 1, stacked[basis_rank:], stacked[:basis_rank])


def shards(level1_basis, level2_basis, probes):
    leaf_count = level1_basis.shape[0]
    position = lax.axis_index("rows")
    first_bit = position % 2
    second_bit = position // 2 % 2
    basis_two = lax.all_gather(level2_basis, "cols", axis=0, tiled=True)
    gram_one = jnp.einsum("lr,ls->rs", level1_basis, level1_basis, precision=PRECISE)
    basis_count = level2_basis.shape[0]
    rhs_basis = jnp.einsum("lr,kl->rk", level1_basis, level2_basis, precision=PRECISE)
    rhs_probe = jnp.einsum("lr,lk->rk", level1_basis, probes, precision=PRECISE)
    rhs_one = jnp.concatenate([rhs_basis, rhs_probe], axis=1)
    other_gram, other_rhs = partner((gram_one, rhs_one), "rows", 0)
    solved_one = capacity_solve(gram_one, other_gram, rhs_one, other_rhs, first_bit, leaf_count)
    updated_part = level2_basis - jnp.einsum(
        "rk,lr->kl", solved_one[:, :basis_count], level1_basis, precision=PRECISE
    )
    probe_one = probes - jnp.einsum(
        "lr,rk->lk", level1_basis, solved_one[:, basis_count:], precision=PRECISE
    )
    updated_full = lax.all_gather(updated_part, "cols", axis=0, tiled=True)
    gram_two = jnp.einsum("al,bl->ab", basis_two, updated_full, precision=PRECISE)
    rhs_two = jnp.einsum("al,lk->ak", basis_two, probe_one, precision=PRECISE)
    pair_gram, pair_rhs = partner((gram_two, rhs_two), "rows", 0)
    half_gram = gram_two + pair_gram
    half_rhs = rhs_two + pair_rhs
    far_gram, far_rhs = partner((half_gram, half_rhs), "rows", 1)
    solved_two = capacity_solve(half_gram, far_gram, half_rhs, far_rhs, second_bit, leaf_count)
    solution = probe_one - jnp.einsum("al,ak->lk", updated_full, solved_two, precision=PRECISE)
    return (solution, updated_part)


def solution(mesh):
    return jax.shard_map(
        shards,
        mesh=mesh,
        in_specs=(P("rows", None), P("cols", "rows"), P("rows", "cols")),
        out_specs=(P("rows", "cols"), P("cols", "rows")),
        check_vma=False,
    )
```

profile of v0, /device:TPU:6, one launch (start us, length us, event | category | flops | bytes accessed | tf_op | source)
XLA Modules:
  0.0 427.9 jit_solution(1319488633317864175)
XLA Ops:
  3.9 2.9 collective-permute-start
  11.0 3.1 collective-permute-start.1
  15.8 10.5 %all_gather.7 = f32[256,768]{1,0:T(8,128)S(1)} all-gather(f32[64,768]{1,0:T(8,128)S(1)} %copy-done.21), channel_id=1, replica_groups=mesh['rows'=128,'cols'=4] {'cols'}, dimensions={0}, use_global_device_ids=true | all-gather | bytes 983040 | tf_op jit(solution)/shard_map/all_gather | solution.py:46
  28.7 2.6 copy.25
  33.7 11.7 %cholesky.286 = f32[128,128]{1,0:T(8,128)S(1)} custom-call(f32[128,128]{1,0:T(8,128)S(1)} %cholesky.426), custom_call_target="Cholesky" | custom-call | tf_op jit(solution)/shard_map/jit(cholesky)/cholesky | solution.py:34
  45.6 9.8 %custom-call.39 = f32[1,128,128]{1,2,0:T(8,128)S(1)} custom-call(f32[1,128,128]{2,1,0:T(8,128)S(1)} %get-tuple-element.70), custom_call_target="InvertDiagBlocksLowerTriangular" | custom-call | tf_op jit(solution)/shard_map/jit(cholesky)/cholesky | solution.py:34
  57.9 11.7 %cholesky.305 = f32[128,128]{1,0:T(8,128)S(1)} custom-call(f32[128,128]{1,0:T(8,128)S(1)} %cholesky.430), custom_call_target="Cholesky" | custom-call | tf_op jit(solution)/shard_map/jit(cholesky)/cholesky | solution.py:34
  71.0 10.2 %custom-call.40 = f32[1,128,128]{1,2,0:T(8,128)S(1)} custom-call(f32[1,128,128]{2,1,0:T(8,128)S(1)} %get-tuple-element.67), custom_call_target="InvertDiagBlocksLowerTriangular" | custom-call | tf_op jit(solution)/shard_map/jit(cholesky)/cholesky | solution.py:34
  82.7 11.7 %cholesky.326 = f32[128,128]{1,0:T(8,128)S(1)} custom-call(f32[128,128]{1,0:T(8,128)S(1)} %cholesky.435), custom_call_target="Cholesky" | custom-call | tf_op jit(solution)/shard_map/jit(cholesky)/cholesky | solution.py:34
  95.2 9.8 %custom-call.41 = f32[1,128,128]{1,2,0:T(8,128)S(1)} custom-call(f32[1,128,128]{2,1,0:T(8,128)S(1)} %get-tuple-element.64), custom_call_target="InvertDiagBlocksLowerTriangular" | custom-call | tf_op jit(solution)/shard_map/jit(cholesky)/cholesky | solution.py:34
  106.4 11.9 %cholesky.343 = f32[128,128]{1,0:T(8,128)S(1)} custom-call(f32[128,128]{1,0:T(8,128)S(1)} %convolution_subtract_fusion.13), custom_call_target="Cholesky" | custom-call | tf_op jit(solution)/shard_map/jit(cholesky)/cholesky | solution.py:34
  122.6 11.6 %while.2 = (s32[]{:T(128)}, f32[512,512]{1,0:T(8,128)}, s32[4,2]{0,1:T(2,128)S(1)}, f32[4,128,128]{2,1,0:T(8,128)S(1)}, s32[]{:T(128)}) while((s32[]{:T(128)}, f32[512,512]{1,0:T(8,128)}, s32[4,2]{0,1:T(2,128)S(1)}, f32[4,128,128]{2,1,0:T(8,128)S(1)}, s32[]{:T(128)}) %tuple.59), condition=%wide.while_cond, body=%wide.while_body.sunk | while | flops 2 | bytes 131181 | solution.py:35
  134.3 39.3 %custom-call.34 = f32[4,128,128]{1,2,0:T(8,128)S(1)} custom-call(f32[4,128,128]{2,1,0:T(8,128)S(1)} %get-tuple-element.10), custom_call_target="InvertDiagBlocksLowerTriangular" | custom-call | tf_op jit(solution)/shard_map/jit(_cho_solve)/triangular_solve | solution.py:35
  198.8 10.3 %all_gather.6 = f32[256,768]{1,0:T(8,128)S(1)} all-gather(f32[64,768]{1,0:T(8,128)S(1)} %convolution_subtract_fusion.8), channel_id=1, replica_groups=mesh['rows'=128,'cols'=4] {'cols'}, dimensions={0}, use_global_device_ids=true | all-gather | bytes 983040 | tf_op jit(solution)/shard_map/all_gather | solution.py:60
  210.0 3.3 collective-permute-start.2
  213.3 2.8 bitcast_subtract_fusion
  216.1 4.5 %collective-permute-done.2 = f32[256,256]{0,1:T(8,128)S(1)} collective-permute-done((f32[256,256]{0,1:T(8,128)S(1)}, f32[256,256]{0,1:T(8,128)S(1)}, u32[]{:S(2)}, u32[]{:S(2)}) %collective-permute-start.2) | collective-permute-done | bytes 262176 | tf_op jit(solution)/shard_map/ppermute | solution.py:10
  220.7 6.1 %collective-permute-start.3 = (f32[256,256]{0,1:T(8,128)S(1)}, f32[256,256]{0,1:T(8,128)S(1)}, u32[]{:S(2)}, u32[]{:S(2)}) collective-permute-start(f32[256,256]{0,1:T(8,128)S(1)} %add.73), channel_id=1, source_target_pairs={{0,8},{4,12},{8,0},{12,4},{16,24},{20,28},{24,16},{28,20},{32,40},... | collective-permute-start | bytes 786440 | tf_op jit(solution)/shard_map/ppermute | solution.py:10
  229.0 3.0 collective-permute-start.4
  234.9 2.5 copy.36
  240.1 11.7 %cholesky.358 = f32[128,128]{1,0:T(8,128)S(1)} custom-call(f32[128,128]{1,0:T(8,128)S(1)} %cholesky.439), custom_call_target="Cholesky" | custom-call | tf_op jit(solution)/shard_map/jit(cholesky)/cholesky | solution.py:34
  253.0 9.8 %custom-call.42 = f32[1,128,128]{1,2,0:T(8,128)S(1)} custom-call(f32[1,128,128]{2,1,0:T(8,128)S(1)} %get-tuple-element.60), custom_call_target="InvertDiagBlocksLowerTriangular" | custom-call | tf_op jit(solution)/shard_map/jit(cholesky)/cholesky | solution.py:34
  266.0 11.7 %cholesky.377 = f32[128,128]{1,0:T(8,128)S(1)} custom-call(f32[128,128]{1,0:T(8,128)S(1)} %cholesky.443), custom_call_target="Cholesky" | custom-call | tf_op jit(solution)/shard_map/jit(cholesky)/cholesky | solution.py:34
  279.0 10.0 %custom-call.43 = f32[1,128,128]{1,2,0:T(8,128)S(1)} custom-call(f32[1,128,128]{2,1,0:T(8,128)S(1)} %get-tuple-element.57), custom_call_target="InvertDiagBlocksLowerTriangular" | custom-call | tf_op jit(solution)/shard_map/jit(cholesky)/cholesky | solution.py:34
  291.4 11.7 %cholesky.398 = f32[128,128]{1,0:T(8,128)S(1)} custom-call(f32[128,128]{1,0:T(8,128)S(1)} %cholesky.448), custom_call_target="Cholesky" | custom-call | tf_op jit(solution)/shard_map/jit(cholesky)/cholesky | solution.py:34
  303.7 9.8 %custom-call.44 = f32[1,128,128]{1,2,0:T(8,128)S(1)} custom-call(f32[1,128,128]{2,1,0:T(8,128)S(1)} %get-tuple-element.54), custom_call_target="InvertDiagBlocksLowerTriangular" | custom-call | tf_op jit(solution)/shard_map/jit(cholesky)/cholesky | solution.py:34
  315.8 11.7 %cholesky.415 = f32[128,128]{1,0:T(8,128)S(1)} custom-call(f32[128,128]{1,0:T(8,128)S(1)} %convolution_subtract_fusion.12), custom_call_target="Cholesky" | custom-call | tf_op jit(solution)/shard_map/jit(cholesky)/cholesky | solution.py:34
  332.4 5.7 %collective-permute-start.5 = (f32[256,512]{0,1:T(8,128)}, f32[256,512]{0,1:T(8,128)}, u32[]{:S(2)}, u32[]{:S(2)}) collective-permute-start(f32[256,512]{0,1:T(8,128)} %add.75), channel_id=1, source_target_pairs={{0,8},{4,12},{8,0},{12,4},{16,24},{20,28},{24,16},{28,20},{32,40},... | collective-permute-start | bytes 1572872 | tf_op jit(solution)/shard_map/ppermute | solution.py:10
  343.0 11.5 %while.3 = (s32[]{:T(128)}, f32[512,512]{1,0:T(8,128)}, s32[4,2]{0,1:T(2,128)S(1)}, f32[4,128,128]{2,1,0:T(8,128)S(1)}, s32[]{:T(128)}) while((s32[]{:T(128)}, f32[512,512]{1,0:T(8,128)}, s32[4,2]{0,1:T(2,128)S(1)}, f32[4,128,128]{2,1,0:T(8,128)S(1)}, s32[]{:T(128)}) %tuple.65), condition=%wide.while_cond.1, body=%wide.while_body.1.sunk | while | flops 2 | bytes 131181 | solution.py:35
  354.6 39.9 %custom-call.35 = f32[4,128,128]{1,2,0:T(8,128)} custom-call(f32[4,128,128]{2,1,0:T(8,128)S(1)} %get-tuple-element.18), custom_call_target="InvertDiagBlocksLowerTriangular" | custom-call | tf_op jit(solution)/shard_map/jit(_cho_solve)/triangular_solve | solution.py:35
  420.9 3.7 convolution_subtract_fusion
  424.6 3.0 copy.41
  (179 shorter events, 124.6 us)
Async XLA Ops:
  0.6 1.1 copy-start
  0.6 6.1 %copy-start.8 = (f32[768,512]{1,0:T(8,128)S(1)}, f32[768,512]{1,0:T(8,128)}, u32[]{:S(2)}) copy-start(f32[768,512]{1,0:T(8,128)} %param.6) | copy-start | bytes 4718596
  3.9 4.4 %copy-start.21 = (f32[64,768]{1,0:T(8,128)S(1)}, f32[64,768]{1,0:T(8,128)}, u32[]{:S(2)}) copy-start(f32[64,768]{1,0:T(8,128)} %param.5) | copy-start | bytes 589828
  3.9 22.4 %collective-permute-start = (f32[256,256]{0,1:T(8,128)}, f32[256,256]{0,1:T(8,128)}, u32[]{:S(2)}, u32[]{:S(2)}) collective-permute-start(f32[256,256]{0,1:T(8,128)} %fusion.105), channel_id=1, source_target_pairs={{0,4},{4,0},{8,12},{12,8},{16,20},{20,16},{24,28},{28,24},{32,36},... | collective-permute-start | bytes 786440 | tf_op jit(solution)/shard_map/ppermute | solution.py:10
  8.3 1.4 copy-start.9
  11.0 162.6 %collective-permute-start.1 = (f32[256,576]{0,1:T(8,128)}, f32[256,576]{0,1:T(8,128)}, u32[]{:S(2)}, u32[]{:S(2)}) collective-permute-start(f32[256,576]{0,1:T(8,128)} %copy.27), channel_id=1, source_target_pairs={{0,4},{4,0},{8,12},{12,8},{16,20},{20,16},{24,28},{28,24},{32,36},... | collective-permute-start | bytes 1769480 | tf_op jit(solution)/shard_map/ppermute | solution.py:10
  14.1 17.2 %copy-start.3 = (f32[256,256]{0,1:T(8,128)}, f32[256,256]{0,1:T(8,128)S(1)}, u32[]{:S(2)}) copy-start(f32[256,256]{0,1:T(8,128)S(1)} %get-tuple-element.75) | copy-start | bytes 786436
  14.1 17.2 %copy-start.5 = (f32[256,256]{0,1:T(8,128)}, f32[256,256]{0,1:T(8,128)S(1)}, u32[]{:S(2)}) copy-start(f32[256,256]{0,1:T(8,128)S(1)} %get-tuple-element.76) | copy-start | bytes 786436
  26.2 182.9 %copy-start.1 = (f32[256,768]{1,0:T(8,128)}, f32[256,768]{1,0:T(8,128)S(1)}, u32[]{:S(2)}) copy-start(f32[256,768]{1,0:T(8,128)S(1)} %all_gather.7) | copy-start | bytes 2359300
  32.7 1.0 copy-start.14
  122.6 52.4 %copy-start.10 = (f32[256,512]{1,0:T(8,128)S(1)}, f32[256,512]{1,0:T(8,128)}, u32[]{:S(2)}) copy-start(f32[256,512]{1,0:T(8,128)} %copy-done.9) | copy-start | bytes 1572868
  173.6 9.2 %copy-start.23 = (f32[4,128,128]{1,2,0:T(8,128)}, f32[4,128,128]{1,2,0:T(8,128)S(1)}, u32[]{:S(2)}) copy-start(f32[4,128,128]{1,2,0:T(8,128)S(1)} %custom-call.34) | copy-start | bytes 786436
  188.0 3.4 copy-start.16
  193.9 3.4 copy-start.22
  198.2 0.7 copy-start.25
  198.8 14.5 %copy-start.7 = (f32[768,512]{0,1:T(8,128)S(1)}, f32[768,512]{0,1:T(8,128)}, u32[]{:S(2)}) copy-start(f32[768,512]{0,1:T(8,128)} %copy.34) | copy-start | bytes 4718596
  210.0 16.7 %copy-start.2 = (f32[256,768]{1,0:T(8,128)S(1)}, f32[256,768]{1,0:T(8,128)}, u32[]{:S(2)}) copy-start(f32[256,768]{1,0:T(8,128)} %copy-done.1) | copy-start | bytes 2359300
  210.0 10.6 %collective-permute-start.2 = (f32[256,256]{0,1:T(8,128)S(1)}, f32[256,256]{0,1:T(8,128)S(1)}, u32[]{:S(2)}, u32[]{:S(2)}) collective-permute-start(f32[256,256]{0,1:T(8,128)S(1)} %convolution_bitcast_fusion.1), channel_id=1, source_target_pairs={{0,4},{4,0},{8,12},{12,8},{16,20},{20,16},{24,28},{28,24},{32,36},... | collective-permute-start | bytes 786440 | tf_op jit(solution)/shard_map/ppermute | solution.py:10
  220.6 13.2 %copy-start.4 = (f32[256,256]{0,1:T(8,128)S(1)}, f32[256,256]{0,1:T(8,128)}, u32[]{:S(2)}) copy-start(f32[256,256]{0,1:T(8,128)} %copy-done.3) | copy-start | bytes 786436
  220.7 13.1 %copy-start.6 = (f32[256,256]{0,1:T(8,128)S(1)}, f32[256,256]{0,1:T(8,128)}, u32[]{:S(2)}) copy-start(f32[256,256]{0,1:T(8,128)} %copy-done.5) | copy-start | bytes 786436
  220.7 12.3 %collective-permute-start.3 = (f32[256,256]{0,1:T(8,128)S(1)}, f32[256,256]{0,1:T(8,128)S(1)}, u32[]{:S(2)}, u32[]{:S(2)}) collective-permute-start(f32[256,256]{0,1:T(8,128)S(1)} %add.73), channel_id=1, source_target_pairs={{0,8},{4,12},{8,0},{12,4},{16,24},{20,28},{24,16},{28,20},{32,40},... | collective-permute-start | bytes 786440 | tf_op jit(solution)/shard_map/ppermute | solution.py:10
  229.0 101.4 %collective-permute-start.4 = (f32[256,512]{0,1:T(8,128)}, f32[256,512]{0,1:T(8,128)}, u32[]{:S(2)}, u32[]{:S(2)}) collective-permute-start(f32[256,512]{0,1:T(8,128)} %convolution_bitcast_fusion), channel_id=1, source_target_pairs={{0,4},{4,0},{8,12},{12,8},{16,20},{20,16},{24,28},{28,24},{32,36},... | collective-permute-start | bytes 1572872 | tf_op jit(solution)/shard_map/ppermute | solution.py:10
  233.0 0.7 copy-start.19
  233.0 0.8 copy-start.20
  239.2 1.0 copy-start.15
  332.4 62.1 %collective-permute-start.5 = (f32[256,512]{0,1:T(8,128)}, f32[256,512]{0,1:T(8,128)}, u32[]{:S(2)}, u32[]{:S(2)}) collective-permute-start(f32[256,512]{0,1:T(8,128)} %add.75), channel_id=1, source_target_pairs={{0,8},{4,12},{8,0},{12,4},{16,24},{20,28},{24,16},{28,20},{32,40},... | collective-permute-start | bytes 1572872 | tf_op jit(solution)/shard_map/ppermute | solution.py:10
  394.5 1.3 copy-start.24
  398.1 5.3 %copy-start.11 = (f32[128,512]{1,0:T(8,128)}, f32[128,512]{1,0:T(8,128)S(1)}, u32[]{:S(2)}) copy-start(f32[128,512]{1,0:T(8,128)S(1)} %fusion.43) | copy-start | bytes 786436
  403.8 0.7 copy-start.12
  412.1 3.9 copy-start.13
  412.1 3.9 copy-start.17
  415.3 0.7 copy-start.18
where the time goes:
time: 434 us; the launch traced here: 428 us
  other arithmetic  255 us (59%)
  matrix products  66.2 us (15%)
  local copies, waits for them, and re-layouts  49.2 us (11%)
  starting transfers between devices  24 us (6%)
  blocking collectives  20.8 us (5%)
  between operations  6.72 us (2%)
  waiting for transfers between devices  5.47 us (1%)
    another operation x30, other arithmetic, capacity_solve(): factor = jnp.linalg.cholesky(capacitance)  161 us
    another operation x5, other arithmetic, capacity_solve(): jax.scipy.linalg.cho_solve((factor, True), jnp.concatenate([rhs_low, rhs_...  82.7 us
    another operation x28, matrix products, capacity_solve(): jax.scipy.linalg.cho_solve((factor, True), jnp.concatenate([rhs_low, rhs_...  37.7 us
    ppermute x6, starting transfers between devices, partner(): lax.ppermute(value, axis, [(i, i ^ 1 << bit) for i in range(lax.axis_size...  24 us
    another operation x24, local copies, waits for them, and re-layouts  23 us
    another operation x12, matrix products, capacity_solve(): factor = jnp.linalg.cholesky(capacitance)  13.2 us
    unnamed x56, local copies, waits for them, and re-layouts  10.6 us
    all_gather x1, blocking collectives, shards(): basis_two = lax.all_gather(level2_basis, 'cols', axis=0, tiled=True)  10.5 us
  transfers between devices with their start and end apart: 6, of which 2 were waited for; matrix products, arithmetic and copies ran while one was open for 71% of the time, Pallas kernels for 0%

commit v1 on v0

v1 whole, which is shorter than its diff:
```python
import jax
import jax.numpy as jnp
from jax import lax
from jax.experimental import pallas as pl
from jax.experimental.pallas import tpu as pltpu
from jax.sharding import PartitionSpec as P

F32 = jnp.float32
BF16 = jnp.bfloat16
NN = (((1,), (0,)), ((), ()))
NT = (((1,), (1,)), ((), ()))
VMEM_BYTES = 56 * 2**20


def halves(x):
    high = x.astype(BF16)
    low = (x - high.astype(F32)).astype(BF16)
    return high, low


def pass_dot(a, b, dims):
    return lax.dot_general(a, b, dims, preferred_element_type=F32)


def dot3(a, b, dims=NN):
    a_high, a_low = halves(a)
    b_high, b_low = halves(b)
    cross = pass_dot(a_high, b_low, dims) + pass_dot(a_low, b_high, dims)
    return pass_dot(a_high, b_high, dims) + cross


def dot6(a, b, dims=NN):
    return lax.dot_general(a, b, dims, precision=lax.Precision.HIGHEST, preferred_element_type=F32)


def unit_matrix(n):
    return (lax.broadcasted_iota(jnp.int32, (n, n), 0) == lax.broadcasted_iota(jnp.int32, (n, n), 1)).astype(F32)


def invert(matrices, works, floor):
    n = matrices[0].shape[0]
    eye = unit_matrix(n)
    low = floor * 0.98
    tops = [jnp.max(jnp.sum(jnp.abs(m[...]), axis=0, keepdims=True), axis=1, keepdims=True) for m in matrices]
    top = tops[0]
    for other in tops[1:]:
        top = jnp.maximum(top, other)
    top = jnp.max(top) * 1.02
    scale = 2.0 / (top + low)
    spread = (top - low) / (top + low)
    square = spread * spread
    gain = 2.0 / (2.0 - square)
    for m, w in zip(matrices, works):
        w[...] = (gain * scale) * (2.0 * eye - scale * m[...])

    def coarse(state):
        square = state * state
        gain = 2.0 / (2.0 - square)
        for m, w in zip(matrices, works):
            x = w[...]
            w[...] = gain * (2.0 * x - dot3(x, dot3(m[...], x)))
        return square / (2.0 - square)

    lax.while_loop(lambda state: state > 1e-2, coarse, square / (2.0 - square))
    steps = jnp.where(top > 200.0 * low, 4, 2)

    def fine(_, carry):
        for m, w in zip(matrices, works):
            x = w[...]
            w[...] = x + dot3(x, eye - dot6(m[...], x))
        return carry

    lax.fori_loop(0, steps, fine, 0)


def refine_schur(schur, start):
    eye = unit_matrix(schur.shape[0])
    spread = 1.0 / 7.0
    x = start * (8.0 / 7.0)
    for step in range(2):
        square = spread * spread
        gain = 2.0 / (2.0 - square)
        spread = square / (2.0 - square)
        x = gain * (2.0 * x - dot3(x, dot3(schur, x)))
    return x + dot3(x, eye - dot6(schur, x))


def first_kernel(coupling, y1_ref, y2t_ref, z_ref, cap_ref, inv_ref, bt_ref, dd_ref, rhs_ref):
    y1 = y1_ref[...]
    y2t = y2t_ref[...]
    y1t = y1.T
    n = y1.shape[1]
    cap_ref[...] = dot6(y1t, y1) + (2.0 * coupling) * unit_matrix(n)
    bt_ref[...] = dot6(y2t, y1)
    dd_ref[...] = dot6(y2t, y2t, NT)
    z = z_ref[...]
    rhs_ref[:n] = dot3(y1t, z)
    rhs_ref[n:] = dot3(y2t, z)
    invert([cap_ref], [inv_ref], 2.0 * coupling)


def pair_kernel(coupling, cap_ref, inv_ref, bt_ref, dd_ref, other_inv_ref, other_bt_ref, t_ref, et_ref, et_other_ref, p_ref):
    other = other_inv_ref[...]
    bt = bt_ref[...]
    other_bt = other_bt_ref[...]
    t = refine_schur(cap_ref[...] - coupling * coupling * other, inv_ref[...])
    t_ref[...] = t
    et = dot6(bt + coupling * dot6(other_bt, other), t)
    et_ref[...] = et
    p_ref[...] = dd_ref[...] - dot6(et, bt, NT)
    et_other_ref[...] = dot6(other_bt + coupling * et, other)


def rhs_kernel(coupling, t_ref, et_ref, et_other_ref, other_inv_ref, rhs_ref, other_rhs_ref, f_ref, ez_ref):
    n = t_ref.shape[0]
    own = rhs_ref[:n]
    other = other_rhs_ref[:n]
    f_ref[...] = rhs_ref[n:] + other_rhs_ref[n:] - dot3(et_ref[...], own) - dot3(et_other_ref[...], other)
    ez_ref[...] = dot3(t_ref[...], own + coupling * dot3(other_inv_ref[...], other))


def quad_kernel(coupling, p_ref, t_ref, far_ref, cap_ref, far_cap_ref, own_ref):
    n = t_ref.shape[0]
    diagonal = (2.0 * coupling) * unit_matrix(n)
    cap_ref[...] = p_ref[0] + p_ref[1] + diagonal
    far_cap_ref[...] = p_ref[2] + p_ref[3] + diagonal
    invert([cap_ref, far_cap_ref], [own_ref, far_ref], 2.0 * coupling)
    t_ref[...] = refine_schur(cap_ref[...] - coupling * coupling * far_ref[...], own_ref[...])


def last_kernel(coupling, t_ref, far_ref, f_ref, f_far_ref, ez_ref, et_ref, y1_ref, y2t_ref, z_ref, out_ref):
    k = dot3(t_ref[...], f_ref[...] + coupling * dot3(far_ref[...], f_far_ref[...]))
    c1 = ez_ref[...] - dot3(et_ref[...].T, k)
    out_ref[...] = z_ref[...] - dot3(y1_ref[...], c1) - dot3(y2t_ref[...].T, k)


def updated_kernel(y2_ref, et_ref, y1_ref, out_ref):
    out_ref[...] = y2_ref[...] - dot3(et_ref[...], y1_ref[...], NT)


def call(kernel, outs, *args, **kw):
    return pl.pallas_call(
        kernel,
        out_shape=[jax.ShapeDtypeStruct(o, F32) for o in outs],
        in_specs=[pl.BlockSpec(memory_space=pltpu.VMEM)] * len(args),
        out_specs=[pl.BlockSpec(memory_space=pltpu.VMEM)] * len(outs),
        compiler_params=pltpu.CompilerParams(vmem_limit_bytes=VMEM_BYTES),
        **kw,
    )(*args)


def shards(level1_basis, level2_basis, probes):
    points, rank = level1_basis.shape
    part, columns = level2_basis.shape[0], probes.shape[1]
    coupling = points / 3.0
    n_rows = lax.axis_size("rows")
    quads = [[4 * q + i for i in range(4)] for q in range(n_rows // 4)]
    place = lax.axis_index("rows") % 4
    square = (rank, rank)

    def kern(f):
        return lambda *refs: f(coupling, *refs)

    def swap(value, bits):
        return lax.ppermute(value, "rows", [(i, i ^ bits) for i in range(n_rows)])

    y2t = lax.all_gather(level2_basis, "cols", axis=0, tiled=True)
    cap, inv, bt, dd, rhs = call(
        kern(first_kernel), [square, square, square, square, (2 * rank, columns)], level1_basis, y2t, probes
    )
    other = swap(jnp.concatenate([inv, bt], axis=0), 1)
    other_inv, other_bt = other[:rank], other[rank:]
    other_rhs = swap(rhs, 1)
    t, et, et_other, p = call(kern(pair_kernel), [square] * 4, cap, inv, bt, dd, other_inv, other_bt)
    f_own, ez = call(kern(rhs_kernel), [(rank, columns)] * 2, t, et, et_other, other_inv, rhs, other_rhs)
    all_p = lax.all_gather(p, "rows", axis_index_groups=quads)
    f_far = swap(f_own, 3)
    all_p = jnp.where(place >= 2, jnp.concatenate([all_p[2:], all_p[:2]], axis=0), all_p)
    t2, far2, _, _, _ = call(kern(quad_kernel), [square] * 5, all_p)
    (out,) = call(
        kern(last_kernel), [(points, columns)], t2, far2, f_own, f_far, ez, et, level1_basis, y2t, probes
    )
    start = lax.axis_index("cols") * part
    et_part = lax.dynamic_slice_in_dim(et, start, part, axis=0)
    (updated,) = call(updated_kernel, [(part, points)], level2_basis, et_part, level1_basis)
    return out, updated


def solution(mesh):
    return jax.shard_map(
        shards,
        mesh=mesh,
        in_specs=(P("rows", None), P("cols", "rows"), P("rows", "cols")),
        out_specs=(P("rows", "cols"), P("cols", "rows")),
        check_vma=False,
    )
```

time: 434 us -> 125 us (0.29)
  the two profiles are of different devices: /device:TPU:6 before, /device:TPU:384 now
where the time goes in v1:
time: 125 us
  waiting for transfers between devices  40.3 us (32%)
  Pallas kernels  39.1 us (31%)
  between operations  14.1 us (11%)
  blocking collectives  11.9 us (10%)
  starting transfers between devices  11.6 us (9%)
  local copies, waits for them, and re-layouts  5.64 us (5%)
  other arithmetic  2.17 us (2%)
    ppermute x3, waiting for transfers between devices, swap(): return lax.ppermute(value, 'rows', [(i, i ^ bits) for i in range(n_rows)])  40.3 us
    pallas_call x6, Pallas kernels, call(): pl.pallas_call(kernel, out_shape=[jax.ShapeDtypeStruct(o, F32) for o in o...  39.1 us
    all_gather x1, blocking collectives, shards(): y2t = lax.all_gather(level2_basis, 'cols', axis=0, tiled=True)  11.9 us
    ppermute x3, starting transfers between devices, swap(): return lax.ppermute(value, 'rows', [(i, i ^ bits) for i in range(n_rows)])  11.6 us
  transfers between devices with their start and end apart: 4, of which 2 were waited for; matrix products, arithmetic and copies ran while one was open for 3% of the time, Pallas kernels for 14%

profile of v1, /device:TPU:384, one launch (start us, length us, event | category | flops | bytes accessed | tf_op | source)
XLA Modules:
  0.0 124.9 jit_solution(3987733324882822905)
XLA Ops:
  7.2 0.0 all-gather.3.cloned.1.call-start
  7.2 11.9 %all_gather.9.refs_1_.refs_7_ = f32[256,768]{1,0:T(8,128)} all-gather(f32[64,768]{1,0:T(8,128)} %y2_ref.1), channel_id=1, replica_groups=mesh['rows'=128,'cols'=4] {'cols'}, dimensions={0}, use_global_device_ids=true | all-gather | bytes 983040 | tf_op jit(solution)/shard_map/all_gather | solution.py:167
  19.1 9.7 %shard_map.50 = (f32[256,256]{1,0:T(8,128)}, f32[256,256]{1,0:T(8,128)}, f32[256,256]{1,0:T(8,128)}, f32[256,256]{1,0:T(8,128)}, f32[512,512]{1,0:T(8,128)}) custom-call(f32[768,256]{1,0:T(8,128)} %y1_ref.1, f32[256,768]{1,0:T(8,128)} %all_gather.9.refs_1_.refs_7_, f32[768,512]{1,0:T(8,128)} %refs_8_.1), custom_call_target="tpu_custom_call" | custom-call | tf_op jit(solution)/shard_map/pallas_call | solution.py:142
  28.8 1.1 pad_maximum_fusion
  29.9 0.0 copy-start.1
  29.9 3.5 %collective-permute-start = (f32[512,256]{1,0:T(8,128)S(1)}, f32[512,256]{1,0:T(8,128)S(1)}, u32[]{:S(2)}, u32[]{:S(2)}) collective-permute-start(f32[512,256]{1,0:T(8,128)S(1)} %pad_maximum_fusion), channel_id=1, source_target_pairs={{0,4},{4,0},{8,12},{12,8},{16,20},{20,16},{24,28},{28,24},{32,36},... | collective-permute-start | bytes 1572872 | tf_op jit(solution)/shard_map/ppermute | solution.py:165
  33.4 12.7 %collective-permute-done = f32[512,256]{1,0:T(8,128)S(1)} collective-permute-done((f32[512,256]{1,0:T(8,128)S(1)}, f32[512,256]{1,0:T(8,128)S(1)}, u32[]{:S(2)}, u32[]{:S(2)}) %collective-permute-start) | collective-permute-done | bytes 524320 | tf_op jit(solution)/shard_map/ppermute | solution.py:165
  46.1 0.9 fusion.1
  47.0 5.6 %shard_map.51 = (f32[256,256]{1,0:T(8,128)}, f32[256,256]{1,0:T(8,128)}, f32[256,256]{1,0:T(8,128)}, f32[256,256]{1,0:T(8,128)}) custom-call(f32[256,256]{1,0:T(8,128)} %get-tuple-element.15.refs_0_, f32[256,256]{1,0:T(8,128)} %get-tuple-element.16.refs_1_, f32[256,256]{1,0:T(8,128)} %get-tuple-element.17.refs_2_, f32[256,256]{1,0:T(8,128)} %get-tuple-element.18.refs_3_, ...), custom_call_target="tpu_custom_call" | custom-call | tf_op jit(solution)/shard_map/pallas_call | solution.py:142
  52.6 0.0 all-gather.3.cloned.1.call-update
  52.6 0.0 copy-done.1
  52.6 3.4 %collective-permute-start.1 = (f32[512,512]{1,0:T(8,128)S(1)}, f32[512,512]{1,0:T(8,128)S(1)}, u32[]{:S(2)}, u32[]{:S(2)}) collective-permute-start(f32[512,512]{1,0:T(8,128)S(1)} %copy-done.1), channel_id=1, source_target_pairs={{0,4},{4,0},{8,12},{12,8},{16,20},{20,16},{24,28},{28,24},{32,36},... | collective-permute-start | bytes 3145736 | tf_op jit(solution)/shard_map/ppermute | solution.py:165
  56.0 1.5 %constant_dynamic-slice_fusion.et_ref = f32[64,256]{1,0:T(8,128)} fusion(f32[256,256]{1,0:T(8,128)} %get-tuple-element.23.refs_1_.refs_5_, s32[]{:T(128)S(6)} %select_n.21), kind=kLoop, calls=%fused_computation.2 | loop fusion | bytes 131076 | tf_op jit(solution)/shard_map/dynamic_slice | solution.py:184
  57.5 2.5 %shard_map.55 = f32[64,768]{1,0:T(8,128)} custom-call(f32[64,768]{1,0:T(8,128)} %y2_ref.1, f32[64,256]{1,0:T(8,128)} %constant_dynamic-slice_fusion.et_ref, f32[768,256]{1,0:T(8,128)} %y1_ref.1), custom_call_target="tpu_custom_call" | custom-call | tf_op jit(solution)/shard_map/pallas_call | solution.py:142
  60.0 27.6 %collective-permute-done.1.refs_5_ = f32[512,512]{1,0:T(8,128)S(1)} collective-permute-done((f32[512,512]{1,0:T(8,128)S(1)}, f32[512,512]{1,0:T(8,128)S(1)}, u32[]{:S(2)}, u32[]{:S(2)}) %collective-permute-start.1) | collective-permute-done | bytes 1048608 | tf_op jit(solution)/shard_map/ppermute | solution.py:165
  87.6 0.0 copy-start.2
  87.6 1.0 copy-done.2
  88.5 3.8 %shard_map.53 = (f32[256,512]{1,0:T(8,128)}, f32[256,512]{1,0:T(8,128)}) custom-call(f32[256,256]{1,0:T(8,128)} %get-tuple-element.22.refs_0_, f32[256,256]{1,0:T(8,128)} %get-tuple-element.23.refs_1_.refs_5_, f32[256,256]{1,0:T(8,128)} %get-tuple-element.24.refs_2_, f32[256,256]{1,0:T(8,128)} %get-tuple-element.31.refs_4_.refs_3_, ...), custom_call_target="tpu_custom_call" | custom-call | tf_op jit(solution)/shard_map/pallas_call | solution.py:142
  92.4 4.7 %collective-permute-start.2 = (f32[256,512]{1,0:T(8,128)}, f32[256,512]{1,0:T(8,128)S(1)}, u32[]{:S(2)}, u32[]{:S(2)}) collective-permute-start(f32[256,512]{1,0:T(8,128)} %get-tuple-element.26.refs_2_), channel_id=1, source_target_pairs={{0,12},{4,8},{8,4},{12,0},{16,28},{20,24},{24,20},{28,16},{32,44},... | collective-permute-start | bytes 1572872 | tf_op jit(solution)/shard_map/ppermute | solution.py:165
  97.0 0.0 all-gather.3.cloned.1.call-done
  97.1 0.0 copy-start
  97.1 1.4 %fusion = (f32[512,256]{1,0:T(8,128)S(1)}, f32[512,256]{1,0:T(8,128)S(1)}) fusion(f32[1024,256]{1,0:T(8,128)} %all-gather.3.cloned.1.call-done), kind=kLoop, calls=%fused_computation.3 | loop fusion | bytes 2097152 | tf_op jit(solution)/shard_map/slice | solution.py:178
  98.4 0.2 copy-done
  98.6 1.1 maximum_select_fusion.refs_0_
  99.7 11.4 %shard_map.52 = (f32[256,256]{1,0:T(8,128)}, f32[256,256]{1,0:T(8,128)}, f32[256,256]{1,0:T(8,128)}, f32[256,256]{1,0:T(8,128)}, f32[256,256]{1,0:T(8,128)}) custom-call(f32[4,256,256]{2,1,0:T(8,128)} %maximum_select_fusion.refs_0_), custom_call_target="tpu_custom_call" | custom-call | tf_op jit(solution)/shard_map/pallas_call | solution.py:142
  111.1 0.0 collective-permute-done.2.refs_3_
  111.1 0.0 copy-start.3
  111.1 0.8 copy-done.3
  111.9 6.2 %shard_map.54 = f32[768,512]{1,0:T(8,128)} custom-call(f32[256,256]{1,0:T(8,128)} %get-tuple-element.20.refs_0_, f32[256,256]{1,0:T(8,128)} %get-tuple-element.21.refs_1_, f32[256,512]{1,0:T(8,128)} %get-tuple-element.26.refs_2_, f32[256,512]{1,0:T(8,128)} %copy-done.3, f32[256,512]{1,0:T(8,128)} %get-tuple-element.27.refs_4_, ...), custom_call_target="tpu_custom_call" | custom-call | tf_op jit(solution)/shard_map/pallas_call | solution.py:142
Async XLA Ops:
  7.2 89.9 %all-gather.3.cloned.1.call-start = ((), (), s32[]{:S(2)}) async-start(), calls=%async_computation | async-start | bytes 1310720 | tf_op jit(solution)/shard_map/all_gather | solution.py:176
  29.9 22.7 %copy-start.1 = (f32[512,512]{1,0:T(8,128)S(1)}, f32[512,512]{1,0:T(8,128)}, u32[]{:S(2)}) copy-start(f32[512,512]{1,0:T(8,128)} %get-tuple-element.25.refs_4_) | copy-start | bytes 3145732
  29.9 16.2 %collective-permute-start = (f32[512,256]{1,0:T(8,128)S(1)}, f32[512,256]{1,0:T(8,128)S(1)}, u32[]{:S(2)}, u32[]{:S(2)}) collective-permute-start(f32[512,256]{1,0:T(8,128)S(1)} %pad_maximum_fusion), channel_id=1, source_target_pairs={{0,4},{4,0},{8,12},{12,8},{16,20},{20,16},{24,28},{28,24},{32,36},... | collective-permute-start | bytes 1572872 | tf_op jit(solution)/shard_map/ppermute | solution.py:165
  52.6 34.9 %collective-permute-start.1 = (f32[512,512]{1,0:T(8,128)S(1)}, f32[512,512]{1,0:T(8,128)S(1)}, u32[]{:S(2)}, u32[]{:S(2)}) collective-permute-start(f32[512,512]{1,0:T(8,128)S(1)} %copy-done.1), channel_id=1, source_target_pairs={{0,4},{4,0},{8,12},{12,8},{16,20},{20,16},{24,28},{28,24},{32,36},... | collective-permute-start | bytes 3145736 | tf_op jit(solution)/shard_map/ppermute | solution.py:165
  87.6 1.0 copy-start.2
  92.4 18.7 %collective-permute-start.2 = (f32[256,512]{1,0:T(8,128)}, f32[256,512]{1,0:T(8,128)S(1)}, u32[]{:S(2)}, u32[]{:S(2)}) collective-permute-start(f32[256,512]{1,0:T(8,128)} %get-tuple-element.26.refs_2_), channel_id=1, source_target_pairs={{0,12},{4,8},{8,4},{12,0},{16,28},{20,24},{24,20},{28,16},{32,44},... | collective-permute-start | bytes 1572872 | tf_op jit(solution)/shard_map/ppermute | solution.py:165
  97.1 1.5 %copy-start = (f32[1024,256]{1,0:T(8,128)S(1)}, f32[1024,256]{1,0:T(8,128)}, u32[]{:S(2)}) copy-start(f32[1024,256]{1,0:T(8,128)} %all-gather.3.cloned.1.call-done) | copy-start | bytes 3145732
  111.1 0.8 copy-start.3
Sparse Core Ops, SparseCore 0:
  52.7 34.7 all-gather.2

commit v2 on v1

v2 whole, which is shorter than its diff:
```python
import jax
import jax.numpy as jnp
from jax import lax
from jax.experimental import pallas as pl
from jax.experimental.pallas import tpu as pltpu
from jax.sharding import PartitionSpec as P

F32 = jnp.float32
BF16 = jnp.bfloat16
NN = (((1,), (0,)), ((), ()))
NT = (((1,), (1,)), ((), ()))
VMEM_BYTES = 56 * 2**20


def halves(x):
    high = x.astype(BF16)
    low = (x - high.astype(F32)).astype(BF16)
    return high, low


def pass_dot(a, b, dims):
    return lax.dot_general(a, b, dims, preferred_element_type=F32)


def dot3(a, b, dims=NN):
    a_high, a_low = halves(a)
    b_high, b_low = halves(b)
    cross = pass_dot(a_high, b_low, dims) + pass_dot(a_low, b_high, dims)
    return pass_dot(a_high, b_high, dims) + cross


def dot6(a, b, dims=NN):
    return lax.dot_general(a, b, dims, precision=lax.Precision.HIGHEST, preferred_element_type=F32)


def unit_matrix(n):
    return (lax.broadcasted_iota(jnp.int32, (n, n), 0) == lax.broadcasted_iota(jnp.int32, (n, n), 1)).astype(F32)


def invert(matrices, works, floor):
    n = matrices[0].shape[0]
    eye = unit_matrix(n)
    low = floor * 0.98
    tops = [jnp.max(jnp.sum(jnp.abs(m[...]), axis=0, keepdims=True), axis=1, keepdims=True) for m in matrices]
    top = tops[0]
    for other in tops[1:]:
        top = jnp.maximum(top, other)
    top = jnp.max(top) * 1.02
    scale = 2.0 / (top + low)
    spread = (top - low) / (top + low)
    square = spread * spread
    gain = 2.0 / (2.0 - square)
    for m, w in zip(matrices, works):
        w[...] = (gain * scale) * (2.0 * eye - scale * m[...])

    def coarse(state):
        square = state * state
        gain = 2.0 / (2.0 - square)
        for m, w in zip(matrices, works):
            x = w[...]
            w[...] = gain * (2.0 * x - dot3(x, dot3(m[...], x)))
        return square / (2.0 - square)

    lax.while_loop(lambda state: state > 1e-2, coarse, square / (2.0 - square))
    steps = jnp.where(top > 200.0 * low, 4, 2)

    def fine(_, carry):
        for m, w in zip(matrices, works):
            x = w[...]
            w[...] = x + dot3(x, eye - dot6(m[...], x))
        return carry

    lax.fori_loop(0, steps, fine, 0)


def refine_schur(schur, start):
    eye = unit_matrix(schur.shape[0])
    spread = 1.0 / 7.0
    x = start * (8.0 / 7.0)
    for step in range(2):
        square = spread * spread
        gain = 2.0 / (2.0 - square)
        spread = square / (2.0 - square)
        x = gain * (2.0 * x - dot3(x, dot3(schur, x)))
    return x + dot3(x, eye - dot6(schur, x))


def leaf_kernel(coupling, y1_ref, z_ref, cap_ref, y_ref):
    y1 = y1_ref[...]
    y1t = y1.T
    cap_ref[...] = dot6(y1t, y1) + (2.0 * coupling) * unit_matrix(y1.shape[1])
    y_ref[...] = dot3(y1t, z_ref[...])


def invert_kernel(coupling, cap_ref, inv_ref):
    invert([cap_ref], [inv_ref], 2.0 * coupling)


def cross_kernel(coupling, y1_ref, near_ref, far_ref, inv_ref, bt_ref, sent_ref, dd_ref):
    y2t = jnp.concatenate([near_ref[...], far_ref[...]], axis=0)
    bt = dot6(y2t, y1_ref[...])
    bt_ref[...] = bt
    sent_ref[...] = jnp.where(lax.axis_index("cols") % 2 == 0, inv_ref[...], bt)
    dd_ref[...] = dot6(y2t, y2t, NT)


def project_kernel(coupling, near_ref, far_ref, z_ref, bt_ref, w_ref):
    z = z_ref[...]
    half = near_ref.shape[0]
    w_ref[:half] = dot3(near_ref[...], z)
    w_ref[half:] = dot3(far_ref[...], z)


def pair_kernel(coupling, cap_ref, inv_ref, bt_ref, other_ref, dd_ref, t_ref, et_ref, p_ref):
    n = cap_ref.shape[0]
    bt = bt_ref[...]
    other_inv = other_ref[:n]
    t = refine_schur(cap_ref[...] - coupling * coupling * other_inv, inv_ref[...])
    t_ref[...] = t
    et = dot6(bt + coupling * dot6(other_ref[n:], other_inv), t)
    et_ref[...] = et
    p_ref[...] = dd_ref[...] - dot6(et, bt, NT)


def rhs_kernel(coupling, t_ref, et_ref, other_ref, y_ref, other_y_ref, w_ref, other_w_ref, f_ref, ez_ref):
    n = t_ref.shape[0]
    own = y_ref[...]
    other = other_y_ref[...]
    et = et_ref[...]
    other_inv = other_ref[:n]
    et_other = dot3(other_ref[n:] + coupling * et, other_inv)
    f_ref[...] = w_ref[...] + other_w_ref[...] - dot3(et, own) - dot3(et_other, other)
    ez_ref[...] = dot3(t_ref[...], own + coupling * dot3(other_inv, other))


def apply_kernel(coupling, y1_ref, near_ref, far_ref, z_ref, et_ref, ez_ref, z1_ref, ut_ref, updated_ref):
    y1 = y1_ref[...]
    half = near_ref.shape[0]
    part = updated_ref.shape[0]
    change = dot3(et_ref[...], y1, NT)
    ut_ref[:half] = near_ref[...] - change[:half]
    ut_ref[half:] = far_ref[...] - change[half:]
    start = (lax.axis_index("cols") % 2) * part
    updated_ref[...] = ut_ref[pl.ds(pl.multiple_of(start, part), part), :]
    z1_ref[...] = z_ref[...] - dot3(y1, ez_ref[...])


def quad_kernel(coupling, p_ref, other_p_ref, cap_ref, inv_ref):
    cap_ref[...] = p_ref[...] + other_p_ref[...] + (2.0 * coupling) * unit_matrix(p_ref.shape[0])
    invert([cap_ref], [inv_ref], 2.0 * coupling)


def last_kernel(coupling, cap_ref, inv_ref, far_ref, f_ref, f_far_ref, z1_ref, ut_ref, out_ref):
    far = far_ref[...]
    t = refine_schur(cap_ref[...] - coupling * coupling * far, inv_ref[...])
    k = dot3(t, f_ref[...] + coupling * dot3(far, f_far_ref[...]))
    out_ref[...] = z1_ref[...] - dot3(ut_ref[...].T, k)


def call(kernel, outs, *args, micros=5):
    return pl.pallas_call(
        kernel,
        out_shape=[jax.ShapeDtypeStruct(o, F32) for o in outs],
        in_specs=[pl.BlockSpec(memory_space=pltpu.VMEM)] * len(args),
        out_specs=[pl.BlockSpec(memory_space=pltpu.VMEM)] * len(outs),
        compiler_params=pltpu.CompilerParams(vmem_limit_bytes=VMEM_BYTES),
        cost_estimate=pl.CostEstimate(flops=int(micros * 1e9), bytes_accessed=int(micros * 3e6), transcendentals=0),
    )(*args)


def shards(level1_basis, level2_basis, probes):
    points, rank = level1_basis.shape
    part, columns = level2_basis.shape[0], probes.shape[1]
    coupling = points / 3.0
    n_cols = lax.axis_size("cols")
    square, wide = (rank, rank), (rank, columns)

    def run(kernel, outs, *args, micros):
        return call(lambda *refs: kernel(coupling, *refs), outs, *args, micros=micros)

    def swap(value, bits, axis="rows"):
        return lax.ppermute(value, axis, [(i, i ^ bits) for i in range(lax.axis_size(axis))])

    def core_gather(value):
        groups = [[2 * i, 2 * i + 1] for i in range(n_cols // 2)]
        return lax.all_gather(value, "cols", axis=0, tiled=True, axis_index_groups=groups)

    near = core_gather(level2_basis)
    far = swap(near, 2, "cols")
    cap, y = run(leaf_kernel, [square, wide], level1_basis, probes, micros=4)
    other_y = swap(y, 1)
    (inv,) = run(invert_kernel, [square], cap, micros=10)
    bt, sent, dd = run(cross_kernel, [square] * 3, level1_basis, near, far, inv, micros=3)
    other_half = swap(sent, 1)
    (w,) = run(project_kernel, [wide], near, far, probes, bt, micros=3)
    other_w = swap(w, 1)
    other = core_gather(other_half)
    t, et, p = run(pair_kernel, [square] * 3, cap, inv, bt, other, dd, micros=20)
    other_p = swap(p, 1)
    f, ez = run(rhs_kernel, [wide] * 2, t, et, other, y, other_y, w, other_w, micros=4)
    f_far = swap(f, 3)
    cap_two, inv_two = run(quad_kernel, [square] * 2, p, other_p, micros=6)
    far_two = swap(inv_two, 3)
    z1, ut, updated = run(
        apply_kernel, [(points, columns), (rank, points), (part, points)], level1_basis, near, far, probes, et, ez, micros=4
    )
    (out,) = run(last_kernel, [(points, columns)], cap_two, inv_two, far_two, f, f_far, z1, ut, micros=7)
    return out, updated


def solution(mesh):
    return jax.shard_map(
        shards,
        mesh=mesh,
        in_specs=(P("rows", None), P("cols", "rows"), P("rows", "cols")),
        out_specs=(P("rows", "cols"), P("cols", "rows")),
        check_vma=False,
    )
```

time: 125 us -> 84.7 us (0.68)
  the two profiles are of different devices: /device:TPU:384 before, /device:TPU:16 now
where the time goes in v2:
time: 84.7 us; the launch traced here: 84.2 us
  Pallas kernels  44.2 us (52%)
  starting transfers between devices  26.5 us (31%)
  waiting for transfers between devices  5.05 us (6%)
  blocking collectives  4.6 us (5%)
  local copies, waits for them, and re-layouts  3.13 us (4%)
    pallas_call x9, Pallas kernels, call(): pl.pallas_call(kernel, out_shape=[jax.ShapeDtypeStruct(o, F32) for o in o...  44.2 us
    ppermute x7, starting transfers between devices, swap(): lax.ppermute(value, axis, [(i, i ^ bits) for i in range(lax.axis_size(axi...  26.5 us
    ppermute x7, waiting for transfers between devices, swap(): lax.ppermute(value, axis, [(i, i ^ bits) for i in range(lax.axis_size(axi...  5.05 us
    all_gather x2, blocking collectives, core_gather(): lax.all_gather(value, 'cols', axis=0, tiled=True, axis_index_groups=groups)  4.6 us
    unnamed x14, local copies, waits for them, and re-layouts  3.13 us
  transfers between devices with their start and end apart: 7, of which 3 were waited for; matrix products, arithmetic and copies ran while one was open for 0% of the time, Pallas kernels for 44%

profile of v2, /device:TPU:16, one launch (start us, length us, event | category | flops | bytes accessed | tf_op | source)
XLA Modules:
  0.0 84.2 jit_solution(15421846020582924804)
XLA Ops:
  0.6 2.3 %all_gather.6.refs_1_.refs_0_ = f32[128,768]{1,0:T(8,128)S(1)} all-gather(f32[64,768]{1,0:T(8,128)} %param.4), channel_id=1, replica_groups={{0,1},{2,3},{4,5},{6,7},{8,9},{10,11},{12,13},{14,15},{16,17},{18,19},{..., dimensions={0}, use_global_device_ids=true | all-gather | bytes 589824 | tf_op jit(solution)/shard_map/all_gather | solution.py:186
  2.9 7.6 %collective-permute-start = (f32[128,768]{1,0:T(8,128)S(1)}, f32[128,768]{1,0:T(8,128)S(1)}, u32[]{:S(2)}, u32[]{:S(2)}) collective-permute-start(f32[128,768]{1,0:T(8,128)S(1)} %all_gather.6.refs_1_.refs_0_), channel_id=1, source_target_pairs={{0,2},{1,3},{2,0},{3,1},{4,6},{5,7},{6,4},{7,5},{8,10},{9,11},{10,... | collective-permute-start | bytes 1179656 | tf_op jit(solution)/shard_map/ppermute | solution.py:182
  10.5 4.0 %shard_map.50 = (f32[256,256]{1,0:T(8,128)}, f32[256,512]{1,0:T(8,128)}) custom-call(f32[768,256]{1,0:T(8,128)} %refs_0_.5, f32[768,512]{1,0:T(8,128)} %refs_3_.1), custom_call_target="tpu_custom_call" | custom-call | flops 4000000000 | bytes 12000000 | tf_op jit(solution)/shard_map/pallas_call | solution.py:161
  14.5 1.9 %collective-permute-start.4 = (f32[256,512]{1,0:T(8,128)}, f32[256,512]{1,0:T(8,128)S(1)}, u32[]{:S(2)}, u32[]{:S(2)}) collective-permute-start(f32[256,512]{1,0:T(8,128)} %get-tuple-element.26.refs_3_), channel_id=1, source_target_pairs={{0,4},{4,0},{8,12},{12,8},{16,20},{20,16},{24,28},{28,24},{32,36},... | collective-permute-start | bytes 1572872 | tf_op jit(solution)/shard_map/ppermute | solution.py:182
  16.4 5.5 %shard_map.51.refs_3_.refs_1_ = f32[256,256]{1,0:T(8,128)} custom-call(f32[256,256]{1,0:T(8,128)} %get-tuple-element.17.refs_0_), custom_call_target="tpu_custom_call" | custom-call | flops 10000000000 | bytes 30000000 | tf_op jit(solution)/shard_map/pallas_call | solution.py:161
  22.0 0.0 collective-permute-done.refs_2_.refs_1_
  22.0 0.7 copy-done.4
  22.7 3.7 %shard_map.52 = (f32[256,256]{1,0:T(8,128)}, f32[256,256]{1,0:T(8,128)}, f32[256,256]{1,0:T(8,128)}) custom-call(f32[768,256]{1,0:T(8,128)} %refs_0_.5, f32[128,768]{1,0:T(8,128)} %copy-done, f32[128,768]{1,0:T(8,128)} %copy-done.4, f32[256,256]{1,0:T(8,128)} %shard_map.51.refs_3_.refs_1_), custom_call_target="tpu_custom_call" | custom-call | flops 3000000000 | bytes 9000000 | tf_op jit(solution)/shard_map/pallas_call | solution.py:161
  26.5 3.9 %collective-permute-start.1 = (f32[256,256]{1,0:T(8,128)}, f32[256,256]{1,0:T(8,128)S(1)}, u32[]{:S(2)}, u32[]{:S(2)}) collective-permute-start(f32[256,256]{1,0:T(8,128)} %get-tuple-element.19), channel_id=1, source_target_pairs={{0,4},{4,0},{8,12},{12,8},{16,20},{20,16},{24,28},{28,24},{32,36},... | collective-permute-start | bytes 786440 | tf_op jit(solution)/shard_map/ppermute | solution.py:182
  30.4 3.3 %shard_map.55.refs_5_ = f32[256,512]{1,0:T(8,128)} custom-call(f32[128,768]{1,0:T(8,128)} %copy-done, f32[128,768]{1,0:T(8,128)} %copy-done.4, f32[768,512]{1,0:T(8,128)} %refs_3_.1, f32[256,256]{1,0:T(8,128)} %get-tuple-element.18.refs_2_.refs_3_), custom_call_target="tpu_custom_call" | custom-call | flops 3000000000 | bytes 9000000 | tf_op jit(solution)/shard_map/pallas_call | solution.py:161
  33.7 1.9 %collective-permute-start.5 = (f32[256,512]{1,0:T(8,128)}, f32[256,512]{1,0:T(8,128)S(1)}, u32[]{:S(2)}, u32[]{:S(2)}) collective-permute-start(f32[256,512]{1,0:T(8,128)} %shard_map.55.refs_5_), channel_id=1, source_target_pairs={{0,4},{4,0},{8,12},{12,8},{16,20},{20,16},{24,28},{28,24},{32,36},... | collective-permute-start | bytes 1572872 | tf_op jit(solution)/shard_map/ppermute | solution.py:182
  35.6 1.0 %collective-permute-done.1 = f32[256,256]{1,0:T(8,128)S(1)} collective-permute-done((f32[256,256]{1,0:T(8,128)}, f32[256,256]{1,0:T(8,128)S(1)}, u32[]{:S(2)}, u32[]{:S(2)}) %collective-permute-start.1) | collective-permute-done | bytes 262176 | tf_op jit(solution)/shard_map/ppermute | solution.py:182
  36.6 2.3 %all_gather.7.refs_3_.refs_2_ = f32[512,256]{1,0:T(8,128)} all-gather(f32[256,256]{1,0:T(8,128)S(1)} %collective-permute-done.1), channel_id=1, replica_groups={{0,1},{2,3},{4,5},{6,7},{8,9},{10,11},{12,13},{14,15},{16,17},{18,19},{..., dimensions={0}, use_global_device_ids=true | all-gather | bytes 786432 | tf_op jit(solution)/shard_map/all_gather | solution.py:186
  38.9 5.5 %shard_map.53 = (f32[256,256]{1,0:T(8,128)}, f32[256,256]{1,0:T(8,128)}, f32[256,256]{1,0:T(8,128)}) custom-call(f32[256,256]{1,0:T(8,128)} %get-tuple-element.17.refs_0_, f32[256,256]{1,0:T(8,128)} %shard_map.51.refs_3_.refs_1_, f32[256,256]{1,0:T(8,128)} %get-tuple-element.18.refs_2_.refs_3_, f32[512,256]{1,0:T(8,128)} %all_gather.7.refs_3_.refs_2_, ...), custom_call_target="tpu_custom_call" | custom-call | flops 20000000000 | bytes 60000000 | tf_op jit(solution)/shard_map/pallas_call | solution.py:161
  44.4 4.0 %collective-permute-start.2 = (f32[256,256]{1,0:T(8,128)}, f32[256,256]{1,0:T(8,128)S(1)}, u32[]{:S(2)}, u32[]{:S(2)}) collective-permute-start(f32[256,256]{1,0:T(8,128)} %get-tuple-element.21.refs_0_), channel_id=1, source_target_pairs={{0,4},{4,0},{8,12},{12,8},{16,20},{20,16},{24,28},{28,24},{32,36},... | collective-permute-start | bytes 786440 | tf_op jit(solution)/shard_map/ppermute | solution.py:182
  48.4 0.0 collective-permute-done.4.refs_4_
  48.4 0.5 collective-permute-done.5.refs_6_
  48.9 0.3 copy-done.1
  49.2 0.5 copy-done.2
  49.7 4.2 %shard_map.56 = (f32[256,512]{1,0:T(8,128)}, f32[256,512]{1,0:T(8,128)}) custom-call(f32[256,256]{1,0:T(8,128)} %get-tuple-element.24.refs_0_, f32[256,256]{1,0:T(8,128)} %get-tuple-element.25.refs_1_.refs_4_, f32[512,256]{1,0:T(8,128)} %all_gather.7.refs_3_.refs_2_, f32[256,512]{1,0:T(8,128)} %get-tuple-element.26.refs_3_, f32[256,512]{1,0:T(8,128)} %copy-done.1, ...), custom_call_target="tpu_custom_call" | custom-call | flops 4000000000 | bytes 12000000 | tf_op jit(solution)/shard_map/pallas_call | solution.py:161
  53.9 1.9 %collective-permute-start.6 = (f32[256,512]{1,0:T(8,128)}, f32[256,512]{1,0:T(8,128)S(1)}, u32[]{:S(2)}, u32[]{:S(2)}) collective-permute-start(f32[256,512]{1,0:T(8,128)} %get-tuple-element.27.refs_3_), channel_id=1, source_target_pairs={{0,12},{4,8},{8,4},{12,0},{16,28},{20,24},{24,20},{28,16},{32,44},... | collective-permute-start | bytes 1572872 | tf_op jit(solution)/shard_map/ppermute | solution.py:182
  55.8 0.0 collective-permute-done.2.refs_1_
  55.8 0.0 copy-start.5
  55.8 0.7 copy-done.5
  56.5 6.4 %shard_map.54 = (f32[256,256]{1,0:T(8,128)}, f32[256,256]{1,0:T(8,128)}) custom-call(f32[256,256]{1,0:T(8,128)} %get-tuple-element.21.refs_0_, f32[256,256]{1,0:T(8,128)} %copy-done.5), custom_call_target="tpu_custom_call" | custom-call | flops 6000000000 | bytes 18000000 | tf_op jit(solution)/shard_map/pallas_call | solution.py:161
  62.9 5.3 %collective-permute-start.3 = (f32[256,256]{1,0:T(8,128)}, f32[256,256]{1,0:T(8,128)S(1)}, u32[]{:S(2)}, u32[]{:S(2)}) collective-permute-start(f32[256,256]{1,0:T(8,128)} %get-tuple-element.23.refs_1_), channel_id=1, source_target_pairs={{0,12},{4,8},{8,4},{12,0},{16,28},{20,24},{24,20},{28,16},{32,44},... | collective-permute-start | bytes 786440 | tf_op jit(solution)/shard_map/ppermute | solution.py:182
  68.2 4.4 %shard_map.57 = (f32[768,512]{1,0:T(8,128)}, f32[256,768]{1,0:T(8,128)}, f32[64,768]{1,0:T(8,128)}) custom-call(f32[768,256]{1,0:T(8,128)} %refs_0_.5, f32[128,768]{1,0:T(8,128)} %copy-done, f32[128,768]{1,0:T(8,128)} %copy-done.4, f32[768,512]{1,0:T(8,128)} %refs_3_.1, f32[256,256]{1,0:T(8,128)} %get-tuple-element.25.refs_1_.refs_4_, ...), custom_call_target="tpu_custom_call" | custom-call | flops 4000000000 | bytes 12000000 | tf_op jit(solution)/shard_map/pallas_call | solution.py:161
  72.7 3.5 %collective-permute-done.3.refs_2_ = f32[256,256]{1,0:T(8,128)S(1)} collective-permute-done((f32[256,256]{1,0:T(8,128)}, f32[256,256]{1,0:T(8,128)S(1)}, u32[]{:S(2)}, u32[]{:S(2)}) %collective-permute-start.3) | collective-permute-done | bytes 262176 | tf_op jit(solution)/shard_map/ppermute | solution.py:182
  76.2 0.0 collective-permute-done.6.refs_4_
  76.2 0.7 copy-done.6
  76.9 0.2 copy-done.3
  77.1 7.1 %shard_map.58 = f32[768,512]{1,0:T(8,128)} custom-call(f32[256,256]{1,0:T(8,128)} %get-tuple-element.22.refs_0_, f32[256,256]{1,0:T(8,128)} %get-tuple-element.23.refs_1_, f32[256,256]{1,0:T(8,128)} %copy-done.6, f32[256,512]{1,0:T(8,128)} %get-tuple-element.27.refs_3_, f32[256,512]{1,0:T(8,128)} %copy-done.3, f32[768,512]{1,0:T(8,128)} %get-tuple-element.29.refs_5_, ...), custom_call_target="tpu_custom_call" | custom-call | flops 7000000000 | bytes 21000000 | tf_op jit(solution)/shard_map/pallas_call | solution.py:161
  (7 shorter events, 0.0 us)
Async XLA Ops:
  2.9 11.6 %copy-start = (f32[128,768]{1,0:T(8,128)}, f32[128,768]{1,0:T(8,128)S(1)}, u32[]{:S(2)}) copy-start(f32[128,768]{1,0:T(8,128)S(1)} %all_gather.6.refs_1_.refs_0_) | copy-start | bytes 1179652
  2.9 19.0 %collective-permute-start = (f32[128,768]{1,0:T(8,128)S(1)}, f32[128,768]{1,0:T(8,128)S(1)}, u32[]{:S(2)}, u32[]{:S(2)}) collective-permute-start(f32[128,768]{1,0:T(8,128)S(1)} %all_gather.6.refs_1_.refs_0_), channel_id=1, source_target_pairs={{0,2},{1,3},{2,0},{3,1},{4,6},{5,7},{6,4},{7,5},{8,10},{9,11},{10,... | collective-permute-start | bytes 1179656 | tf_op jit(solution)/shard_map/ppermute | solution.py:182
  14.5 33.9 %collective-permute-start.4 = (f32[256,512]{1,0:T(8,128)}, f32[256,512]{1,0:T(8,128)S(1)}, u32[]{:S(2)}, u32[]{:S(2)}) collective-permute-start(f32[256,512]{1,0:T(8,128)} %get-tuple-element.26.refs_3_), channel_id=1, source_target_pairs={{0,4},{4,0},{8,12},{12,8},{16,20},{20,16},{24,28},{28,24},{32,36},... | collective-permute-start | bytes 1572872 | tf_op jit(solution)/shard_map/ppermute | solution.py:182
  22.0 0.7 copy-start.4
  26.5 10.2 %collective-permute-start.1 = (f32[256,256]{1,0:T(8,128)}, f32[256,256]{1,0:T(8,128)S(1)}, u32[]{:S(2)}, u32[]{:S(2)}) collective-permute-start(f32[256,256]{1,0:T(8,128)} %get-tuple-element.19), channel_id=1, source_target_pairs={{0,4},{4,0},{8,12},{12,8},{16,20},{20,16},{24,28},{28,24},{32,36},... | collective-permute-start | bytes 786440 | tf_op jit(solution)/shard_map/ppermute | solution.py:182
  33.7 15.2 %collective-permute-start.5 = (f32[256,512]{1,0:T(8,128)}, f32[256,512]{1,0:T(8,128)S(1)}, u32[]{:S(2)}, u32[]{:S(2)}) collective-permute-start(f32[256,512]{1,0:T(8,128)} %shard_map.55.refs_5_), channel_id=1, source_target_pairs={{0,4},{4,0},{8,12},{12,8},{16,20},{20,16},{24,28},{28,24},{32,36},... | collective-permute-start | bytes 1572872 | tf_op jit(solution)/shard_map/ppermute | solution.py:182
  44.4 11.4 %collective-permute-start.2 = (f32[256,256]{1,0:T(8,128)}, f32[256,256]{1,0:T(8,128)S(1)}, u32[]{:S(2)}, u32[]{:S(2)}) collective-permute-start(f32[256,256]{1,0:T(8,128)} %get-tuple-element.21.refs_0_), channel_id=1, source_target_pairs={{0,4},{4,0},{8,12},{12,8},{16,20},{20,16},{24,28},{28,24},{32,36},... | collective-permute-start | bytes 786440 | tf_op jit(solution)/shard_map/ppermute | solution.py:182
  48.4 0.8 copy-start.1
  48.9 0.8 copy-start.2
  53.9 22.3 %collective-permute-start.6 = (f32[256,512]{1,0:T(8,128)}, f32[256,512]{1,0:T(8,128)S(1)}, u32[]{:S(2)}, u32[]{:S(2)}) collective-permute-start(f32[256,512]{1,0:T(8,128)} %get-tuple-element.27.refs_3_), channel_id=1, source_target_pairs={{0,12},{4,8},{8,4},{12,0},{16,28},{20,24},{24,20},{28,16},{32,44},... | collective-permute-start | bytes 1572872 | tf_op jit(solution)/shard_map/ppermute | solution.py:182
  55.8 0.7 copy-start.5
  62.9 13.3 %collective-permute-start.3 = (f32[256,256]{1,0:T(8,128)}, f32[256,256]{1,0:T(8,128)S(1)}, u32[]{:S(2)}, u32[]{:S(2)}) collective-permute-start(f32[256,256]{1,0:T(8,128)} %get-tuple-element.23.refs_1_), channel_id=1, source_target_pairs={{0,12},{4,8},{8,4},{12,0},{16,28},{20,24},{24,20},{28,16},{32,44},... | collective-permute-start | bytes 786440 | tf_op jit(solution)/shard_map/ppermute | solution.py:182
  76.2 0.7 copy-start.6
  76.2 0.9 %copy-start.3 = (f32[256,512]{1,0:T(8,128)}, f32[256,512]{1,0:T(8,128)S(1)}, u32[]{:S(2)}) copy-start(f32[256,512]{1,0:T(8,128)S(1)} %collective-permute-done.6.refs_4_) | copy-start | bytes 1572868

commit v3 on v2

v3 whole, which is shorter than its diff:
```python
import jax
import jax.numpy as jnp
from jax import lax
from jax.experimental import pallas as pl
from jax.experimental.pallas import tpu as pltpu
from jax.sharding import PartitionSpec as P

F32 = jnp.float32
BF16 = jnp.bfloat16
NN = (((1,), (0,)), ((), ()))
NT = (((1,), (1,)), ((), ()))
VMEM_BYTES = 20 * 2**20


def halves(x):
    high = x.astype(BF16)
    low = (x - high.astype(F32)).astype(BF16)
    return high, low


def pass_dot(a, b, dims):
    return lax.dot_general(a, b, dims, preferred_element_type=F32)


def dot3(a, b, dims=NN):
    a_high, a_low = halves(a)
    b_high, b_low = halves(b)
    cross = pass_dot(a_high, b_low, dims) + pass_dot(a_low, b_high, dims)
    return pass_dot(a_high, b_high, dims) + cross


def dot6(a, b, dims=NN):
    return lax.dot_general(a, b, dims, precision=lax.Precision.HIGHEST, preferred_element_type=F32)


def unit_matrix(n):
    return (lax.broadcasted_iota(jnp.int32, (n, n), 0) == lax.broadcasted_iota(jnp.int32, (n, n), 1)).astype(F32)


def invert(matrices, works, floor):
    n = matrices[0].shape[0]
    eye = unit_matrix(n)
    low = floor * 0.98
    tops = [jnp.max(jnp.sum(jnp.abs(m[...]), axis=0, keepdims=True), axis=1, keepdims=True) for m in matrices]
    top = tops[0]
    for other in tops[1:]:
        top = jnp.maximum(top, other)
    top = jnp.max(top) * 1.02
    scale = 2.0 / (top + low)
    spread = (top - low) / (top + low)
    square = spread * spread
    gain = 2.0 / (2.0 - square)
    for m, w in zip(matrices, works):
        w[...] = (gain * scale) * (2.0 * eye - scale * m[...])

    def coarse(state):
        square = state * state
        gain = 2.0 / (2.0 - square)
        for m, w in zip(matrices, works):
            x = w[...]
            w[...] = gain * (2.0 * x - dot3(x, dot3(m[...], x)))
        return square / (2.0 - square)

    lax.while_loop(lambda state: state > 1e-2, coarse, square / (2.0 - square))
    wide = top > 256.0 * low
    steps = jnp.where(wide, 4, 2)

    def fine(_, carry):
        for m, w in zip(matrices, works):
            x = w[...]
            w[...] = x + dot3(x, eye - dot6(m[...], x))
        return carry

    lax.fori_loop(0, steps, fine, 0)
    return wide


def flag(wide):
    return jnp.broadcast_to(jnp.where(wide, 1.0, 0.0), (8, 128)).astype(F32)


def refine_schur(schur, start):
    eye = unit_matrix(schur.shape[0])
    spread = 1.0 / 7.0
    x = start * (8.0 / 7.0)
    for step in range(2):
        square = spread * spread
        gain = 2.0 / (2.0 - square)
        spread = square / (2.0 - square)
        x = gain * (2.0 * x - dot3(x, dot3(schur, x)))
    return x + dot3(x, eye - dot6(schur, x))


def leaf_kernel(coupling, y1_ref, z_ref, cap_ref, y_ref):
    y1 = y1_ref[...]
    y1t = y1.T
    cap_ref[...] = dot6(y1t, y1) + (2.0 * coupling) * unit_matrix(y1.shape[1])
    y_ref[...] = dot3(y1t, z_ref[...])


def invert_kernel(coupling, cap_ref, inv_ref, wide_ref):
    wide_ref[...] = flag(invert([cap_ref], [inv_ref], 2.0 * coupling))


def cross_kernel(coupling, wide_ref, y1_ref, near_ref, far_ref, cap_ref, inv_ref, bt_ref, ht_ref, sent_ref, dd_ref):
    y2t = jnp.concatenate([near_ref[...], far_ref[...]], axis=0)
    bt_ref[...] = dot6(y2t, y1_ref[...])
    ht_ref[...] = dot6(bt_ref[...], inv_ref[...])

    @pl.when(wide_ref[0, 0] > 0.5)
    def _():
        h = ht_ref[...]
        ht_ref[...] = h + dot3(bt_ref[...] - dot6(h, cap_ref[...]), inv_ref[...])

    sent_ref[...] = jnp.where(lax.axis_index("cols") % 2 == 0, inv_ref[...], ht_ref[...])
    dd_ref[...] = dot6(y2t, y2t, NT)


def project_kernel(coupling, near_ref, far_ref, z_ref, y_ref, ht_ref, w_ref, v_ref):
    z = z_ref[...]
    half = near_ref.shape[0]
    w_ref[:half] = dot3(near_ref[...], z)
    w_ref[half:] = dot3(far_ref[...], z)
    v_ref[...] = w_ref[...] - dot3(ht_ref[...], y_ref[...])


def pair_kernel(coupling, wide_ref, cap_ref, inv_ref, bt_ref, other_ref, dd_ref, schur_ref, t_ref, et_ref, p_ref):
    n = cap_ref.shape[0]
    bt = bt_ref[...]
    schur_ref[...] = cap_ref[...] - coupling * coupling * other_ref[:n]
    t_ref[...] = refine_schur(schur_ref[...], inv_ref[...])
    et_ref[...] = dot6(bt + coupling * other_ref[n:], t_ref[...])

    @pl.when(wide_ref[0, 0] > 0.5)
    def _():
        et = et_ref[...]
        et_ref[...] = et + dot3(bt_ref[...] + coupling * other_ref[n:] - dot6(et, schur_ref[...]), t_ref[...])

    p_ref[...] = dd_ref[...] - dot6(et_ref[...], bt, NT)


def rhs_kernel(coupling, wide_ref, schur_ref, t_ref, et_ref, y_ref, other_ref, other_y_ref, w_ref, other_v_ref, f_ref, ez_ref):
    n = t_ref.shape[0]
    g = y_ref[...] + coupling * dot3(other_ref[:n], other_y_ref[...])
    f_ref[...] = w_ref[...] + other_v_ref[...] - dot3(et_ref[...], g)
    ez_ref[...] = dot3(t_ref[...], g)

    @pl.when(wide_ref[0, 0] > 0.5)
    def _():
        e = ez_ref[...]
        ez_ref[...] = e + dot3(t_ref[...], g - dot6(schur_ref[...], e))


def apply_kernel(coupling, y1_ref, near_ref, far_ref, z_ref, et_ref, ez_ref, z1_ref, high_ref, low_ref, updated_ref, ut_ref):
    y1 = y1_ref[...]
    half = near_ref.shape[0]
    part = updated_ref.shape[0]
    change = dot3(et_ref[...], y1, NT)
    ut_ref[:half] = near_ref[...] - change[:half]
    ut_ref[half:] = far_ref[...] - change[half:]
    start = (lax.axis_index("cols") % 2) * part
    updated_ref[...] = ut_ref[pl.ds(pl.multiple_of(start, part), part), :]
    high_ref[...], low_ref[...] = halves(ut_ref[...].T)
    z1_ref[...] = z_ref[...] - dot3(y1, ez_ref[...])


def quad_kernel(coupling, p_ref, other_p_ref, cap_ref, inv_ref, wide_ref):
    cap_ref[...] = p_ref[...] + other_p_ref[...] + (2.0 * coupling) * unit_matrix(p_ref.shape[0])
    wide_ref[...] = flag(invert([cap_ref], [inv_ref], 2.0 * coupling))


def last_kernel(coupling, wide_ref, cap_ref, inv_ref, far_ref, f_ref, f_far_ref, z1_ref, high_ref, low_ref, out_ref, k_ref):
    schur = cap_ref[...] - coupling * coupling * far_ref[...]
    t = refine_schur(schur, inv_ref[...])
    g = f_ref[...] + coupling * dot3(far_ref[...], f_far_ref[...])
    k_ref[...] = dot3(t, g)

    @pl.when(wide_ref[0, 0] > 0.5)
    def _():
        k = k_ref[...]
        k_ref[...] = k + dot3(t, g - dot6(schur, k))

    k_high, k_low = halves(k_ref[...])
    high = high_ref[...]
    change = pass_dot(high, k_low, NN) + pass_dot(low_ref[...], k_high, NN)
    out_ref[...] = z1_ref[...] - pass_dot(high, k_high, NN) - change


def call(kernel, outs, *args, micros, scratch=()):
    return pl.pallas_call(
        kernel,
        out_shape=[o if isinstance(o, jax.ShapeDtypeStruct) else jax.ShapeDtypeStruct(o, F32) for o in outs],
        in_specs=[pl.BlockSpec(memory_space=pltpu.VMEM)] * len(args),
        out_specs=[pl.BlockSpec(memory_space=pltpu.VMEM)] * len(outs),
        scratch_shapes=[pltpu.VMEM(shape, F32) for shape in scratch],
        compiler_params=pltpu.CompilerParams(vmem_limit_bytes=VMEM_BYTES),
        cost_estimate=pl.CostEstimate(flops=int(micros * 1e9), bytes_accessed=int(micros * 3e6), transcendentals=0),
    )(*args)


def shards(level1_basis, level2_basis, probes):
    points, rank = level1_basis.shape
    part, columns = level2_basis.shape[0], probes.shape[1]
    coupling = points / 3.0
    n_cols = lax.axis_size("cols")
    square, tall, tile = (rank, rank), (rank, columns), (8, 128)

    def run(kernel, outs, *args, **kw):
        return call(lambda *refs: kernel(coupling, *refs), outs, *args, **kw)

    def swap(value, bits, axis="rows"):
        return lax.ppermute(value, axis, [(i, i ^ bits) for i in range(lax.axis_size(axis))])

    def core_gather(value):
        groups = [[2 * i, 2 * i + 1] for i in range(n_cols // 2)]
        return lax.all_gather(value, "cols", axis=0, tiled=True, axis_index_groups=groups)

    near = core_gather(level2_basis)
    far = swap(near, 2, "cols")
    cap, y = run(leaf_kernel, [square, tall], level1_basis, probes, micros=4)
    other_y = swap(y, 1)
    inv, wide = run(invert_kernel, [square, tile], cap, micros=10)
    bt, ht, sent, dd = run(cross_kernel, [square] * 4, wide, level1_basis, near, far, cap, inv, micros=4)
    other_half = swap(sent, 1)
    w, v = run(project_kernel, [tall] * 2, near, far, probes, y, ht, micros=3)
    other_v = swap(v, 1)
    other = core_gather(other_half)
    schur, t, et, p = run(pair_kernel, [square] * 4, wide, cap, inv, bt, other, dd, micros=20)
    other_p = swap(p, 1)
    f, ez = run(rhs_kernel, [tall] * 2, wide, schur, t, et, y, other, other_y, w, other_v, micros=4)
    f_far = swap(f, 3)
    cap_two, inv_two, wide_two = run(quad_kernel, [square, square, tile], p, other_p, micros=6)
    far_two = swap(inv_two, 3)
    half = jax.ShapeDtypeStruct((points, rank), BF16)
    z1, high, low, updated = run(
        apply_kernel,
        [(points, columns), half, half, (part, points)],
        *(level1_basis, near, far, probes, et, ez),
        micros=4,
        scratch=[(rank, points)],
    )
    (out,) = run(
        last_kernel,
        [(points, columns)],
        *(wide_two, cap_two, inv_two, far_two, f, f_far, z1, high, low),
        micros=7,
        scratch=[(rank, columns)],
    )
    return out, updated


def solution(mesh):
    return jax.shard_map(
        shards,
        mesh=mesh,
        in_specs=(P("rows", None), P("cols", "rows"), P("rows", "cols")),
        out_specs=(P("rows", "cols"), P("cols", "rows")),
        check_vma=False,
    )
```

time: 84.7 us -> 74.9 us (0.88)
  Pallas kernels: 44.2 us -> 23.8 us
  waiting for transfers between devices: 5.05 us -> 20.8 us
  starting transfers between devices: 26.5 us -> 22 us
    pallas_call x9, Pallas kernels: 44.2 us -> 23.8 us  [call(): pl.pallas_call(kernel, out_shape=[o if isinstance(o, jax.ShapeDtypeStruct...]
    ppermute x7, waiting for transfers between devices: 5.05 us -> 20.8 us  [swap(): lax.ppermute(value, axis, [(i, i ^ bits) for i in range(lax.axis_size(axi...]
    ppermute x7, starting transfers between devices: 26.5 us -> 22 us  [swap(): lax.ppermute(value, axis, [(i, i ^ bits) for i in range(lax.axis_size(axi...]
    unnamed x14 -> x8, local copies, waits for them, and re-layouts: 3.13 us -> 2.55 us
  transfers between devices with their start and end apart: 7 -> 7, of which waited for: 3 -> 4; matrix products, arithmetic and copies ran while one was open for 0% -> 0% of each run, Pallas kernels for 44% -> 25%
where the time goes in v3:
time: 74.9 us; the launch traced here: 74.5 us
  Pallas kernels  23.8 us (32%)
  starting transfers between devices  22 us (29%)
  waiting for transfers between devices  20.8 us (28%)
  blocking collectives  4.47 us (6%)
  local copies, waits for them, and re-layouts  2.55 us (3%)
  between operations  0.8 us (1%)
    pallas_call x9, Pallas kernels, call(): pl.pallas_call(kernel, out_shape=[o if isinstance(o, jax.ShapeDtypeStruct...  23.8 us
    ppermute x7, starting transfers between devices, swap(): lax.ppermute(value, axis, [(i, i ^ bits) for i in range(lax.axis_size(axi...  22 us
    ppermute x7, waiting for transfers between devices, swap(): lax.ppermute(value, axis, [(i, i ^ bits) for i in range(lax.axis_size(axi...  20.8 us
    all_gather x2, blocking collectives, core_gather(): lax.all_gather(value, 'cols', axis=0, tiled=True, axis_index_groups=groups)  4.47 us
    unnamed x8, local copies, waits for them, and re-layouts  2.55 us
  transfers between devices with their start and end apart: 7, of which 4 were waited for; matrix products, arithmetic and copies ran while one was open for 0% of the time, Pallas kernels for 25%

profile of v3, /device:TPU:16, one launch (start us, length us, event | category | flops | bytes accessed | tf_op | source)
XLA Modules:
  0.0 74.5 jit_solution(421525708420903956)
XLA Ops:
  0.6 2.3 %all_gather.6.refs_2_.refs_0_.refs_1_ = f32[128,768]{1,0:T(8,128)S(1)} all-gather(f32[64,768]{1,0:T(8,128)} %param.4), channel_id=1, replica_groups={{0,1},{2,3},{4,5},{6,7},{8,9},{10,11},{12,13},{14,15},{16,17},{18,19},{..., dimensions={0}, use_global_device_ids=true | all-gather | bytes 589824 | tf_op jit(solution)/shard_map/all_gather | solution.py:216
  2.9 7.6 %collective-permute-start = (f32[128,768]{1,0:T(8,128)S(1)}, f32[128,768]{1,0:T(8,128)S(1)}, u32[]{:S(2)}, u32[]{:S(2)}) collective-permute-start(f32[128,768]{1,0:T(8,128)S(1)} %all_gather.6.refs_2_.refs_0_.refs_1_), channel_id=1, source_target_pairs={{0,2},{1,3},{2,0},{3,1},{4,6},{5,7},{6,4},{7,5},{8,10},{9,11},{10,... | collective-permute-start | bytes 1179656 | tf_op jit(solution)/shard_map/ppermute | solution.py:212
  10.5 0.0 copy-start
  10.6 1.4 %copy-done = f32[768,512]{1,0:T(8,128)S(1)} copy-done((f32[768,512]{1,0:T(8,128)S(1)}, f32[768,512]{1,0:T(8,128)}, u32[]{:S(2)}) %copy-start) | copy-done | bytes 1572888
  12.0 1.1 %copy-done.2 = f32[768,256]{1,0:T(8,128)S(1)} copy-done((f32[768,256]{1,0:T(8,128)S(1)}, f32[768,256]{1,0:T(8,128)}, u32[]{:S(2)}) %copy-start.2) | copy-done | bytes 786456
  13.1 1.5 %shard_map.50 = (f32[256,256]{1,0:T(8,128)S(1)}, f32[256,512]{1,0:T(8,128)S(1)}) custom-call(f32[768,256]{1,0:T(8,128)S(1)} %copy-done.2, f32[768,512]{1,0:T(8,128)S(1)} %copy-done), custom_call_target="tpu_custom_call" | custom-call | flops 4000000000 | bytes 12000000 | tf_op jit(solution)/shard_map/pallas_call | solution.py:190
  14.6 1.9 %collective-permute-start.4 = (f32[256,512]{1,0:T(8,128)S(1)}, f32[256,512]{1,0:T(8,128)S(1)}, u32[]{:S(2)}, u32[]{:S(2)}) collective-permute-start(f32[256,512]{1,0:T(8,128)S(1)} %get-tuple-element.38.refs_3_.refs_4_), channel_id=1, source_target_pairs={{0,4},{4,0},{8,12},{12,8},{16,20},{20,16},{24,28},{28,24},{32,36},... | collective-permute-start | bytes 1572872 | tf_op jit(solution)/shard_map/ppermute | solution.py:212
  16.5 0.0 copy-start.3
  16.5 3.9 %shard_map.51 = (f32[256,256]{1,0:T(8,128)S(1)}, f32[8,128]{1,0:T(8,128)S(1)}) custom-call(f32[256,256]{1,0:T(8,128)S(1)} %get-tuple-element.25.refs_0_.refs_4_.refs_1_), custom_call_target="tpu_custom_call" | custom-call | flops 10000000000 | bytes 30000000 | tf_op jit(solution)/shard_map/pallas_call | solution.py:190
  20.5 0.0 collective-permute-done.refs_3_.refs_1_.refs_2_
  20.5 0.0 copy-done.3
  20.5 0.0 copy-start.1
  20.5 2.3 %shard_map.52 = (f32[256,256]{1,0:T(8,128)S(1)}, f32[256,256]{1,0:T(8,128)S(1)}, f32[256,256]{1,0:T(8,128)S(1)}, f32[256,256]{1,0:T(8,128)S(1)}) custom-call(f32[8,128]{1,0:T(8,128)S(1)} %get-tuple-element.26.refs_0_, f32[768,256]{1,0:T(8,128)S(1)} %copy-done.3, f32[128,768]{1,0:T(8,128)S(1)} %all_gather.6.refs_2_.refs_0_.refs_1_, ...), custom_call_target="tpu_custom_call" | custom-call | flops 4000000000 | bytes 12000000 | tf_op jit(solution)/shard_map/pallas_call | solution.py:190
  22.8 3.9 %collective-permute-start.1 = (f32[256,256]{1,0:T(8,128)S(1)}, f32[256,256]{1,0:T(8,128)S(1)}, u32[]{:S(2)}, u32[]{:S(2)}) collective-permute-start(f32[256,256]{1,0:T(8,128)S(1)} %get-tuple-element.29), channel_id=1, source_target_pairs={{0,4},{4,0},{8,12},{12,8},{16,20},{20,16},{24,28},{28,24},{32,36},... | collective-permute-start | bytes 786440 | tf_op jit(solution)/shard_map/ppermute | solution.py:212
  26.7 0.0 copy-done.1
  26.7 1.1 %shard_map.55 = (f32[256,512]{1,0:T(8,128)S(1)}, f32[256,512]{1,0:T(8,128)S(1)}) custom-call(f32[128,768]{1,0:T(8,128)S(1)} %all_gather.6.refs_2_.refs_0_.refs_1_, f32[128,768]{1,0:T(8,128)S(1)} %collective-permute-done.refs_3_.refs_1_.refs_2_, f32[768,512]{1,0:T(8,128)S(1)} %copy-done.1, f32[256,512]{1,0:T(8,128)S(1)} %get-tuple-element.38.refs_3_.refs_4_, ...), custom_call_target="tpu_custom_call" | custom-call | flops 3000000000 | bytes 9000000 | tf_op jit(solution)/shard_map/pallas_call | solution.py:190
  27.8 1.9 %collective-permute-start.5 = (f32[256,512]{1,0:T(8,128)S(1)}, f32[256,512]{1,0:T(8,128)S(1)}, u32[]{:S(2)}, u32[]{:S(2)}) collective-permute-start(f32[256,512]{1,0:T(8,128)S(1)} %get-tuple-element.41), channel_id=1, source_target_pairs={{0,4},{4,0},{8,12},{12,8},{16,20},{20,16},{24,28},{28,24},{32,36},... | collective-permute-start | bytes 1572872 | tf_op jit(solution)/shard_map/ppermute | solution.py:212
  29.8 7.2 %collective-permute-done.1 = f32[256,256]{1,0:T(8,128)S(1)} collective-permute-done((f32[256,256]{1,0:T(8,128)S(1)}, f32[256,256]{1,0:T(8,128)S(1)}, u32[]{:S(2)}, u32[]{:S(2)}) %collective-permute-start.1) | collective-permute-done | bytes 262176 | tf_op jit(solution)/shard_map/ppermute | solution.py:212
  36.9 2.2 %all_gather.7.refs_4_.refs_5_ = f32[512,256]{1,0:T(8,128)S(1)} all-gather(f32[256,256]{1,0:T(8,128)S(1)} %collective-permute-done.1), channel_id=1, replica_groups={{0,1},{2,3},{4,5},{6,7},{8,9},{10,11},{12,13},{14,15},{16,17},{18,19},{..., dimensions={0}, use_global_device_ids=true | all-gather | bytes 786432 | tf_op jit(solution)/shard_map/all_gather | solution.py:216
  39.1 3.1 %shard_map.53 = (f32[256,256]{1,0:T(8,128)S(1)}, f32[256,256]{1,0:T(8,128)S(1)}, f32[256,256]{1,0:T(8,128)S(1)}, f32[256,256]{1,0:T(8,128)S(1)}) custom-call(f32[8,128]{1,0:T(8,128)S(1)} %get-tuple-element.26.refs_0_, f32[256,256]{1,0:T(8,128)S(1)} %get-tuple-element.25.refs_0_.refs_4_.refs_1_, f32[256,256]{1,0:T(8,128)S(1)} %get-tuple-element.27.refs_5_.refs_2_, ...), custom_call_target="tpu_custom_call" | custom-call | flops 20000000000 | bytes 60000000 | tf_op jit(solution)/shard_map/pallas_call | solution.py:190
  42.2 1.9 %collective-permute-start.2 = (f32[256,256]{1,0:T(8,128)S(1)}, f32[256,256]{1,0:T(8,128)S(1)}, u32[]{:S(2)}, u32[]{:S(2)}) collective-permute-start(f32[256,256]{1,0:T(8,128)S(1)} %get-tuple-element.31.refs_0_), channel_id=1, source_target_pairs={{0,4},{4,0},{8,12},{12,8},{16,20},{20,16},{24,28},{28,24},{32,36},... | collective-permute-start | bytes 786440 | tf_op jit(solution)/shard_map/ppermute | solution.py:212
  44.1 0.0 collective-permute-done.4.refs_6_
  44.1 3.1 %collective-permute-done.5.refs_8_ = f32[256,512]{1,0:T(8,128)S(1)} collective-permute-done((f32[256,512]{1,0:T(8,128)S(1)}, f32[256,512]{1,0:T(8,128)S(1)}, u32[]{:S(2)}, u32[]{:S(2)}) %collective-permute-start.5) | collective-permute-done | bytes 524320 | tf_op jit(solution)/shard_map/ppermute | solution.py:212
  47.2 1.0 %shard_map.56 = (f32[256,512]{1,0:T(8,128)S(1)}, f32[256,512]{1,0:T(8,128)S(1)}) custom-call(f32[8,128]{1,0:T(8,128)S(1)} %get-tuple-element.26.refs_0_, f32[256,256]{1,0:T(8,128)S(1)} %get-tuple-element.35.refs_1_, f32[256,256]{1,0:T(8,128)S(1)} %get-tuple-element.36.refs_2_, f32[256,256]{1,0:T(8,128)S(1)} %get-tuple-element.37.refs_3_.refs_4_, ...), custom_call_target="tpu_custom_call" | custom-call | flops 4000000000 | bytes 12000000 | tf_op jit(solution)/shard_map/pallas_call | solution.py:190
  48.2 1.9 %collective-permute-start.6 = (f32[256,512]{1,0:T(8,128)S(1)}, f32[256,512]{1,0:T(8,128)S(1)}, u32[]{:S(2)}, u32[]{:S(2)}) collective-permute-start(f32[256,512]{1,0:T(8,128)S(1)} %get-tuple-element.42.refs_4_), channel_id=1, source_target_pairs={{0,12},{4,8},{8,4},{12,0},{16,28},{20,24},{24,20},{28,16},{32,44},... | collective-permute-start | bytes 1572872 | tf_op jit(solution)/shard_map/ppermute | solution.py:212
  50.1 2.5 %collective-permute-done.2.refs_1_ = f32[256,256]{1,0:T(8,128)S(1)} collective-permute-done((f32[256,256]{1,0:T(8,128)S(1)}, f32[256,256]{1,0:T(8,128)S(1)}, u32[]{:S(2)}, u32[]{:S(2)}) %collective-permute-start.2) | collective-permute-done | bytes 262176 | tf_op jit(solution)/shard_map/ppermute | solution.py:212
  52.7 4.6 %shard_map.54 = (f32[256,256]{1,0:T(8,128)S(1)}, f32[256,256]{1,0:T(8,128)S(1)}, f32[8,128]{1,0:T(8,128)S(1)}) custom-call(f32[256,256]{1,0:T(8,128)S(1)} %get-tuple-element.31.refs_0_, f32[256,256]{1,0:T(8,128)S(1)} %collective-permute-done.2.refs_1_), custom_call_target="tpu_custom_call" | custom-call | flops 6000000000 | bytes 18000000 | tf_op jit(solution)/shard_map/pallas_call | solution.py:190
  57.3 2.8 %collective-permute-start.3 = (f32[256,256]{1,0:T(8,128)S(1)}, f32[256,256]{1,0:T(8,128)S(1)}, u32[]{:S(2)}, u32[]{:S(2)}) collective-permute-start(f32[256,256]{1,0:T(8,128)S(1)} %get-tuple-element.34.refs_2_), channel_id=1, source_target_pairs={{0,12},{4,8},{8,4},{12,0},{16,28},{20,24},{24,20},{28,16},{32,44},... | collective-permute-start | bytes 786440 | tf_op jit(solution)/shard_map/ppermute | solution.py:212
  60.1 1.4 %shard_map.57 = (f32[768,512]{1,0:T(8,128)S(1)}, bf16[768,256]{1,0:T(8,128)(2,1)S(1)}, bf16[768,256]{1,0:T(8,128)(2,1)S(1)}, f32[64,768]{1,0:T(8,128)}) custom-call(f32[768,256]{1,0:T(8,128)S(1)} %copy-done.3, f32[128,768]{1,0:T(8,128)S(1)} %all_gather.6.refs_2_.refs_0_.refs_1_, f32[128,768]{1,0:T(8,128)S(1)} %collective-permute-done.refs_3_.refs_1_.refs_2_, ...), custom_call_target="tpu_custom_call" | custom-call | flops 4000000000 | bytes 12000000 | tf_op jit(solution)/shard_map/pallas_call | solution.py:190
  61.5 8.1 %collective-permute-done.3.refs_3_ = f32[256,256]{1,0:T(8,128)S(1)} collective-permute-done((f32[256,256]{1,0:T(8,128)S(1)}, f32[256,256]{1,0:T(8,128)S(1)}, u32[]{:S(2)}, u32[]{:S(2)}) %collective-permute-start.3) | collective-permute-done | bytes 262176 | tf_op jit(solution)/shard_map/ppermute | solution.py:212
  69.6 0.0 collective-permute-done.6.refs_5_
  69.6 4.9 %shard_map.58 = f32[768,512]{1,0:T(8,128)} custom-call(f32[8,128]{1,0:T(8,128)S(1)} %get-tuple-element.32.refs_0_, f32[256,256]{1,0:T(8,128)S(1)} %get-tuple-element.33.refs_1_, f32[256,256]{1,0:T(8,128)S(1)} %get-tuple-element.34.refs_2_, f32[256,256]{1,0:T(8,128)S(1)} %collective-permute-done.3.refs_3_, f32[256,512]{1,0:T(8,128)S(1)} %get-tuple-element.42.refs_4_, ...), custom_call_target="tpu_custom_call" | custom-call | flops 7000000000 | bytes 21000000 | tf_op jit(solution)/shard_map/pallas_call | solution.py:190
  (1 shorter events, 0.0 us)
Async XLA Ops:
  2.9 17.5 %collective-permute-start = (f32[128,768]{1,0:T(8,128)S(1)}, f32[128,768]{1,0:T(8,128)S(1)}, u32[]{:S(2)}, u32[]{:S(2)}) collective-permute-start(f32[128,768]{1,0:T(8,128)S(1)} %all_gather.6.refs_2_.refs_0_.refs_1_), channel_id=1, source_target_pairs={{0,2},{1,3},{2,0},{3,1},{4,6},{5,7},{6,4},{7,5},{8,10},{9,11},{10,... | collective-permute-start | bytes 1179656 | tf_op jit(solution)/shard_map/ppermute | solution.py:212
  10.5 1.4 %copy-start = (f32[768,512]{1,0:T(8,128)S(1)}, f32[768,512]{1,0:T(8,128)}, u32[]{:S(2)}) copy-start(f32[768,512]{1,0:T(8,128)} %refs_3_.1) | copy-start | bytes 4718596
  12.0 1.1 %copy-start.2 = (f32[768,256]{1,0:T(8,128)S(1)}, f32[768,256]{1,0:T(8,128)}, u32[]{:S(2)}) copy-start(f32[768,256]{1,0:T(8,128)} %refs_0_.3) | copy-start | bytes 2359300
  14.6 29.5 %collective-permute-start.4 = (f32[256,512]{1,0:T(8,128)S(1)}, f32[256,512]{1,0:T(8,128)S(1)}, u32[]{:S(2)}, u32[]{:S(2)}) collective-permute-start(f32[256,512]{1,0:T(8,128)S(1)} %get-tuple-element.38.refs_3_.refs_4_), channel_id=1, source_target_pairs={{0,4},{4,0},{8,12},{12,8},{16,20},{20,16},{24,28},{28,24},{32,36},... | collective-permute-start | bytes 1572872 | tf_op jit(solution)/shard_map/ppermute | solution.py:212
  16.5 3.9 %copy-start.3 = (f32[768,256]{1,0:T(8,128)S(1)}, f32[768,256]{1,0:T(8,128)}, u32[]{:S(2)}) copy-start(f32[768,256]{1,0:T(8,128)} %refs_0_.3) | copy-start | bytes 2359300
  20.5 6.3 %copy-start.1 = (f32[768,512]{1,0:T(8,128)S(1)}, f32[768,512]{1,0:T(8,128)}, u32[]{:S(2)}) copy-start(f32[768,512]{1,0:T(8,128)} %refs_3_.1) | copy-start | bytes 4718596
  22.8 14.1 %collective-permute-start.1 = (f32[256,256]{1,0:T(8,128)S(1)}, f32[256,256]{1,0:T(8,128)S(1)}, u32[]{:S(2)}, u32[]{:S(2)}) collective-permute-start(f32[256,256]{1,0:T(8,128)S(1)} %get-tuple-element.29), channel_id=1, source_target_pairs={{0,4},{4,0},{8,12},{12,8},{16,20},{20,16},{24,28},{28,24},{32,36},... | collective-permute-start | bytes 786440 | tf_op jit(solution)/shard_map/ppermute | solution.py:212
  27.8 19.4 %collective-permute-start.5 = (f32[256,512]{1,0:T(8,128)S(1)}, f32[256,512]{1,0:T(8,128)S(1)}, u32[]{:S(2)}, u32[]{:S(2)}) collective-permute-start(f32[256,512]{1,0:T(8,128)S(1)} %get-tuple-element.41), channel_id=1, source_target_pairs={{0,4},{4,0},{8,12},{12,8},{16,20},{20,16},{24,28},{28,24},{32,36},... | collective-permute-start | bytes 1572872 | tf_op jit(solution)/shard_map/ppermute | solution.py:212
  42.2 10.5 %collective-permute-start.2 = (f32[256,256]{1,0:T(8,128)S(1)}, f32[256,256]{1,0:T(8,128)S(1)}, u32[]{:S(2)}, u32[]{:S(2)}) collective-permute-start(f32[256,256]{1,0:T(8,128)S(1)} %get-tuple-element.31.refs_0_), channel_id=1, source_target_pairs={{0,4},{4,0},{8,12},{12,8},{16,20},{20,16},{24,28},{28,24},{32,36},... | collective-permute-start | bytes 786440 | tf_op jit(solution)/shard_map/ppermute | solution.py:212
  48.2 21.4 %collective-permute-start.6 = (f32[256,512]{1,0:T(8,128)S(1)}, f32[256,512]{1,0:T(8,128)S(1)}, u32[]{:S(2)}, u32[]{:S(2)}) collective-permute-start(f32[256,512]{1,0:T(8,128)S(1)} %get-tuple-element.42.refs_4_), channel_id=1, source_target_pairs={{0,12},{4,8},{8,4},{12,0},{16,28},{20,24},{24,20},{28,16},{32,44},... | collective-permute-start | bytes 1572872 | tf_op jit(solution)/shard_map/ppermute | solution.py:212
  57.3 12.3 %collective-permute-start.3 = (f32[256,256]{1,0:T(8,128)S(1)}, f32[256,256]{1,0:T(8,128)S(1)}, u32[]{:S(2)}, u32[]{:S(2)}) collective-permute-start(f32[256,256]{1,0:T(8,128)S(1)} %get-tuple-element.34.refs_2_), channel_id=1, source_target_pairs={{0,12},{4,8},{8,4},{12,0},{16,28},{20,24},{24,20},{28,16},{32,44},... | collective-permute-start | bytes 786440 | tf_op jit(solution)/shard_map/ppermute | solution.py:212

commit v4 on v3

v4 whole, which is shorter than its diff:
```python
import jax
import jax.numpy as jnp
from jax import lax
from jax.experimental import pallas as pl
from jax.experimental.pallas import tpu as pltpu
from jax.sharding import PartitionSpec as P

F32 = jnp.float32
BF16 = jnp.bfloat16
NN = (((1,), (0,)), ((), ()))
NT = (((1,), (1,)), ((), ()))
VMEM_BYTES = 20 * 2**20


def halves(x):
    high = x.astype(BF16)
    low = (x - high.astype(F32)).astype(BF16)
    return high, low


def pass_dot(a, b, dims):
    return lax.dot_general(a, b, dims, preferred_element_type=F32)


def dot3(a, b, dims=NN):
    a_high, a_low = halves(a)
    b_high, b_low = halves(b)
    cross = pass_dot(a_high, b_low, dims) + pass_dot(a_low, b_high, dims)
    return pass_dot(a_high, b_high, dims) + cross


def dot6(a, b, dims=NN):
    return lax.dot_general(a, b, dims, precision=lax.Precision.HIGHEST, preferred_element_type=F32)


def unit_matrix(n):
    return (lax.broadcasted_iota(jnp.int32, (n, n), 0) == lax.broadcasted_iota(jnp.int32, (n, n), 1)).astype(F32)


def invert(matrix, floor, store, pair):
    n = matrix.shape[0]
    eye = unit_matrix(n)
    low = floor * 0.98
    top = jnp.max(jnp.sum(jnp.abs(matrix[...]), axis=0, keepdims=True)) * 1.02
    scale = 2.0 / (top + low)
    spread = (top - low) / (top + low)
    narrow = top < 64.0 * low
    wide = top > 256.0 * low

    @pl.when(narrow)
    def _():
        pair[:n] = scale * eye
        pair[n:] = eye - scale * matrix[...]

        def step(state):
            square = state * state
            gain = 2.0 / (2.0 - square)
            both = pair[...]
            product = dot3(both, both[n:])
            pair[:n] = gain * (both[:n] + product[:n])
            pair[n:] = (1.0 - gain) * eye + gain * product[n:]
            return square / (2.0 - square)

        lax.while_loop(lambda state: state > 1e-3, step, spread)
        x = pair[:n]
        store[...] = x + dot3(x, eye - dot6(matrix[...], x))

    @pl.when(jnp.logical_not(narrow))
    def _():
        store[...] = scale * eye

        def coarse(state):
            square = state * state
            gain = 2.0 / (2.0 - square)
            x = store[...]
            store[...] = gain * (2.0 * x - dot3(x, dot3(matrix[...], x)))
            return square / (2.0 - square)

        lax.while_loop(lambda state: state > 1e-2, coarse, spread)

        def fine(_, carry):
            x = store[...]
            store[...] = x + dot3(x, eye - dot6(matrix[...], x))
            return carry

        lax.fori_loop(0, jnp.where(wide, 4, 2), fine, 0)

    return wide


def flag(wide):
    return jnp.broadcast_to(jnp.where(wide, 1.0, 0.0), (8, 128)).astype(F32)


def refine_schur(schur, start):
    x = start * (8.0 / 7.0)
    r = unit_matrix(schur.shape[0]) - dot6(schur, x)
    r_two = dot3(r, r)
    x = x + dot6(x, r)
    r_four = dot3(r_two, r_two)
    x = x + dot3(x, r_two)
    return x + dot3(x, r_four)


def pack(matrix, out_ref):
    n = matrix.shape[0] // 2
    out_ref[:n] = matrix[:n, :n]
    out_ref[n : 2 * n] = 0.5 * (matrix[n:, :n] + matrix[:n, n:].T)
    out_ref[2 * n :] = matrix[n:, n:]


def unpack(packed):
    n = packed.shape[1]
    low = packed[n : 2 * n]
    top = jnp.concatenate([packed[:n], low.T], axis=1)
    return jnp.concatenate([top, jnp.concatenate([low, packed[2 * n :]], axis=1)], axis=0)


def leaf_kernel(coupling, y1_hbm, z_hbm, part_hbm, cap_ref, y_ref, part_ref, y1_ref, z_ref, sems):
    load_y1 = pltpu.make_async_copy(y1_hbm, y1_ref, sems.at[0])
    load_z = pltpu.make_async_copy(z_hbm, z_ref, sems.at[1])
    load_part = pltpu.make_async_copy(part_hbm, part_ref, sems.at[2])
    load_y1.start()
    load_z.start()
    load_part.start()
    load_y1.wait()
    y1 = y1_ref[...]
    y1t = y1.T
    cap_ref[...] = dot6(y1t, y1) + (2.0 * coupling) * unit_matrix(y1.shape[1])
    load_z.wait()
    y_ref[...] = dot3(y1t, z_ref[...])
    load_part.wait()


def invert_kernel(coupling, cap_ref, inv_ref, wide_ref, pair_ref):
    wide_ref[...] = flag(invert(cap_ref, 2.0 * coupling, inv_ref, pair_ref))


def cross_kernel(coupling, wide_ref, y1_ref, y2t_ref, cap_ref, inv_ref, bt_ref, ht_ref, sent_ref, dd_ref):
    y2t = y2t_ref[...]
    bt_ref[...] = dot6(y2t, y1_ref[...])
    ht_ref[...] = dot6(bt_ref[...], inv_ref[...])

    @pl.when(wide_ref[0, 0] > 0.5)
    def _():
        h = ht_ref[...]
        ht_ref[...] = h + dot3(bt_ref[...] - dot6(h, cap_ref[...]), inv_ref[...])

    sent_ref[...] = jnp.where(lax.axis_index("cols") % 2 == 0, inv_ref[...], ht_ref[...])
    dd_ref[...] = dot6(y2t, y2t, NT)


def project_kernel(coupling, y2t_ref, z_ref, y_ref, ht_ref, w_ref, v_ref):
    w_ref[...] = dot3(y2t_ref[...], z_ref[...])
    v_ref[...] = w_ref[...] - dot3(ht_ref[...], y_ref[...])


def pair_kernel(coupling, wide_ref, cap_ref, inv_ref, bt_ref, other_ref, dd_ref, schur_ref, t_ref, et_ref, p_ref):
    n = cap_ref.shape[0]
    bt = bt_ref[...]
    schur_ref[...] = cap_ref[...] - coupling * coupling * other_ref[:n]
    t_ref[...] = refine_schur(schur_ref[...], inv_ref[...])
    et_ref[...] = dot6(bt + coupling * other_ref[n:], t_ref[...])

    @pl.when(wide_ref[0, 0] > 0.5)
    def _():
        et = et_ref[...]
        et_ref[...] = et + dot3(bt_ref[...] + coupling * other_ref[n:] - dot6(et, schur_ref[...]), t_ref[...])

    pack(dd_ref[...] - dot6(et_ref[...], bt, NT), p_ref)


def rhs_kernel(coupling, wide_ref, schur_ref, t_ref, et_ref, y_ref, other_ref, other_y_ref, w_ref, other_v_ref, f_ref, ez_ref):
    n = t_ref.shape[0]
    g = y_ref[...] + coupling * dot3(other_ref[:n], other_y_ref[...])
    f_ref[...] = w_ref[...] + other_v_ref[...] - dot3(et_ref[...], g)
    ez_ref[...] = dot3(t_ref[...], g)

    @pl.when(wide_ref[0, 0] > 0.5)
    def _():
        e = ez_ref[...]
        ez_ref[...] = e + dot3(t_ref[...], g - dot6(schur_ref[...], e))


def apply_kernel(coupling, y1_ref, y2t_ref, z_ref, et_ref, ez_ref, z1_ref, high_ref, low_ref, updated_ref, ut_ref):
    y1 = y1_ref[...]
    part = updated_ref.shape[0]
    ut_ref[...] = y2t_ref[...] - dot3(et_ref[...], y1, NT)
    start = (lax.axis_index("cols") % 2) * (2 * part)
    updated_ref[...] = ut_ref[pl.ds(pl.multiple_of(start, part), part), :]
    high_ref[...], low_ref[...] = halves(ut_ref[...].T)
    z1_ref[...] = z_ref[...] - dot3(y1, ez_ref[...])


def quad_kernel(coupling, p_ref, other_p_ref, cap_ref, inv_ref, wide_ref, sent_ref, pair_ref):
    cap_ref[...] = unpack(p_ref[...] + other_p_ref[...]) + (2.0 * coupling) * unit_matrix(cap_ref.shape[0])
    wide_ref[...] = flag(invert(cap_ref, 2.0 * coupling, inv_ref, pair_ref))
    pack(inv_ref[...], sent_ref)


def last_kernel(coupling, wide_ref, cap_ref, inv_ref, far_ref, f_ref, f_far_ref, z1_ref, high_ref, low_ref, out_hbm, k_ref, out_ref, sems):
    far = unpack(far_ref[...])
    schur = cap_ref[...] - coupling * coupling * far
    t = refine_schur(schur, inv_ref[...])
    g = f_ref[...] + coupling * dot3(far, f_far_ref[...])
    k_ref[...] = dot3(t, g)

    @pl.when(wide_ref[0, 0] > 0.5)
    def _():
        k = k_ref[...]
        k_ref[...] = k + dot3(t, g - dot6(schur, k))

    k_high, k_low = halves(k_ref[...])
    pieces = sems.shape[0]
    rows = out_ref.shape[0] // pieces
    stores = []
    for i in range(pieces):
        block = slice(i * rows, (i + 1) * rows)
        high = high_ref[block]
        change = pass_dot(high, k_low, NN) + pass_dot(low_ref[block], k_high, NN)
        out_ref[block] = z1_ref[block] - pass_dot(high, k_high, NN) - change
        store = pltpu.make_async_copy(out_ref.at[block], out_hbm.at[block], sems.at[i])
        store.start()
        stores.append(store)
    for store in stores:
        store.wait()


def call(kernel, outs, *args, micros, scratch=(), space=pltpu.VMEM, out_space=pltpu.VMEM, grant=VMEM_BYTES):
    return pl.pallas_call(
        kernel,
        out_shape=[o if isinstance(o, jax.ShapeDtypeStruct) else jax.ShapeDtypeStruct(o, F32) for o in outs],
        in_specs=[pl.BlockSpec(memory_space=space)] * len(args),
        out_specs=[pl.BlockSpec(memory_space=out_space)] * len(outs),
        scratch_shapes=[pltpu.VMEM(x, F32) if isinstance(x, tuple) else x for x in scratch],
        compiler_params=pltpu.CompilerParams(vmem_limit_bytes=grant),
        cost_estimate=pl.CostEstimate(flops=int(micros * 1e9), bytes_accessed=int(micros * 3e6), transcendentals=0),
    )(*args)


def shards(level1_basis, level2_basis, probes):
    points, rank = level1_basis.shape
    part, columns = level2_basis.shape[0], probes.shape[1]
    coupling = points / 3.0
    n_cols = lax.axis_size("cols")
    square, tall, tile = (rank, rank), (rank, columns), (8, 128)
    packed = (3 * rank // 2, rank // 2)

    def run(kernel, outs, *args, **kw):
        return call(lambda *refs: kernel(coupling, *refs), outs, *args, **kw)

    def swap(value, bits, axis="rows"):
        return lax.ppermute(value, axis, [(i, i ^ bits) for i in range(lax.axis_size(axis))])

    def core_gather(value):
        groups = [[2 * i, 2 * i + 1] for i in range(n_cols // 2)]
        return lax.all_gather(value, "cols", axis=0, tiled=True, axis_index_groups=groups)

    cap, y, own_part = run(
        leaf_kernel,
        [square, tall, (part, points)],
        *(level1_basis, probes, level2_basis),
        micros=3,
        scratch=[(points, rank), (points, columns), pltpu.SemaphoreType.DMA((3,))],
        space=pltpu.HBM,
        grant=62 * 2**20,
    )
    far_part = swap(own_part, 2, "cols")
    other_y = swap(y, 1)
    inv, wide = run(invert_kernel, [square, tile], cap, micros=4, scratch=[(2 * rank, rank)])
    y2t = core_gather(jnp.concatenate([own_part, far_part], axis=0))
    bt, ht, sent, dd = run(cross_kernel, [square] * 4, wide, level1_basis, y2t, cap, inv, micros=4)
    other_half = swap(sent, 1)
    w, v = run(project_kernel, [tall] * 2, y2t, probes, y, ht, micros=3)
    other_v = swap(v, 1)
    other = core_gather(other_half)
    schur, t, et, p = run(pair_kernel, [square] * 3 + [packed], wide, cap, inv, bt, other, dd, micros=20)
    other_p = swap(p, 1)
    f, ez = run(rhs_kernel, [tall] * 2, wide, schur, t, et, y, other, other_y, w, other_v, micros=4)
    f_far = swap(f, 3)
    cap_two, inv_two, wide_two, sent_two = run(
        quad_kernel, [square, square, tile, packed], p, other_p, micros=6, scratch=[(2 * rank, rank)]
    )
    far_two = swap(sent_two, 3)
    half = jax.ShapeDtypeStruct((points, rank), BF16)
    z1, high, low, updated = run(
        apply_kernel,
        [(points, columns), half, half, (part, points)],
        *(level1_basis, y2t, probes, et, ez),
        micros=4,
        scratch=[(rank, points)],
    )
    (out,) = run(
        last_kernel,
        [(points, columns)],
        *(wide_two, cap_two, inv_two, far_two, f, f_far, z1, high, low),
        micros=7,
        scratch=[(rank, columns), (points, columns), pltpu.SemaphoreType.DMA((3,))],
        out_space=pltpu.HBM,
    )
    return out, updated


def solution(mesh):
    return jax.shard_map(
        shards,
        mesh=mesh,
        in_specs=(P("rows", None), P("cols", "rows"), P("rows", "cols")),
        out_specs=(P("rows", "cols"), P("cols", "rows")),
        check_vma=False,
    )
```

time: 74.9 us -> 70.9 us (0.947)
  waiting for transfers between devices: 20.8 us -> 15.8 us
  starting transfers between devices: 22 us -> 25.6 us
  local copies, waits for them, and re-layouts: 2.55 us -> 0.96 us
  Pallas kernels: 23.8 us -> 22.5 us
    ppermute x7, waiting for transfers between devices: 20.8 us -> 15.8 us  [swap(): lax.ppermute(value, axis, [(i, i ^ bits) for i in range(lax.axis_size(axi...]
    ppermute x7, starting transfers between devices: 22 us -> 25.6 us  [swap(): lax.ppermute(value, axis, [(i, i ^ bits) for i in range(lax.axis_size(axi...]
    unnamed x8 -> x10, local copies, waits for them, and re-layouts: 2.55 us -> 0.96 us
    pallas_call x9, Pallas kernels: 23.8 us -> 22.5 us  [call(): pl.pallas_call(kernel, out_shape=[o if isinstance(o, jax.ShapeDtypeStruct...]
  transfers between devices with their start and end apart: 7 -> 7, of which waited for: 4 -> 4; matrix products, arithmetic and copies ran while one was open for 0% -> 0% of each run, Pallas kernels for 25% -> 21%
where the time goes in v4:
time: 70.9 us; the launch traced here: 70.5 us
  starting transfers between devices  25.6 us (36%)
  Pallas kernels  22.5 us (32%)
  waiting for transfers between devices  15.8 us (22%)
  blocking collectives  4.67 us (7%)
  between operations  0.97 us (1%)
  local copies, waits for them, and re-layouts  0.96 us (1%)
    ppermute x7, starting transfers between devices, swap(): lax.ppermute(value, axis, [(i, i ^ bits) for i in range(lax.axis_size(axi...  25.6 us
    pallas_call x9, Pallas kernels, call(): pl.pallas_call(kernel, out_shape=[o if isinstance(o, jax.ShapeDtypeStruct...  22.5 us
    ppermute x7, waiting for transfers between devices, swap(): lax.ppermute(value, axis, [(i, i ^ bits) for i in range(lax.axis_size(axi...  15.8 us
    all_gather x2, blocking collectives, core_gather(): lax.all_gather(value, 'cols', axis=0, tiled=True, axis_index_groups=groups)  4.67 us
  transfers between devices with their start and end apart: 7, of which 4 were waited for; matrix products, arithmetic and copies ran while one was open for 0% of the time, Pallas kernels for 21%

profile of v4, /device:TPU:16, one launch (start us, length us, event | category | flops | bytes accessed | tf_op | source)
XLA Modules:
  0.0 70.5 jit_solution(4795167382319774581)
XLA Ops:
  0.6 3.7 %shard_map.50 = (f32[256,256]{1,0:T(8,128)}, f32[256,512]{1,0:T(8,128)}, f32[64,768]{1,0:T(8,128)}) custom-call(f32[768,256]{1,0:T(8,128)} %refs_0_.3, f32[768,512]{1,0:T(8,128)} %refs_2_.3, f32[64,768]{1,0:T(8,128)} %refs_2_.2), custom_call_target="tpu_custom_call" | custom-call | flops 3000000000 | bytes 9000000 | tf_op jit(solution)/shard_map/pallas_call | solution.py:230
  4.4 7.6 %collective-permute-start = (f32[64,768]{1,0:T(8,128)}, f32[64,768]{1,0:T(8,128)S(1)}, u32[]{:S(2)}, u32[]{:S(2)}) collective-permute-start(f32[64,768]{1,0:T(8,128)} %get-tuple-element.30), channel_id=1, source_target_pairs={{0,2},{1,3},{2,0},{3,1},{4,6},{5,7},{6,4},{7,5},{8,10},{9,11},{10,... | collective-permute-start | bytes 589832 | tf_op jit(solution)/shard_map/ppermute | solution.py:253
  12.0 1.9 %collective-permute-start.4 = (f32[256,512]{1,0:T(8,128)}, f32[256,512]{1,0:T(8,128)S(1)}, u32[]{:S(2)}, u32[]{:S(2)}) collective-permute-start(f32[256,512]{1,0:T(8,128)} %get-tuple-element.42.refs_2_.refs_4_), channel_id=1, source_target_pairs={{0,4},{4,0},{8,12},{12,8},{16,20},{20,16},{24,28},{28,24},{32,36},... | collective-permute-start | bytes 1572872 | tf_op jit(solution)/shard_map/ppermute | solution.py:253
  13.9 0.0 copy-start.3
  13.9 0.9 %copy-done.3 = f32[256,256]{1,0:T(8,128)S(1)} copy-done((f32[256,256]{1,0:T(8,128)S(1)}, f32[256,256]{1,0:T(8,128)}, u32[]{:S(2)}) %copy-start.3) | copy-done | bytes 262168
  14.9 3.0 %shard_map.51 = (f32[256,256]{1,0:T(8,128)S(1)}, f32[8,128]{1,0:T(8,128)S(1)}) custom-call(f32[256,256]{1,0:T(8,128)S(1)} %copy-done.3), custom_call_target="tpu_custom_call" | custom-call | flops 4000000000 | bytes 12000000 | tf_op jit(solution)/shard_map/pallas_call | solution.py:230
  17.9 0.0 copy-start.1
  17.9 0.0 collective-permute-done
  17.9 0.0 copy-done.4
  18.0 2.5 %all_gather.6.refs_2_.refs_0_.refs_1_ = f32[256,768]{1,0:T(8,128)S(1)} all-gather(f32[128,768]{1,0:T(8,128)S(1)} %pad_maximum_fusion), channel_id=1, replica_groups={{0,1},{2,3},{4,5},{6,7},{8,9},{10,11},{12,13},{14,15},{16,17},{18,19},{..., dimensions={0}, use_global_device_ids=true | all-gather | bytes 1179648 | tf_op jit(solution)/shard_map/all_gather | solution.py:257
  20.5 0.0 copy-done.1
  20.5 2.3 %shard_map.52 = (f32[256,256]{1,0:T(8,128)S(1)}, f32[256,256]{1,0:T(8,128)S(1)}, f32[256,256]{1,0:T(8,128)S(1)}, f32[256,256]{1,0:T(8,128)S(1)}) custom-call(f32[8,128]{1,0:T(8,128)S(1)} %get-tuple-element.28.refs_0_, f32[768,256]{1,0:T(8,128)S(1)} %copy-done.1, f32[256,768]{1,0:T(8,128)S(1)} %all_gather.6.refs_2_.refs_0_.refs_1_, f32[256,256]{1,0:T(8,128)S(1)} %copy-done.3, ...), custom_call_target="tpu_custom_call" | custom-call | flops 4000000000 | bytes 12000000 | tf_op jit(solution)/shard_map/pallas_call | solution.py:230
  22.8 3.9 %collective-permute-start.1 = (f32[256,256]{1,0:T(8,128)S(1)}, f32[256,256]{1,0:T(8,128)S(1)}, u32[]{:S(2)}, u32[]{:S(2)}) collective-permute-start(f32[256,256]{1,0:T(8,128)S(1)} %get-tuple-element.32), channel_id=1, source_target_pairs={{0,4},{4,0},{8,12},{12,8},{16,20},{20,16},{24,28},{28,24},{32,36},... | collective-permute-start | bytes 786440 | tf_op jit(solution)/shard_map/ppermute | solution.py:253
  26.7 0.0 copy-done
  26.7 0.0 copy-done.2
  26.7 1.0 %shard_map.55 = (f32[256,512]{1,0:T(8,128)S(1)}, f32[256,512]{1,0:T(8,128)S(1)}) custom-call(f32[256,768]{1,0:T(8,128)S(1)} %all_gather.6.refs_2_.refs_0_.refs_1_, f32[768,512]{1,0:T(8,128)S(1)} %copy-done, f32[256,512]{1,0:T(8,128)S(1)} %copy-done.2, f32[256,256]{1,0:T(8,128)S(1)} %get-tuple-element.43.refs_3_), custom_call_target="tpu_custom_call" | custom-call | flops 3000000000 | bytes 9000000 | tf_op jit(solution)/shard_map/pallas_call | solution.py:230
  27.8 1.9 %collective-permute-start.5 = (f32[256,512]{1,0:T(8,128)S(1)}, f32[256,512]{1,0:T(8,128)S(1)}, u32[]{:S(2)}, u32[]{:S(2)}) collective-permute-start(f32[256,512]{1,0:T(8,128)S(1)} %get-tuple-element.45), channel_id=1, source_target_pairs={{0,4},{4,0},{8,12},{12,8},{16,20},{20,16},{24,28},{28,24},{32,36},... | collective-permute-start | bytes 1572872 | tf_op jit(solution)/shard_map/ppermute | solution.py:253
  29.7 4.1 %collective-permute-done.1 = f32[256,256]{1,0:T(8,128)S(1)} collective-permute-done((f32[256,256]{1,0:T(8,128)S(1)}, f32[256,256]{1,0:T(8,128)S(1)}, u32[]{:S(2)}, u32[]{:S(2)}) %collective-permute-start.1) | collective-permute-done | bytes 262176 | tf_op jit(solution)/shard_map/ppermute | solution.py:253
  33.8 2.2 %all_gather.7.refs_4_.refs_5_ = f32[512,256]{1,0:T(8,128)S(1)} all-gather(f32[256,256]{1,0:T(8,128)S(1)} %collective-permute-done.1), channel_id=1, replica_groups={{0,1},{2,3},{4,5},{6,7},{8,9},{10,11},{12,13},{14,15},{16,17},{18,19},{..., dimensions={0}, use_global_device_ids=true | all-gather | bytes 786432 | tf_op jit(solution)/shard_map/all_gather | solution.py:257
  36.0 2.7 %shard_map.53 = (f32[256,256]{1,0:T(8,128)S(1)}, f32[256,256]{1,0:T(8,128)S(1)}, f32[256,256]{1,0:T(8,128)S(1)}, f32[384,128]{1,0:T(8,128)S(1)}) custom-call(f32[8,128]{1,0:T(8,128)S(1)} %get-tuple-element.28.refs_0_, f32[256,256]{1,0:T(8,128)S(1)} %copy-done.3, f32[256,256]{1,0:T(8,128)S(1)} %get-tuple-element.29.refs_4_.refs_2_, ...), custom_call_target="tpu_custom_call" | custom-call | flops 20000000000 | bytes 60000000 | tf_op jit(solution)/shard_map/pallas_call | solution.py:230
  38.6 4.0 %collective-permute-start.2 = (f32[384,128]{1,0:T(8,128)S(1)}, f32[384,128]{1,0:T(8,128)S(1)}, u32[]{:S(2)}, u32[]{:S(2)}) collective-permute-start(f32[384,128]{1,0:T(8,128)S(1)} %get-tuple-element.34.refs_0_), channel_id=1, source_target_pairs={{0,4},{4,0},{8,12},{12,8},{16,20},{20,16},{24,28},{28,24},{32,36},... | collective-permute-start | bytes 589832 | tf_op jit(solution)/shard_map/ppermute | solution.py:253
  42.6 0.0 collective-permute-done.4.refs_6_
  42.6 2.4 %collective-permute-done.5.refs_8_ = f32[256,512]{1,0:T(8,128)S(1)} collective-permute-done((f32[256,512]{1,0:T(8,128)S(1)}, f32[256,512]{1,0:T(8,128)S(1)}, u32[]{:S(2)}, u32[]{:S(2)}) %collective-permute-start.5) | collective-permute-done | bytes 524320 | tf_op jit(solution)/shard_map/ppermute | solution.py:253
  45.0 1.0 %shard_map.56 = (f32[256,512]{1,0:T(8,128)S(1)}, f32[256,512]{1,0:T(8,128)S(1)}) custom-call(f32[8,128]{1,0:T(8,128)S(1)} %get-tuple-element.28.refs_0_, f32[256,256]{1,0:T(8,128)S(1)} %get-tuple-element.39.refs_1_, f32[256,256]{1,0:T(8,128)S(1)} %get-tuple-element.40.refs_2_, f32[256,256]{1,0:T(8,128)S(1)} %get-tuple-element.41.refs_3_, ...), custom_call_target="tpu_custom_call" | custom-call | flops 4000000000 | bytes 12000000 | tf_op jit(solution)/shard_map/pallas_call | solution.py:230
  46.0 1.9 %collective-permute-start.6 = (f32[256,512]{1,0:T(8,128)S(1)}, f32[256,512]{1,0:T(8,128)S(1)}, u32[]{:S(2)}, u32[]{:S(2)}) collective-permute-start(f32[256,512]{1,0:T(8,128)S(1)} %get-tuple-element.46.refs_4_), channel_id=1, source_target_pairs={{0,12},{4,8},{8,4},{12,0},{16,28},{20,24},{24,20},{28,16},{32,44},... | collective-permute-start | bytes 1572872 | tf_op jit(solution)/shard_map/ppermute | solution.py:253
  48.0 0.8 %collective-permute-done.2.refs_1_ = f32[384,128]{1,0:T(8,128)S(1)} collective-permute-done((f32[384,128]{1,0:T(8,128)S(1)}, f32[384,128]{1,0:T(8,128)S(1)}, u32[]{:S(2)}, u32[]{:S(2)}) %collective-permute-start.2) | collective-permute-done | bytes 196640 | tf_op jit(solution)/shard_map/ppermute | solution.py:253
  48.8 3.4 %shard_map.54 = (f32[256,256]{1,0:T(8,128)S(1)}, f32[256,256]{1,0:T(8,128)S(1)}, f32[8,128]{1,0:T(8,128)S(1)}, f32[384,128]{1,0:T(8,128)S(1)}) custom-call(f32[384,128]{1,0:T(8,128)S(1)} %get-tuple-element.34.refs_0_, f32[384,128]{1,0:T(8,128)S(1)} %collective-permute-done.2.refs_1_), custom_call_target="tpu_custom_call" | custom-call | flops 6000000000 | bytes 18000000 | tf_op jit(solution)/shard_map/pallas_call | solution.py:230
  52.1 4.3 %collective-permute-start.3 = (f32[384,128]{1,0:T(8,128)S(1)}, f32[384,128]{1,0:T(8,128)S(1)}, u32[]{:S(2)}, u32[]{:S(2)}) collective-permute-start(f32[384,128]{1,0:T(8,128)S(1)} %get-tuple-element.38), channel_id=1, source_target_pairs={{0,12},{4,8},{8,4},{12,0},{16,28},{20,24},{24,20},{28,16},{32,44},... | collective-permute-start | bytes 589832 | tf_op jit(solution)/shard_map/ppermute | solution.py:253
  56.5 1.4 %shard_map.57 = (f32[768,512]{1,0:T(8,128)S(1)}, bf16[768,256]{1,0:T(8,128)(2,1)S(1)}, bf16[768,256]{1,0:T(8,128)(2,1)S(1)}, f32[64,768]{1,0:T(8,128)}) custom-call(f32[768,256]{1,0:T(8,128)S(1)} %copy-done.1, f32[256,768]{1,0:T(8,128)S(1)} %all_gather.6.refs_2_.refs_0_.refs_1_, f32[768,512]{1,0:T(8,128)S(1)} %copy-done, ...), custom_call_target="tpu_custom_call" | custom-call | flops 4000000000 | bytes 12000000 | tf_op jit(solution)/shard_map/pallas_call | solution.py:230
  57.9 8.4 %collective-permute-done.3.refs_3_ = f32[384,128]{1,0:T(8,128)S(1)} collective-permute-done((f32[384,128]{1,0:T(8,128)S(1)}, f32[384,128]{1,0:T(8,128)S(1)}, u32[]{:S(2)}, u32[]{:S(2)}) %collective-permute-start.3) | collective-permute-done | bytes 196640 | tf_op jit(solution)/shard_map/ppermute | solution.py:253
  66.3 0.0 collective-permute-done.6.refs_5_
  66.3 4.0 %shard_map.58 = f32[768,512]{1,0:T(8,128)} custom-call(f32[8,128]{1,0:T(8,128)S(1)} %get-tuple-element.35.refs_0_, f32[256,256]{1,0:T(8,128)S(1)} %get-tuple-element.36.refs_1_, f32[256,256]{1,0:T(8,128)S(1)} %get-tuple-element.37.refs_2_, f32[384,128]{1,0:T(8,128)S(1)} %collective-permute-done.3.refs_3_, f32[256,512]{1,0:T(8,128)S(1)} %get-tuple-element.46.refs_4_, ...), custom_call_target="tpu_custom_call" | custom-call | flops 7000000000 | bytes 21000000 | tf_op jit(solution)/shard_map/pallas_call | solution.py:230
  (4 shorter events, 0.0 us)
Async XLA Ops:
  4.4 13.5 %collective-permute-start = (f32[64,768]{1,0:T(8,128)}, f32[64,768]{1,0:T(8,128)S(1)}, u32[]{:S(2)}, u32[]{:S(2)}) collective-permute-start(f32[64,768]{1,0:T(8,128)} %get-tuple-element.30), channel_id=1, source_target_pairs={{0,2},{1,3},{2,0},{3,1},{4,6},{5,7},{6,4},{7,5},{8,10},{9,11},{10,... | collective-permute-start | bytes 589832 | tf_op jit(solution)/shard_map/ppermute | solution.py:253
  12.0 30.6 %collective-permute-start.4 = (f32[256,512]{1,0:T(8,128)}, f32[256,512]{1,0:T(8,128)S(1)}, u32[]{:S(2)}, u32[]{:S(2)}) collective-permute-start(f32[256,512]{1,0:T(8,128)} %get-tuple-element.42.refs_2_.refs_4_), channel_id=1, source_target_pairs={{0,4},{4,0},{8,12},{12,8},{16,20},{20,16},{24,28},{28,24},{32,36},... | collective-permute-start | bytes 1572872 | tf_op jit(solution)/shard_map/ppermute | solution.py:253
  13.9 1.0 %copy-start.3 = (f32[256,256]{1,0:T(8,128)S(1)}, f32[256,256]{1,0:T(8,128)}, u32[]{:S(2)}) copy-start(f32[256,256]{1,0:T(8,128)} %get-tuple-element.27.refs_0_.refs_3_.refs_1_) | copy-start | bytes 786436
  14.9 3.0 %copy-start.4 = (f32[64,768]{1,0:T(8,128)S(1)}, f32[64,768]{1,0:T(8,128)}, u32[]{:S(2)}) copy-start(f32[64,768]{1,0:T(8,128)} %get-tuple-element.30) | copy-start | bytes 589828
  17.9 2.6 %copy-start.1 = (f32[768,256]{1,0:T(8,128)S(1)}, f32[768,256]{1,0:T(8,128)}, u32[]{:S(2)}) copy-start(f32[768,256]{1,0:T(8,128)} %refs_0_.3) | copy-start | bytes 2359300
  20.5 6.3 %copy-start = (f32[768,512]{1,0:T(8,128)S(1)}, f32[768,512]{1,0:T(8,128)}, u32[]{:S(2)}) copy-start(f32[768,512]{1,0:T(8,128)} %refs_2_.3) | copy-start | bytes 4718596
  20.5 6.3 %copy-start.2 = (f32[256,512]{1,0:T(8,128)S(1)}, f32[256,512]{1,0:T(8,128)}, u32[]{:S(2)}) copy-start(f32[256,512]{1,0:T(8,128)} %get-tuple-element.42.refs_2_.refs_4_) | copy-start | bytes 1572868
  22.8 11.0 %collective-permute-start.1 = (f32[256,256]{1,0:T(8,128)S(1)}, f32[256,256]{1,0:T(8,128)S(1)}, u32[]{:S(2)}, u32[]{:S(2)}) collective-permute-start(f32[256,256]{1,0:T(8,128)S(1)} %get-tuple-element.32), channel_id=1, source_target_pairs={{0,4},{4,0},{8,12},{12,8},{16,20},{20,16},{24,28},{28,24},{32,36},... | collective-permute-start | bytes 786440 | tf_op jit(solution)/shard_map/ppermute | solution.py:253
  27.8 17.3 %collective-permute-start.5 = (f32[256,512]{1,0:T(8,128)S(1)}, f32[256,512]{1,0:T(8,128)S(1)}, u32[]{:S(2)}, u32[]{:S(2)}) collective-permute-start(f32[256,512]{1,0:T(8,128)S(1)} %get-tuple-element.45), channel_id=1, source_target_pairs={{0,4},{4,0},{8,12},{12,8},{16,20},{20,16},{24,28},{28,24},{32,36},... | collective-permute-start | bytes 1572872 | tf_op jit(solution)/shard_map/ppermute | solution.py:253
  38.6 10.1 %collective-permute-start.2 = (f32[384,128]{1,0:T(8,128)S(1)}, f32[384,128]{1,0:T(8,128)S(1)}, u32[]{:S(2)}, u32[]{:S(2)}) collective-permute-start(f32[384,128]{1,0:T(8,128)S(1)} %get-tuple-element.34.refs_0_), channel_id=1, source_target_pairs={{0,4},{4,0},{8,12},{12,8},{16,20},{20,16},{24,28},{28,24},{32,36},... | collective-permute-start | bytes 589832 | tf_op jit(solution)/shard_map/ppermute | solution.py:253
  46.0 20.3 %collective-permute-start.6 = (f32[256,512]{1,0:T(8,128)S(1)}, f32[256,512]{1,0:T(8,128)S(1)}, u32[]{:S(2)}, u32[]{:S(2)}) collective-permute-start(f32[256,512]{1,0:T(8,128)S(1)} %get-tuple-element.46.refs_4_), channel_id=1, source_target_pairs={{0,12},{4,8},{8,4},{12,0},{16,28},{20,24},{24,20},{28,16},{32,44},... | collective-permute-start | bytes 1572872 | tf_op jit(solution)/shard_map/ppermute | solution.py:253
  52.1 14.2 %collective-permute-start.3 = (f32[384,128]{1,0:T(8,128)S(1)}, f32[384,128]{1,0:T(8,128)S(1)}, u32[]{:S(2)}, u32[]{:S(2)}) collective-permute-start(f32[384,128]{1,0:T(8,128)S(1)} %get-tuple-element.38), channel_id=1, source_target_pairs={{0,12},{4,8},{8,4},{12,0},{16,28},{20,24},{24,20},{28,16},{32,44},... | collective-permute-start | bytes 589832 | tf_op jit(solution)/shard_map/ppermute | solution.py:253

commit v5 on v4

--- a/solution.py
+++ b/solution.py
@@ -1,3 +1,5 @@
+import functools
+
 import jax
 import jax.numpy as jnp
 from jax import lax
@@ -96,7 +98,7 @@
     x = start * (8.0 / 7.0)
     r = unit_matrix(schur.shape[0]) - dot6(schur, x)
     r_two = dot3(r, r)
-    x = x + dot6(x, r)
+    x = x + dot3(x, r)
     r_four = dot3(r_two, r_two)
     x = x + dot3(x, r_two)
     return x + dot3(x, r_four)
@@ -150,9 +152,12 @@
     dd_ref[...] = dot6(y2t, y2t, NT)
 
 
-def project_kernel(coupling, y2t_ref, z_ref, y_ref, ht_ref, w_ref, v_ref):
+def project_kernel(coupling, y2t_ref, z_ref, y_ref, ht_ref, w_ref, left_ref, right_ref):
     w_ref[...] = dot3(y2t_ref[...], z_ref[...])
-    v_ref[...] = w_ref[...] - dot3(ht_ref[...], y_ref[...])
+    v = w_ref[...] - dot3(ht_ref[...], y_ref[...])
+    half = left_ref.shape[1]
+    left_ref[...] = v[:, :half]
+    right_ref[...] = v[:, half:]
 
 
 def pair_kernel(coupling, wide_ref, cap_ref, inv_ref, bt_ref, other_ref, dd_ref, schur_ref, t_ref, et_ref, p_ref):
@@ -170,10 +175,11 @@
     pack(dd_ref[...] - dot6(et_ref[...], bt, NT), p_ref)
 
 
-def rhs_kernel(coupling, wide_ref, schur_ref, t_ref, et_ref, y_ref, other_ref, other_y_ref, w_ref, other_v_ref, f_ref, ez_ref):
+def rhs_kernel(coupling, first, wide_ref, schur_ref, t_ref, et_ref, y_ref, other_ref, other_y_ref, w_ref, other_v_ref, f_ref, ez_ref):
     n = t_ref.shape[0]
-    g = y_ref[...] + coupling * dot3(other_ref[:n], other_y_ref[...])
-    f_ref[...] = w_ref[...] + other_v_ref[...] - dot3(et_ref[...], g)
+    columns = slice(first, first + f_ref.shape[1])
+    g = y_ref[:, columns] + coupling * dot3(other_ref[:n], other_y_ref[:, columns])
+    f_ref[...] = w_ref[:, columns] + other_v_ref[...] - dot3(et_ref[...], g)
     ez_ref[...] = dot3(t_ref[...], g)
 
     @pl.when(wide_ref[0, 0] > 0.5)
@@ -182,14 +188,16 @@
         ez_ref[...] = e + dot3(t_ref[...], g - dot6(schur_ref[...], e))
 
 
-def apply_kernel(coupling, y1_ref, y2t_ref, z_ref, et_ref, ez_ref, z1_ref, high_ref, low_ref, updated_ref, ut_ref):
+def apply_kernel(coupling, y1_ref, y2t_ref, z_ref, et_ref, left_ref, right_ref, z1_ref, high_ref, low_ref, updated_ref, ut_ref):
     y1 = y1_ref[...]
     part = updated_ref.shape[0]
     ut_ref[...] = y2t_ref[...] - dot3(et_ref[...], y1, NT)
     start = (lax.axis_index("cols") % 2) * (2 * part)
     updated_ref[...] = ut_ref[pl.ds(pl.multiple_of(start, part), part), :]
     high_ref[...], low_ref[...] = halves(ut_ref[...].T)
-    z1_ref[...] = z_ref[...] - dot3(y1, ez_ref[...])
+    half = left_ref.shape[1]
+    z1_ref[:, :half] = z_ref[:, :half] - dot3(y1, left_ref[...])
+    z1_ref[:, half:] = z_ref[:, half:] - dot3(y1, right_ref[...])
 
 
 def quad_kernel(coupling, p_ref, other_p_ref, cap_ref, inv_ref, wide_ref, sent_ref, pair_ref):
@@ -198,17 +206,22 @@
     pack(inv_ref[...], sent_ref)
 
 
-def last_kernel(coupling, wide_ref, cap_ref, inv_ref, far_ref, f_ref, f_far_ref, z1_ref, high_ref, low_ref, out_hbm, k_ref, out_ref, sems):
+def last_kernel(coupling, wide_ref, cap_ref, inv_ref, far_ref, *refs):
+    left_ref, right_ref, left_far_ref, right_far_ref, z1_ref, high_ref, low_ref, out_hbm, k_ref, out_ref, sems = refs
     far = unpack(far_ref[...])
     schur = cap_ref[...] - coupling * coupling * far
     t = refine_schur(schur, inv_ref[...])
-    g = f_ref[...] + coupling * dot3(far, f_far_ref[...])
-    k_ref[...] = dot3(t, g)
+    g_left = left_ref[...] + coupling * dot3(far, left_far_ref[...])
+    g_right = right_ref[...] + coupling * dot3(far, right_far_ref[...])
+    half = left_ref.shape[1]
+    k_ref[:, :half] = dot3(t, g_left)
+    k_ref[:, half:] = dot3(t, g_right)
 
     @pl.when(wide_ref[0, 0] > 0.5)
     def _():
-        k = k_ref[...]
-        k_ref[...] = k + dot3(t, g - dot6(schur, k))
+        for g, columns in ((g_left, slice(None, half)), (g_right, slice(half, None))):
+            k = k_ref[:, columns]
+            k_ref[:, columns] = k + dot3(t, g - dot6(schur, k))
 
     k_high, k_low = halves(k_ref[...])
     pieces = sems.shape[0]
@@ -271,29 +284,38 @@
     y2t = core_gather(jnp.concatenate([own_part, far_part], axis=0))
     bt, ht, sent, dd = run(cross_kernel, [square] * 4, wide, level1_basis, y2t, cap, inv, micros=4)
     other_half = swap(sent, 1)
-    w, v = run(project_kernel, [tall] * 2, y2t, probes, y, ht, micros=3)
-    other_v = swap(v, 1)
+    w, v_left, v_right = run(project_kernel, [tall, (rank, columns // 2), (rank, columns // 2)], y2t, probes, y, ht, micros=3)
+    other_v_left = swap(v_left, 1)
+    other_v_right = swap(v_right, 1)
     other = core_gather(other_half)
     schur, t, et, p = run(pair_kernel, [square] * 3 + [packed], wide, cap, inv, bt, other, dd, micros=20)
     other_p = swap(p, 1)
-    f, ez = run(rhs_kernel, [tall] * 2, wide, schur, t, et, y, other, other_y, w, other_v, micros=4)
-    f_far = swap(f, 3)
+    half = columns // 2
+
+    def rhs(first, other_v):
+        kernel = functools.partial(rhs_kernel, coupling, first)
+        return call(kernel, [(rank, half)] * 2, wide, schur, t, et, y, other, other_y, w, other_v, micros=3)
+
+    f_left, ez_left = rhs(0, other_v_left)
+    far_left = swap(f_left, 3)
+    f_right, ez_right = rhs(half, other_v_right)
+    far_right = swap(f_right, 3)
     cap_two, inv_two, wide_two, sent_two = run(
         quad_kernel, [square, square, tile, packed], p, other_p, micros=6, scratch=[(2 * rank, rank)]
     )
     far_two = swap(sent_two, 3)
-    half = jax.ShapeDtypeStruct((points, rank), BF16)
+    bits = jax.ShapeDtypeStruct((points, rank), BF16)
     z1, high, low, updated = run(
         apply_kernel,
-        [(points, columns), half, half, (part, points)],
-        *(level1_basis, y2t, probes, et, ez),
+        [(points, columns), bits, bits, (part, points)],
+        *(level1_basis, y2t, probes, et, ez_left, ez_right),
         micros=4,
         scratch=[(rank, points)],
     )
     (out,) = run(
         last_kernel,
         [(points, columns)],
-        *(wide_two, cap_two, inv_two, far_two, f, f_far, z1, high, low),
+        *(wide_two, cap_two, inv_two, far_two, f_left, f_right, far_left, far_right, z1, high, low),
         micros=7,
         scratch=[(rank, columns), (points, columns), pltpu.SemaphoreType.DMA((3,))],
         out_space=pltpu.HBM,

time: 70.9 us -> 68.4 us (0.965)
  waiting for transfers between devices: 15.8 us -> 6.76 us
  starting transfers between devices: 25.6 us -> 32.3 us
    ppermute x7 -> x9, waiting for transfers between devices: 15.8 us -> 6.76 us  [swap(): lax.ppermute(value, axis, [(i, i ^ bits) for i in range(lax.axis_size(axi...]
    ppermute x7 -> x9, starting transfers between devices: 25.6 us -> 32.3 us  [swap(): lax.ppermute(value, axis, [(i, i ^ bits) for i in range(lax.axis_size(axi...]
    pallas_call x9 -> x10, Pallas kernels: 22.5 us -> 22.3 us  [call(): pl.pallas_call(kernel, out_shape=[o if isinstance(o, jax.ShapeDtypeStruct...]
  transfers between devices with their start and end apart: 7 -> 9, of which waited for: 4 -> 3; matrix products, arithmetic and copies ran while one was open for 0% -> 0% of each run, Pallas kernels for 21% -> 22%
where the time goes in v5:
time: 68.4 us; the launch traced here: 68 us
  starting transfers between devices  32.3 us (47%)
  Pallas kernels  22.3 us (33%)
  waiting for transfers between devices  6.76 us (10%)
  blocking collectives  4.67 us (7%)
  between operations  1.01 us (1%)
  local copies, waits for them, and re-layouts  0.96 us (1%)
    ppermute x9, starting transfers between devices, swap(): lax.ppermute(value, axis, [(i, i ^ bits) for i in range(lax.axis_size(axi...  32.3 us
    pallas_call x10, Pallas kernels, call(): pl.pallas_call(kernel, out_shape=[o if isinstance(o, jax.ShapeDtypeStruct...  22.3 us
    ppermute x9, waiting for transfers between devices, swap(): lax.ppermute(value, axis, [(i, i ^ bits) for i in range(lax.axis_size(axi...  6.76 us
    all_gather x2, blocking collectives, core_gather(): lax.all_gather(value, 'cols', axis=0, tiled=True, axis_index_groups=groups)  4.67 us
  transfers between devices with their start and end apart: 9, of which 3 were waited for; matrix products, arithmetic and copies ran while one was open for 0% of the time, Pallas kernels for 22%

profile of v5, /device:TPU:16, one launch (start us, length us, event | category | flops | bytes accessed | tf_op | source)
XLA Modules:
  0.0 68.0 jit_solution(9044588455692683970)
XLA Ops:
  0.6 3.7 %shard_map.50 = (f32[256,256]{1,0:T(8,128)}, f32[256,512]{1,0:T(8,128)}, f32[64,768]{1,0:T(8,128)}) custom-call(f32[768,256]{1,0:T(8,128)} %refs_0_.3, f32[768,512]{1,0:T(8,128)} %refs_2_.3, f32[64,768]{1,0:T(8,128)} %refs_2_.2), custom_call_target="tpu_custom_call" | custom-call | flops 3000000000 | bytes 9000000 | tf_op jit(solution)/shard_map/pallas_call | solution.py:243
  4.4 7.6 %collective-permute-start = (f32[64,768]{1,0:T(8,128)}, f32[64,768]{1,0:T(8,128)S(1)}, u32[]{:S(2)}, u32[]{:S(2)}) collective-permute-start(f32[64,768]{1,0:T(8,128)} %get-tuple-element.33), channel_id=1, source_target_pairs={{0,2},{1,3},{2,0},{3,1},{4,6},{5,7},{6,4},{7,5},{8,10},{9,11},{10,... | collective-permute-start | bytes 589832 | tf_op jit(solution)/shard_map/ppermute | solution.py:266
  12.0 1.9 %collective-permute-start.4 = (f32[256,512]{1,0:T(8,128)}, f32[256,512]{1,0:T(8,128)S(1)}, u32[]{:S(2)}, u32[]{:S(2)}) collective-permute-start(f32[256,512]{1,0:T(8,128)} %get-tuple-element.45.refs_2_.y_ref), channel_id=1, source_target_pairs={{0,4},{4,0},{8,12},{12,8},{16,20},{20,16},{24,28},{28,24},{32,36},... | collective-permute-start | bytes 1572872 | tf_op jit(solution)/shard_map/ppermute | solution.py:266
  13.9 0.9 %copy-done.3 = f32[256,256]{1,0:T(8,128)S(1)} copy-done((f32[256,256]{1,0:T(8,128)S(1)}, f32[256,256]{1,0:T(8,128)}, u32[]{:S(2)}) %copy-start.3) | copy-done | bytes 262168
  14.9 3.0 %shard_map.51 = (f32[256,256]{1,0:T(8,128)S(1)}, f32[8,128]{1,0:T(8,128)S(1)}) custom-call(f32[256,256]{1,0:T(8,128)S(1)} %copy-done.3), custom_call_target="tpu_custom_call" | custom-call | flops 4000000000 | bytes 12000000 | tf_op jit(solution)/shard_map/pallas_call | solution.py:243
  17.9 0.0 copy-start.1
  17.9 0.0 collective-permute-done
  18.0 2.5 %all_gather.6.refs_2_.refs_0_.refs_1_ = f32[256,768]{1,0:T(8,128)S(1)} all-gather(f32[128,768]{1,0:T(8,128)S(1)} %pad_maximum_fusion), channel_id=1, replica_groups={{0,1},{2,3},{4,5},{6,7},{8,9},{10,11},{12,13},{14,15},{16,17},{18,19},{..., dimensions={0}, use_global_device_ids=true | all-gather | bytes 1179648 | tf_op jit(solution)/shard_map/all_gather | solution.py:270
  20.5 2.3 %shard_map.52 = (f32[256,256]{1,0:T(8,128)S(1)}, f32[256,256]{1,0:T(8,128)S(1)}, f32[256,256]{1,0:T(8,128)S(1)}, f32[256,256]{1,0:T(8,128)S(1)}) custom-call(f32[8,128]{1,0:T(8,128)S(1)} %get-tuple-element.31.refs_0_.wide_ref, f32[768,256]{1,0:T(8,128)S(1)} %copy-done.1, f32[256,768]{1,0:T(8,128)S(1)} %all_gather.6.refs_2_.refs_0_.refs_1_, ...), custom_call_target="tpu_custom_call" | custom-call | flops 4000000000 | bytes 12000000 | tf_op jit(solution)/shard_map/pallas_call | solution.py:243
  22.8 3.9 %collective-permute-start.1 = (f32[256,256]{1,0:T(8,128)S(1)}, f32[256,256]{1,0:T(8,128)S(1)}, u32[]{:S(2)}, u32[]{:S(2)}) collective-permute-start(f32[256,256]{1,0:T(8,128)S(1)} %get-tuple-element.35), channel_id=1, source_target_pairs={{0,4},{4,0},{8,12},{12,8},{16,20},{20,16},{24,28},{28,24},{32,36},... | collective-permute-start | bytes 786440 | tf_op jit(solution)/shard_map/ppermute | solution.py:266
  26.7 1.0 %shard_map.55 = (f32[256,512]{1,0:T(8,128)S(1)}, f32[256,256]{1,0:T(8,128)S(1)}, f32[256,256]{1,0:T(8,128)S(1)}) custom-call(f32[256,768]{1,0:T(8,128)S(1)} %all_gather.6.refs_2_.refs_0_.refs_1_, f32[768,512]{1,0:T(8,128)S(1)} %copy-done, f32[256,512]{1,0:T(8,128)S(1)} %copy-done.2, f32[256,256]{1,0:T(8,128)S(1)} %get-tuple-element.46.refs_3_), custom_call_target="tpu_custom_call" | custom-call | flops 3000000000 | bytes 9000000 | tf_op jit(solution)/shard_map/pallas_call | solution.py:243
  27.8 1.9 %collective-permute-start.6 = (f32[256,256]{1,0:T(8,128)S(1)}, f32[256,256]{1,0:T(8,128)S(1)}, u32[]{:S(2)}, u32[]{:S(2)}) collective-permute-start(f32[256,256]{1,0:T(8,128)S(1)} %get-tuple-element.50), channel_id=1, source_target_pairs={{0,4},{4,0},{8,12},{12,8},{16,20},{20,16},{24,28},{28,24},{32,36},... | collective-permute-start | bytes 786440 | tf_op jit(solution)/shard_map/ppermute | solution.py:266
  29.7 3.9 %collective-permute-start.5 = (f32[256,256]{1,0:T(8,128)S(1)}, f32[256,256]{1,0:T(8,128)S(1)}, u32[]{:S(2)}, u32[]{:S(2)}) collective-permute-start(f32[256,256]{1,0:T(8,128)S(1)} %get-tuple-element.48), channel_id=1, source_target_pairs={{0,4},{4,0},{8,12},{12,8},{16,20},{20,16},{24,28},{28,24},{32,36},... | collective-permute-start | bytes 786440 | tf_op jit(solution)/shard_map/ppermute | solution.py:266
  33.6 0.2 collective-permute-done.1
  33.8 2.2 %all_gather.7.refs_4_.other_ref = f32[512,256]{1,0:T(8,128)S(1)} all-gather(f32[256,256]{1,0:T(8,128)S(1)} %collective-permute-done.1), channel_id=1, replica_groups={{0,1},{2,3},{4,5},{6,7},{8,9},{10,11},{12,13},{14,15},{16,17},{18,19},{..., dimensions={0}, use_global_device_ids=true | all-gather | bytes 786432 | tf_op jit(solution)/shard_map/all_gather | solution.py:270
  36.0 2.5 %shard_map.53 = (f32[256,256]{1,0:T(8,128)S(1)}, f32[256,256]{1,0:T(8,128)S(1)}, f32[256,256]{1,0:T(8,128)S(1)}, f32[384,128]{1,0:T(8,128)S(1)}) custom-call(f32[8,128]{1,0:T(8,128)S(1)} %get-tuple-element.31.refs_0_.wide_ref, f32[256,256]{1,0:T(8,128)S(1)} %copy-done.3, f32[256,256]{1,0:T(8,128)S(1)} %get-tuple-element.32.refs_4_.refs_2_, ...), custom_call_target="tpu_custom_call" | custom-call | flops 20000000000 | bytes 60000000 | tf_op jit(solution)/shard_map/pallas_call | solution.py:243
  38.5 4.0 %collective-permute-start.2 = (f32[384,128]{1,0:T(8,128)S(1)}, f32[384,128]{1,0:T(8,128)S(1)}, u32[]{:S(2)}, u32[]{:S(2)}) collective-permute-start(f32[384,128]{1,0:T(8,128)S(1)} %get-tuple-element.37.refs_0_), channel_id=1, source_target_pairs={{0,4},{4,0},{8,12},{12,8},{16,20},{20,16},{24,28},{28,24},{32,36},... | collective-permute-start | bytes 589832 | tf_op jit(solution)/shard_map/ppermute | solution.py:266
  42.5 0.0 collective-permute-done.6.other_v_ref
  42.5 0.0 collective-permute-done.4.other_y_ref
  42.5 0.6 shard_map.57
  43.1 1.9 %collective-permute-start.8 = (f32[256,256]{1,0:T(8,128)S(1)}, f32[256,256]{1,0:T(8,128)S(1)}, u32[]{:S(2)}, u32[]{:S(2)}) collective-permute-start(f32[256,256]{1,0:T(8,128)S(1)} %get-tuple-element.51.refs_5_), channel_id=1, source_target_pairs={{0,12},{4,8},{8,4},{12,0},{16,28},{20,24},{24,20},{28,16},{32,44},... | collective-permute-start | bytes 786440 | tf_op jit(solution)/shard_map/ppermute | solution.py:266
  45.1 0.0 collective-permute-done.5.other_v_ref
  45.1 0.8 %shard_map.56 = (f32[256,256]{1,0:T(8,128)S(1)}, f32[256,256]{1,0:T(8,128)S(1)}) custom-call(f32[8,128]{1,0:T(8,128)S(1)} %get-tuple-element.31.refs_0_.wide_ref, f32[256,256]{1,0:T(8,128)S(1)} %get-tuple-element.42.schur_ref, f32[256,256]{1,0:T(8,128)S(1)} %get-tuple-element.43.t_ref, f32[256,256]{1,0:T(8,128)S(1)} %get-tuple-element.44.et_ref.refs_3_, ...), custom_call_target="tpu_custom_call" | custom-call | flops 3000000000 | bytes 9000000 | tf_op jit(solution)/shard_map/pallas_call | solution.py:243
  45.9 5.1 %collective-permute-start.7 = (f32[256,256]{1,0:T(8,128)S(1)}, f32[256,256]{1,0:T(8,128)S(1)}, u32[]{:S(2)}, u32[]{:S(2)}) collective-permute-start(f32[256,256]{1,0:T(8,128)S(1)} %get-tuple-element.49.refs_4_), channel_id=1, source_target_pairs={{0,12},{4,8},{8,4},{12,0},{16,28},{20,24},{24,20},{28,16},{32,44},... | collective-permute-start | bytes 786440 | tf_op jit(solution)/shard_map/ppermute | solution.py:266
  51.1 0.0 collective-permute-done.2.refs_1_
  51.1 3.2 %shard_map.54 = (f32[256,256]{1,0:T(8,128)S(1)}, f32[256,256]{1,0:T(8,128)S(1)}, f32[8,128]{1,0:T(8,128)S(1)}, f32[384,128]{1,0:T(8,128)S(1)}) custom-call(f32[384,128]{1,0:T(8,128)S(1)} %get-tuple-element.37.refs_0_, f32[384,128]{1,0:T(8,128)S(1)} %collective-permute-done.2.refs_1_), custom_call_target="tpu_custom_call" | custom-call | flops 6000000000 | bytes 18000000 | tf_op jit(solution)/shard_map/pallas_call | solution.py:243
  54.3 1.9 %collective-permute-start.3 = (f32[384,128]{1,0:T(8,128)S(1)}, f32[384,128]{1,0:T(8,128)S(1)}, u32[]{:S(2)}, u32[]{:S(2)}) collective-permute-start(f32[384,128]{1,0:T(8,128)S(1)} %get-tuple-element.41), channel_id=1, source_target_pairs={{0,12},{4,8},{8,4},{12,0},{16,28},{20,24},{24,20},{28,16},{32,44},... | collective-permute-start | bytes 589832 | tf_op jit(solution)/shard_map/ppermute | solution.py:266
  56.2 1.4 %shard_map.58 = (f32[768,512]{1,0:T(8,128)S(1)}, bf16[768,256]{1,0:T(8,128)(2,1)S(1)}, bf16[768,256]{1,0:T(8,128)(2,1)S(1)}, f32[64,768]{1,0:T(8,128)}) custom-call(f32[768,256]{1,0:T(8,128)S(1)} %copy-done.1, f32[256,768]{1,0:T(8,128)S(1)} %all_gather.6.refs_2_.refs_0_.refs_1_, f32[768,512]{1,0:T(8,128)S(1)} %copy-done, ...), custom_call_target="tpu_custom_call" | custom-call | flops 4000000000 | bytes 12000000 | tf_op jit(solution)/shard_map/pallas_call | solution.py:243
  57.6 0.0 collective-permute-done.8.refs_7_
  57.6 3.0 %collective-permute-done.7.refs_6_ = f32[256,256]{1,0:T(8,128)S(1)} collective-permute-done((f32[256,256]{1,0:T(8,128)S(1)}, f32[256,256]{1,0:T(8,128)S(1)}, u32[]{:S(2)}, u32[]{:S(2)}) %collective-permute-start.7) | collective-permute-done | bytes 262176 | tf_op jit(solution)/shard_map/ppermute | solution.py:266
  60.6 3.6 %collective-permute-done.3.refs_3_ = f32[384,128]{1,0:T(8,128)S(1)} collective-permute-done((f32[384,128]{1,0:T(8,128)S(1)}, f32[384,128]{1,0:T(8,128)S(1)}, u32[]{:S(2)}, u32[]{:S(2)}) %collective-permute-start.3) | collective-permute-done | bytes 196640 | tf_op jit(solution)/shard_map/ppermute | solution.py:266
  64.1 3.7 %shard_map.59 = f32[768,512]{1,0:T(8,128)} custom-call(f32[8,128]{1,0:T(8,128)S(1)} %get-tuple-element.38.refs_0_, f32[256,256]{1,0:T(8,128)S(1)} %get-tuple-element.39.refs_1_, f32[256,256]{1,0:T(8,128)S(1)} %get-tuple-element.40.refs_2_, f32[384,128]{1,0:T(8,128)S(1)} %collective-permute-done.3.refs_3_, f32[256,256]{1,0:T(8,128)S(1)} %get-tuple-element.49.refs_4_, ...), custom_call_target="tpu_custom_call" | custom-call | flops 7000000000 | bytes 21000000 | tf_op jit(solution)/shard_map/pallas_call | solution.py:243
  (9 shorter events, 0.0 us)
Async XLA Ops:
  4.4 13.5 %collective-permute-start = (f32[64,768]{1,0:T(8,128)}, f32[64,768]{1,0:T(8,128)S(1)}, u32[]{:S(2)}, u32[]{:S(2)}) collective-permute-start(f32[64,768]{1,0:T(8,128)} %get-tuple-element.33), channel_id=1, source_target_pairs={{0,2},{1,3},{2,0},{3,1},{4,6},{5,7},{6,4},{7,5},{8,10},{9,11},{10,... | collective-permute-start | bytes 589832 | tf_op jit(solution)/shard_map/ppermute | solution.py:266
  12.0 30.5 %collective-permute-start.4 = (f32[256,512]{1,0:T(8,128)}, f32[256,512]{1,0:T(8,128)S(1)}, u32[]{:S(2)}, u32[]{:S(2)}) collective-permute-start(f32[256,512]{1,0:T(8,128)} %get-tuple-element.45.refs_2_.y_ref), channel_id=1, source_target_pairs={{0,4},{4,0},{8,12},{12,8},{16,20},{20,16},{24,28},{28,24},{32,36},... | collective-permute-start | bytes 1572872 | tf_op jit(solution)/shard_map/ppermute | solution.py:266
  13.9 1.0 %copy-start.3 = (f32[256,256]{1,0:T(8,128)S(1)}, f32[256,256]{1,0:T(8,128)}, u32[]{:S(2)}) copy-start(f32[256,256]{1,0:T(8,128)} %get-tuple-element.30.refs_0_.refs_3_.refs_1_) | copy-start | bytes 786436
  14.9 3.0 %copy-start.4 = (f32[64,768]{1,0:T(8,128)S(1)}, f32[64,768]{1,0:T(8,128)}, u32[]{:S(2)}) copy-start(f32[64,768]{1,0:T(8,128)} %get-tuple-element.33) | copy-start | bytes 589828
  17.9 2.6 %copy-start.1 = (f32[768,256]{1,0:T(8,128)S(1)}, f32[768,256]{1,0:T(8,128)}, u32[]{:S(2)}) copy-start(f32[768,256]{1,0:T(8,128)} %refs_0_.3) | copy-start | bytes 2359300
  20.5 6.3 %copy-start = (f32[768,512]{1,0:T(8,128)S(1)}, f32[768,512]{1,0:T(8,128)}, u32[]{:S(2)}) copy-start(f32[768,512]{1,0:T(8,128)} %refs_2_.3) | copy-start | bytes 4718596
  20.5 6.3 %copy-start.2 = (f32[256,512]{1,0:T(8,128)S(1)}, f32[256,512]{1,0:T(8,128)}, u32[]{:S(2)}) copy-start(f32[256,512]{1,0:T(8,128)} %get-tuple-element.45.refs_2_.y_ref) | copy-start | bytes 1572868
  22.8 11.0 %collective-permute-start.1 = (f32[256,256]{1,0:T(8,128)S(1)}, f32[256,256]{1,0:T(8,128)S(1)}, u32[]{:S(2)}, u32[]{:S(2)}) collective-permute-start(f32[256,256]{1,0:T(8,128)S(1)} %get-tuple-element.35), channel_id=1, source_target_pairs={{0,4},{4,0},{8,12},{12,8},{16,20},{20,16},{24,28},{28,24},{32,36},... | collective-permute-start | bytes 786440 | tf_op jit(solution)/shard_map/ppermute | solution.py:266
  27.8 14.7 %collective-permute-start.6 = (f32[256,256]{1,0:T(8,128)S(1)}, f32[256,256]{1,0:T(8,128)S(1)}, u32[]{:S(2)}, u32[]{:S(2)}) collective-permute-start(f32[256,256]{1,0:T(8,128)S(1)} %get-tuple-element.50), channel_id=1, source_target_pairs={{0,4},{4,0},{8,12},{12,8},{16,20},{20,16},{24,28},{28,24},{32,36},... | collective-permute-start | bytes 786440 | tf_op jit(solution)/shard_map/ppermute | solution.py:266
  29.7 15.4 %collective-permute-start.5 = (f32[256,256]{1,0:T(8,128)S(1)}, f32[256,256]{1,0:T(8,128)S(1)}, u32[]{:S(2)}, u32[]{:S(2)}) collective-permute-start(f32[256,256]{1,0:T(8,128)S(1)} %get-tuple-element.48), channel_id=1, source_target_pairs={{0,4},{4,0},{8,12},{12,8},{16,20},{20,16},{24,28},{28,24},{32,36},... | collective-permute-start | bytes 786440 | tf_op jit(solution)/shard_map/ppermute | solution.py:266
  38.5 12.5 %collective-permute-start.2 = (f32[384,128]{1,0:T(8,128)S(1)}, f32[384,128]{1,0:T(8,128)S(1)}, u32[]{:S(2)}, u32[]{:S(2)}) collective-permute-start(f32[384,128]{1,0:T(8,128)S(1)} %get-tuple-element.37.refs_0_), channel_id=1, source_target_pairs={{0,4},{4,0},{8,12},{12,8},{16,20},{20,16},{24,28},{28,24},{32,36},... | collective-permute-start | bytes 589832 | tf_op jit(solution)/shard_map/ppermute | solution.py:266
  43.1 14.4 %collective-permute-start.8 = (f32[256,256]{1,0:T(8,128)S(1)}, f32[256,256]{1,0:T(8,128)S(1)}, u32[]{:S(2)}, u32[]{:S(2)}) collective-permute-start(f32[256,256]{1,0:T(8,128)S(1)} %get-tuple-element.51.refs_5_), channel_id=1, source_target_pairs={{0,12},{4,8},{8,4},{12,0},{16,28},{20,24},{24,20},{28,16},{32,44},... | collective-permute-start | bytes 786440 | tf_op jit(solution)/shard_map/ppermute | solution.py:266
  45.9 14.7 %collective-permute-start.7 = (f32[256,256]{1,0:T(8,128)S(1)}, f32[256,256]{1,0:T(8,128)S(1)}, u32[]{:S(2)}, u32[]{:S(2)}) collective-permute-start(f32[256,256]{1,0:T(8,128)S(1)} %get-tuple-element.49.refs_4_), channel_id=1, source_target_pairs={{0,12},{4,8},{8,4},{12,0},{16,28},{20,24},{24,20},{28,16},{32,44},... | collective-permute-start | bytes 786440 | tf_op jit(solution)/shard_map/ppermute | solution.py:266
  54.3 9.9 %collective-permute-start.3 = (f32[384,128]{1,0:T(8,128)S(1)}, f32[384,128]{1,0:T(8,128)S(1)}, u32[]{:S(2)}, u32[]{:S(2)}) collective-permute-start(f32[384,128]{1,0:T(8,128)S(1)} %get-tuple-element.41), channel_id=1, source_target_pairs={{0,12},{4,8},{8,4},{12,0},{16,28},{20,24},{24,20},{28,16},{32,44},... | collective-permute-start | bytes 589832 | tf_op jit(solution)/shard_map/ppermute | solution.py:266

commit v6 on v5

--- a/solution.py
+++ b/solution.py
@@ -138,9 +138,8 @@
     wide_ref[...] = flag(invert(cap_ref, 2.0 * coupling, inv_ref, pair_ref))
 
 
-def cross_kernel(coupling, wide_ref, y1_ref, y2t_ref, cap_ref, inv_ref, bt_ref, ht_ref, sent_ref, dd_ref):
-    y2t = y2t_ref[...]
-    bt_ref[...] = dot6(y2t, y1_ref[...])
+def cross_kernel(coupling, wide_ref, y1_ref, y2t_ref, cap_ref, inv_ref, bt_ref, ht_ref, sent_ref):
+    bt_ref[...] = dot6(y2t_ref[...], y1_ref[...])
     ht_ref[...] = dot6(bt_ref[...], inv_ref[...])
 
     @pl.when(wide_ref[0, 0] > 0.5)
@@ -149,15 +148,16 @@
         ht_ref[...] = h + dot3(bt_ref[...] - dot6(h, cap_ref[...]), inv_ref[...])
 
     sent_ref[...] = jnp.where(lax.axis_index("cols") % 2 == 0, inv_ref[...], ht_ref[...])
-    dd_ref[...] = dot6(y2t, y2t, NT)
-
-
-def project_kernel(coupling, y2t_ref, z_ref, y_ref, ht_ref, w_ref, left_ref, right_ref):
-    w_ref[...] = dot3(y2t_ref[...], z_ref[...])
+
+
+def project_kernel(coupling, y2t_ref, z_ref, y_ref, ht_ref, dd_ref, w_ref, left_ref, right_ref):
+    y2t = y2t_ref[...]
+    w_ref[...] = dot3(y2t, z_ref[...])
     v = w_ref[...] - dot3(ht_ref[...], y_ref[...])
     half = left_ref.shape[1]
     left_ref[...] = v[:, :half]
     right_ref[...] = v[:, half:]
+    dd_ref[...] = dot6(y2t, y2t, NT)
 
 
 def pair_kernel(coupling, wide_ref, cap_ref, inv_ref, bt_ref, other_ref, dd_ref, schur_ref, t_ref, et_ref, p_ref):
@@ -282,9 +282,10 @@
     other_y = swap(y, 1)
     inv, wide = run(invert_kernel, [square, tile], cap, micros=4, scratch=[(2 * rank, rank)])
     y2t = core_gather(jnp.concatenate([own_part, far_part], axis=0))
-    bt, ht, sent, dd = run(cross_kernel, [square] * 4, wide, level1_basis, y2t, cap, inv, micros=4)
+    bt, ht, sent = run(cross_kernel, [square] * 3, wide, level1_basis, y2t, cap, inv, micros=4)
     other_half = swap(sent, 1)
-    w, v_left, v_right = run(project_kernel, [tall, (rank, columns // 2), (rank, columns // 2)], y2t, probes, y, ht, micros=3)
+    side = (rank, columns // 2)
+    dd, w, v_left, v_right = run(project_kernel, [square, tall, side, side], y2t, probes, y, ht, micros=3)
     other_v_left = swap(v_left, 1)
     other_v_right = swap(v_right, 1)
     other = core_gather(other_half)

time: 68.4 us -> 67.6 us (0.988)
  transfers between devices with their start and end apart: 9 -> 9, of which waited for: 3 -> 2; matrix products, arithmetic and copies ran while one was open for 0% -> 0% of each run, Pallas kernels for 22% -> 22%
where the time goes in v6:
time: 67.6 us; the launch traced here: 67.2 us
  starting transfers between devices  31.8 us (47%)
  Pallas kernels  22.2 us (33%)
  waiting for transfers between devices  6.61 us (10%)
  blocking collectives  4.68 us (7%)
  between operations  1.01 us (1%)
  local copies, waits for them, and re-layouts  0.96 us (1%)
    ppermute x9, starting transfers between devices, swap(): lax.ppermute(value, axis, [(i, i ^ bits) for i in range(lax.axis_size(axi...  31.8 us
    pallas_call x10, Pallas kernels, call(): pl.pallas_call(kernel, out_shape=[o if isinstance(o, jax.ShapeDtypeStruct...  22.2 us
    ppermute x9, waiting for transfers between devices, swap(): lax.ppermute(value, axis, [(i, i ^ bits) for i in range(lax.axis_size(axi...  6.61 us
    all_gather x2, blocking collectives, core_gather(): lax.all_gather(value, 'cols', axis=0, tiled=True, axis_index_groups=groups)  4.68 us
  transfers between devices with their start and end apart: 9, of which 2 were waited for; matrix products, arithmetic and copies ran while one was open for 0% of the time, Pallas kernels for 22%

profile of v6, /device:TPU:16, one launch (start us, length us, event | category | flops | bytes accessed | tf_op | source)
XLA Modules:
  0.0 67.2 jit_solution(15683473865435632094)
XLA Ops:
  0.6 3.7 %shard_map.50 = (f32[256,256]{1,0:T(8,128)}, f32[256,512]{1,0:T(8,128)}, f32[64,768]{1,0:T(8,128)}) custom-call(f32[768,256]{1,0:T(8,128)} %refs_0_.3, f32[768,512]{1,0:T(8,128)} %refs_2_.3, f32[64,768]{1,0:T(8,128)} %refs_2_.2), custom_call_target="tpu_custom_call" | custom-call | flops 3000000000 | bytes 9000000 | tf_op jit(solution)/shard_map/pallas_call | solution.py:243
  4.4 7.6 %collective-permute-start = (f32[64,768]{1,0:T(8,128)}, f32[64,768]{1,0:T(8,128)S(1)}, u32[]{:S(2)}, u32[]{:S(2)}) collective-permute-start(f32[64,768]{1,0:T(8,128)} %get-tuple-element.33), channel_id=1, source_target_pairs={{0,2},{1,3},{2,0},{3,1},{4,6},{5,7},{6,4},{7,5},{8,10},{9,11},{10,... | collective-permute-start | bytes 589832 | tf_op jit(solution)/shard_map/ppermute | solution.py:266
  12.0 1.9 %collective-permute-start.4 = (f32[256,512]{1,0:T(8,128)}, f32[256,512]{1,0:T(8,128)S(1)}, u32[]{:S(2)}, u32[]{:S(2)}) collective-permute-start(f32[256,512]{1,0:T(8,128)} %get-tuple-element.36.refs_2_.y_ref), channel_id=1, source_target_pairs={{0,4},{4,0},{8,12},{12,8},{16,20},{20,16},{24,28},{28,24},{32,36},... | collective-permute-start | bytes 1572872 | tf_op jit(solution)/shard_map/ppermute | solution.py:266
  13.9 0.9 %copy-done.3 = f32[256,256]{1,0:T(8,128)S(1)} copy-done((f32[256,256]{1,0:T(8,128)S(1)}, f32[256,256]{1,0:T(8,128)}, u32[]{:S(2)}) %copy-start.3) | copy-done | bytes 262168
  14.9 3.0 %shard_map.51 = (f32[256,256]{1,0:T(8,128)S(1)}, f32[8,128]{1,0:T(8,128)S(1)}) custom-call(f32[256,256]{1,0:T(8,128)S(1)} %copy-done.3), custom_call_target="tpu_custom_call" | custom-call | flops 4000000000 | bytes 12000000 | tf_op jit(solution)/shard_map/pallas_call | solution.py:243
  17.9 0.0 copy-start.1
  17.9 0.0 collective-permute-done
  18.0 2.5 %all_gather.6.refs_2_.refs_0_.refs_1_ = f32[256,768]{1,0:T(8,128)S(1)} all-gather(f32[128,768]{1,0:T(8,128)S(1)} %pad_maximum_fusion), channel_id=1, replica_groups={{0,1},{2,3},{4,5},{6,7},{8,9},{10,11},{12,13},{14,15},{16,17},{18,19},{..., dimensions={0}, use_global_device_ids=true | all-gather | bytes 1179648 | tf_op jit(solution)/shard_map/all_gather | solution.py:270
  20.5 1.5 %shard_map.52 = (f32[256,256]{1,0:T(8,128)S(1)}, f32[256,256]{1,0:T(8,128)S(1)}, f32[256,256]{1,0:T(8,128)S(1)}) custom-call(f32[8,128]{1,0:T(8,128)S(1)} %get-tuple-element.31.refs_0_.wide_ref, f32[768,256]{1,0:T(8,128)S(1)} %copy-done.1, f32[256,768]{1,0:T(8,128)S(1)} %all_gather.6.refs_2_.refs_0_.refs_1_, f32[256,256]{1,0:T(8,128)S(1)} %copy-done.3, ...), custom_call_target="tpu_custom_call" | custom-call | flops 4000000000 | bytes 12000000 | tf_op jit(solution)/shard_map/pallas_call | solution.py:243
  22.0 3.9 %collective-permute-start.1 = (f32[256,256]{1,0:T(8,128)S(1)}, f32[256,256]{1,0:T(8,128)S(1)}, u32[]{:S(2)}, u32[]{:S(2)}) collective-permute-start(f32[256,256]{1,0:T(8,128)S(1)} %get-tuple-element.35), channel_id=1, source_target_pairs={{0,4},{4,0},{8,12},{12,8},{16,20},{20,16},{24,28},{28,24},{32,36},... | collective-permute-start | bytes 786440 | tf_op jit(solution)/shard_map/ppermute | solution.py:266
  25.9 1.6 %shard_map.53 = (f32[256,256]{1,0:T(8,128)S(1)}, f32[256,512]{1,0:T(8,128)S(1)}, f32[256,256]{1,0:T(8,128)S(1)}, f32[256,256]{1,0:T(8,128)S(1)}) custom-call(f32[256,768]{1,0:T(8,128)S(1)} %all_gather.6.refs_2_.refs_0_.refs_1_, f32[768,512]{1,0:T(8,128)S(1)} %copy-done, f32[256,512]{1,0:T(8,128)S(1)} %copy-done.2, f32[256,256]{1,0:T(8,128)S(1)} %get-tuple-element.37.refs_3_), custom_call_target="tpu_custom_call" | custom-call | flops 3000000000 | bytes 9000000 | tf_op jit(solution)/shard_map/pallas_call | solution.py:243
  27.6 1.9 %collective-permute-start.5 = (f32[256,256]{1,0:T(8,128)S(1)}, f32[256,256]{1,0:T(8,128)S(1)}, u32[]{:S(2)}, u32[]{:S(2)}) collective-permute-start(f32[256,256]{1,0:T(8,128)S(1)} %get-tuple-element.48), channel_id=1, source_target_pairs={{0,4},{4,0},{8,12},{12,8},{16,20},{20,16},{24,28},{28,24},{32,36},... | collective-permute-start | bytes 786440 | tf_op jit(solution)/shard_map/ppermute | solution.py:266
  29.5 3.9 %collective-permute-start.6 = (f32[256,256]{1,0:T(8,128)S(1)}, f32[256,256]{1,0:T(8,128)S(1)}, u32[]{:S(2)}, u32[]{:S(2)}) collective-permute-start(f32[256,256]{1,0:T(8,128)S(1)} %get-tuple-element.50), channel_id=1, source_target_pairs={{0,4},{4,0},{8,12},{12,8},{16,20},{20,16},{24,28},{28,24},{32,36},... | collective-permute-start | bytes 786440 | tf_op jit(solution)/shard_map/ppermute | solution.py:266
  33.4 0.0 collective-permute-done.1
  33.4 2.2 %all_gather.7.refs_4_.other_ref = f32[512,256]{1,0:T(8,128)S(1)} all-gather(f32[256,256]{1,0:T(8,128)S(1)} %collective-permute-done.1), channel_id=1, replica_groups={{0,1},{2,3},{4,5},{6,7},{8,9},{10,11},{12,13},{14,15},{16,17},{18,19},{..., dimensions={0}, use_global_device_ids=true | all-gather | bytes 786432 | tf_op jit(solution)/shard_map/all_gather | solution.py:270
  35.6 2.5 %shard_map.54 = (f32[256,256]{1,0:T(8,128)S(1)}, f32[256,256]{1,0:T(8,128)S(1)}, f32[256,256]{1,0:T(8,128)S(1)}, f32[384,128]{1,0:T(8,128)S(1)}) custom-call(f32[8,128]{1,0:T(8,128)S(1)} %get-tuple-element.31.refs_0_.wide_ref, f32[256,256]{1,0:T(8,128)S(1)} %copy-done.3, f32[256,256]{1,0:T(8,128)S(1)} %get-tuple-element.32.refs_4_.refs_2_, ...), custom_call_target="tpu_custom_call" | custom-call | flops 20000000000 | bytes 60000000 | tf_op jit(solution)/shard_map/pallas_call | solution.py:243
  38.2 3.5 %collective-permute-start.2 = (f32[384,128]{1,0:T(8,128)S(1)}, f32[384,128]{1,0:T(8,128)S(1)}, u32[]{:S(2)}, u32[]{:S(2)}) collective-permute-start(f32[384,128]{1,0:T(8,128)S(1)} %get-tuple-element.39.refs_0_), channel_id=1, source_target_pairs={{0,4},{4,0},{8,12},{12,8},{16,20},{20,16},{24,28},{28,24},{32,36},... | collective-permute-start | bytes 589832 | tf_op jit(solution)/shard_map/ppermute | solution.py:266
  41.7 0.0 collective-permute-done.5.other_v_ref
  41.7 0.0 collective-permute-done.4.other_y_ref
  41.7 0.6 shard_map.56
  42.3 1.9 %collective-permute-start.7 = (f32[256,256]{1,0:T(8,128)S(1)}, f32[256,256]{1,0:T(8,128)S(1)}, u32[]{:S(2)}, u32[]{:S(2)}) collective-permute-start(f32[256,256]{1,0:T(8,128)S(1)} %get-tuple-element.49.refs_4_), channel_id=1, source_target_pairs={{0,12},{4,8},{8,4},{12,0},{16,28},{20,24},{24,20},{28,16},{32,44},... | collective-permute-start | bytes 786440 | tf_op jit(solution)/shard_map/ppermute | solution.py:266
  44.3 0.0 collective-permute-done.6.other_v_ref
  44.3 0.8 %shard_map.57 = (f32[256,256]{1,0:T(8,128)S(1)}, f32[256,256]{1,0:T(8,128)S(1)}) custom-call(f32[8,128]{1,0:T(8,128)S(1)} %get-tuple-element.31.refs_0_.wide_ref, f32[256,256]{1,0:T(8,128)S(1)} %get-tuple-element.44.schur_ref, f32[256,256]{1,0:T(8,128)S(1)} %get-tuple-element.45.t_ref, f32[256,256]{1,0:T(8,128)S(1)} %get-tuple-element.46.et_ref.refs_3_, ...), custom_call_target="tpu_custom_call" | custom-call | flops 3000000000 | bytes 9000000 | tf_op jit(solution)/shard_map/pallas_call | solution.py:243
  45.1 5.1 %collective-permute-start.8 = (f32[256,256]{1,0:T(8,128)S(1)}, f32[256,256]{1,0:T(8,128)S(1)}, u32[]{:S(2)}, u32[]{:S(2)}) collective-permute-start(f32[256,256]{1,0:T(8,128)S(1)} %get-tuple-element.51.refs_5_), channel_id=1, source_target_pairs={{0,12},{4,8},{8,4},{12,0},{16,28},{20,24},{24,20},{28,16},{32,44},... | collective-permute-start | bytes 786440 | tf_op jit(solution)/shard_map/ppermute | solution.py:266
  50.3 0.0 collective-permute-done.2.refs_1_
  50.3 3.2 %shard_map.55 = (f32[256,256]{1,0:T(8,128)S(1)}, f32[256,256]{1,0:T(8,128)S(1)}, f32[8,128]{1,0:T(8,128)S(1)}, f32[384,128]{1,0:T(8,128)S(1)}) custom-call(f32[384,128]{1,0:T(8,128)S(1)} %get-tuple-element.39.refs_0_, f32[384,128]{1,0:T(8,128)S(1)} %collective-permute-done.2.refs_1_), custom_call_target="tpu_custom_call" | custom-call | flops 6000000000 | bytes 18000000 | tf_op jit(solution)/shard_map/pallas_call | solution.py:243
  53.5 1.9 %collective-permute-start.3 = (f32[384,128]{1,0:T(8,128)S(1)}, f32[384,128]{1,0:T(8,128)S(1)}, u32[]{:S(2)}, u32[]{:S(2)}) collective-permute-start(f32[384,128]{1,0:T(8,128)S(1)} %get-tuple-element.43), channel_id=1, source_target_pairs={{0,12},{4,8},{8,4},{12,0},{16,28},{20,24},{24,20},{28,16},{32,44},... | collective-permute-start | bytes 589832 | tf_op jit(solution)/shard_map/ppermute | solution.py:266
  55.4 1.4 %shard_map.58 = (f32[768,512]{1,0:T(8,128)S(1)}, bf16[768,256]{1,0:T(8,128)(2,1)S(1)}, bf16[768,256]{1,0:T(8,128)(2,1)S(1)}, f32[64,768]{1,0:T(8,128)}) custom-call(f32[768,256]{1,0:T(8,128)S(1)} %copy-done.1, f32[256,768]{1,0:T(8,128)S(1)} %all_gather.6.refs_2_.refs_0_.refs_1_, f32[768,512]{1,0:T(8,128)S(1)} %copy-done, ...), custom_call_target="tpu_custom_call" | custom-call | flops 4000000000 | bytes 12000000 | tf_op jit(solution)/shard_map/pallas_call | solution.py:243
  56.8 0.0 collective-permute-done.7.refs_6_
  56.8 3.0 %collective-permute-done.8.refs_7_ = f32[256,256]{1,0:T(8,128)S(1)} collective-permute-done((f32[256,256]{1,0:T(8,128)S(1)}, f32[256,256]{1,0:T(8,128)S(1)}, u32[]{:S(2)}, u32[]{:S(2)}) %collective-permute-start.8) | collective-permute-done | bytes 262176 | tf_op jit(solution)/shard_map/ppermute | solution.py:266
  59.8 3.6 %collective-permute-done.3.refs_3_ = f32[384,128]{1,0:T(8,128)S(1)} collective-permute-done((f32[384,128]{1,0:T(8,128)S(1)}, f32[384,128]{1,0:T(8,128)S(1)}, u32[]{:S(2)}, u32[]{:S(2)}) %collective-permute-start.3) | collective-permute-done | bytes 196640 | tf_op jit(solution)/shard_map/ppermute | solution.py:266
  63.4 3.7 %shard_map.59 = f32[768,512]{1,0:T(8,128)} custom-call(f32[8,128]{1,0:T(8,128)S(1)} %get-tuple-element.40.refs_0_, f32[256,256]{1,0:T(8,128)S(1)} %get-tuple-element.41.refs_1_, f32[256,256]{1,0:T(8,128)S(1)} %get-tuple-element.42.refs_2_, f32[384,128]{1,0:T(8,128)S(1)} %collective-permute-done.3.refs_3_, f32[256,256]{1,0:T(8,128)S(1)} %get-tuple-element.49.refs_4_, ...), custom_call_target="tpu_custom_call" | custom-call | flops 7000000000 | bytes 21000000 | tf_op jit(solution)/shard_map/pallas_call | solution.py:243
  (9 shorter events, 0.0 us)
Async XLA Ops:
  4.4 13.5 %collective-permute-start = (f32[64,768]{1,0:T(8,128)}, f32[64,768]{1,0:T(8,128)S(1)}, u32[]{:S(2)}, u32[]{:S(2)}) collective-permute-start(f32[64,768]{1,0:T(8,128)} %get-tuple-element.33), channel_id=1, source_target_pairs={{0,2},{1,3},{2,0},{3,1},{4,6},{5,7},{6,4},{7,5},{8,10},{9,11},{10,... | collective-permute-start | bytes 589832 | tf_op jit(solution)/shard_map/ppermute | solution.py:266
  12.0 29.7 %collective-permute-start.4 = (f32[256,512]{1,0:T(8,128)}, f32[256,512]{1,0:T(8,128)S(1)}, u32[]{:S(2)}, u32[]{:S(2)}) collective-permute-start(f32[256,512]{1,0:T(8,128)} %get-tuple-element.36.refs_2_.y_ref), channel_id=1, source_target_pairs={{0,4},{4,0},{8,12},{12,8},{16,20},{20,16},{24,28},{28,24},{32,36},... | collective-permute-start | bytes 1572872 | tf_op jit(solution)/shard_map/ppermute | solution.py:266
  13.9 1.0 %copy-start.3 = (f32[256,256]{1,0:T(8,128)S(1)}, f32[256,256]{1,0:T(8,128)}, u32[]{:S(2)}) copy-start(f32[256,256]{1,0:T(8,128)} %get-tuple-element.30.refs_0_.refs_3_.refs_1_) | copy-start | bytes 786436
  14.9 3.0 %copy-start.4 = (f32[64,768]{1,0:T(8,128)S(1)}, f32[64,768]{1,0:T(8,128)}, u32[]{:S(2)}) copy-start(f32[64,768]{1,0:T(8,128)} %get-tuple-element.33) | copy-start | bytes 589828
  17.9 2.6 %copy-start.1 = (f32[768,256]{1,0:T(8,128)S(1)}, f32[768,256]{1,0:T(8,128)}, u32[]{:S(2)}) copy-start(f32[768,256]{1,0:T(8,128)} %refs_0_.3) | copy-start | bytes 2359300
  20.5 5.5 %copy-start = (f32[768,512]{1,0:T(8,128)S(1)}, f32[768,512]{1,0:T(8,128)}, u32[]{:S(2)}) copy-start(f32[768,512]{1,0:T(8,128)} %refs_2_.3) | copy-start | bytes 4718596
  20.5 5.5 %copy-start.2 = (f32[256,512]{1,0:T(8,128)S(1)}, f32[256,512]{1,0:T(8,128)}, u32[]{:S(2)}) copy-start(f32[256,512]{1,0:T(8,128)} %get-tuple-element.36.refs_2_.y_ref) | copy-start | bytes 1572868
  22.0 11.4 %collective-permute-start.1 = (f32[256,256]{1,0:T(8,128)S(1)}, f32[256,256]{1,0:T(8,128)S(1)}, u32[]{:S(2)}, u32[]{:S(2)}) collective-permute-start(f32[256,256]{1,0:T(8,128)S(1)} %get-tuple-element.35), channel_id=1, source_target_pairs={{0,4},{4,0},{8,12},{12,8},{16,20},{20,16},{24,28},{28,24},{32,36},... | collective-permute-start | bytes 786440 | tf_op jit(solution)/shard_map/ppermute | solution.py:266
  27.6 14.1 %collective-permute-start.5 = (f32[256,256]{1,0:T(8,128)S(1)}, f32[256,256]{1,0:T(8,128)S(1)}, u32[]{:S(2)}, u32[]{:S(2)}) collective-permute-start(f32[256,256]{1,0:T(8,128)S(1)} %get-tuple-element.48), channel_id=1, source_target_pairs={{0,4},{4,0},{8,12},{12,8},{16,20},{20,16},{24,28},{28,24},{32,36},... | collective-permute-start | bytes 786440 | tf_op jit(solution)/shard_map/ppermute | solution.py:266
  29.5 14.8 %collective-permute-start.6 = (f32[256,256]{1,0:T(8,128)S(1)}, f32[256,256]{1,0:T(8,128)S(1)}, u32[]{:S(2)}, u32[]{:S(2)}) collective-permute-start(f32[256,256]{1,0:T(8,128)S(1)} %get-tuple-element.50), channel_id=1, source_target_pairs={{0,4},{4,0},{8,12},{12,8},{16,20},{20,16},{24,28},{28,24},{32,36},... | collective-permute-start | bytes 786440 | tf_op jit(solution)/shard_map/ppermute | solution.py:266
  38.2 12.1 %collective-permute-start.2 = (f32[384,128]{1,0:T(8,128)S(1)}, f32[384,128]{1,0:T(8,128)S(1)}, u32[]{:S(2)}, u32[]{:S(2)}) collective-permute-start(f32[384,128]{1,0:T(8,128)S(1)} %get-tuple-element.39.refs_0_), channel_id=1, source_target_pairs={{0,4},{4,0},{8,12},{12,8},{16,20},{20,16},{24,28},{28,24},{32,36},... | collective-permute-start | bytes 589832 | tf_op jit(solution)/shard_map/ppermute | solution.py:266
  42.3 14.5 %collective-permute-start.7 = (f32[256,256]{1,0:T(8,128)S(1)}, f32[256,256]{1,0:T(8,128)S(1)}, u32[]{:S(2)}, u32[]{:S(2)}) collective-permute-start(f32[256,256]{1,0:T(8,128)S(1)} %get-tuple-element.49.refs_4_), channel_id=1, source_target_pairs={{0,12},{4,8},{8,4},{12,0},{16,28},{20,24},{24,20},{28,16},{32,44},... | collective-permute-start | bytes 786440 | tf_op jit(solution)/shard_map/ppermute | solution.py:266
  45.1 14.6 %collective-permute-start.8 = (f32[256,256]{1,0:T(8,128)S(1)}, f32[256,256]{1,0:T(8,128)S(1)}, u32[]{:S(2)}, u32[]{:S(2)}) collective-permute-start(f32[256,256]{1,0:T(8,128)S(1)} %get-tuple-element.51.refs_5_), channel_id=1, source_target_pairs={{0,12},{4,8},{8,4},{12,0},{16,28},{20,24},{24,20},{28,16},{32,44},... | collective-permute-start | bytes 786440 | tf_op jit(solution)/shard_map/ppermute | solution.py:266
  53.5 9.9 %collective-permute-start.3 = (f32[384,128]{1,0:T(8,128)S(1)}, f32[384,128]{1,0:T(8,128)S(1)}, u32[]{:S(2)}, u32[]{:S(2)}) collective-permute-start(f32[384,128]{1,0:T(8,128)S(1)} %get-tuple-element.43), channel_id=1, source_target_pairs={{0,12},{4,8},{8,4},{12,0},{16,28},{20,24},{24,20},{28,16},{32,44},... | collective-permute-start | bytes 589832 | tf_op jit(solution)/shard_map/ppermute | solution.py:266

commit v7 on v6

--- a/solution.py
+++ b/solution.py
@@ -63,7 +63,7 @@
             pair[n:] = (1.0 - gain) * eye + gain * product[n:]
             return square / (2.0 - square)
 
-        lax.while_loop(lambda state: state > 1e-3, step, spread)
+        lax.while_loop(lambda state: state > 2e-4, step, spread)
         x = pair[:n]
         store[...] = x + dot3(x, eye - dot6(matrix[...], x))
 

time: 67.6 us -> 67.6 us (level)
  no operation moved by 1% of the time
where the time goes in v7:
time: 67.6 us; the launch traced here: 67.2 us
  starting transfers between devices  31.8 us (47%)
  Pallas kernels  22.2 us (33%)
  waiting for transfers between devices  6.61 us (10%)
  blocking collectives  4.68 us (7%)
  between operations  1.01 us (1%)
  local copies, waits for them, and re-layouts  0.96 us (1%)
    ppermute x9, starting transfers between devices, swap(): lax.ppermute(value, axis, [(i, i ^ bits) for i in range(lax.axis_size(axi...  31.8 us
    pallas_call x10, Pallas kernels, call(): pl.pallas_call(kernel, out_shape=[o if isinstance(o, jax.ShapeDtypeStruct...  22.2 us
    ppermute x9, waiting for transfers between devices, swap(): lax.ppermute(value, axis, [(i, i ^ bits) for i in range(lax.axis_size(axi...  6.61 us
    all_gather x2, blocking collectives, core_gather(): lax.all_gather(value, 'cols', axis=0, tiled=True, axis_index_groups=groups)  4.68 us
  transfers between devices with their start and end apart: 9, of which 2 were waited for; matrix products, arithmetic and copies ran while one was open for 0% of the time, Pallas kernels for 22%

profile of v7, /device:TPU:16, one launch (start us, length us, event | category | flops | bytes accessed | tf_op | source)
XLA Modules:
  0.0 67.2 jit_solution(7607135373301200041)
XLA Ops:
  0.6 3.7 %shard_map.50 = (f32[256,256]{1,0:T(8,128)}, f32[256,512]{1,0:T(8,128)}, f32[64,768]{1,0:T(8,128)}) custom-call(f32[768,256]{1,0:T(8,128)} %refs_0_.3, f32[768,512]{1,0:T(8,128)} %refs_2_.3, f32[64,768]{1,0:T(8,128)} %refs_2_.2), custom_call_target="tpu_custom_call" | custom-call | flops 3000000000 | bytes 9000000 | tf_op jit(solution)/shard_map/pallas_call | solution.py:243
  4.4 7.6 %collective-permute-start = (f32[64,768]{1,0:T(8,128)}, f32[64,768]{1,0:T(8,128)S(1)}, u32[]{:S(2)}, u32[]{:S(2)}) collective-permute-start(f32[64,768]{1,0:T(8,128)} %get-tuple-element.33), channel_id=1, source_target_pairs={{0,2},{1,3},{2,0},{3,1},{4,6},{5,7},{6,4},{7,5},{8,10},{9,11},{10,... | collective-permute-start | bytes 589832 | tf_op jit(solution)/shard_map/ppermute | solution.py:266
  12.0 1.9 %collective-permute-start.4 = (f32[256,512]{1,0:T(8,128)}, f32[256,512]{1,0:T(8,128)S(1)}, u32[]{:S(2)}, u32[]{:S(2)}) collective-permute-start(f32[256,512]{1,0:T(8,128)} %get-tuple-element.36.refs_2_.y_ref), channel_id=1, source_target_pairs={{0,4},{4,0},{8,12},{12,8},{16,20},{20,16},{24,28},{28,24},{32,36},... | collective-permute-start | bytes 1572872 | tf_op jit(solution)/shard_map/ppermute | solution.py:266
  13.9 0.9 %copy-done.3 = f32[256,256]{1,0:T(8,128)S(1)} copy-done((f32[256,256]{1,0:T(8,128)S(1)}, f32[256,256]{1,0:T(8,128)}, u32[]{:S(2)}) %copy-start.3) | copy-done | bytes 262168
  14.9 3.0 %shard_map.51 = (f32[256,256]{1,0:T(8,128)S(1)}, f32[8,128]{1,0:T(8,128)S(1)}) custom-call(f32[256,256]{1,0:T(8,128)S(1)} %copy-done.3), custom_call_target="tpu_custom_call" | custom-call | flops 4000000000 | bytes 12000000 | tf_op jit(solution)/shard_map/pallas_call | solution.py:243
  17.9 0.0 copy-start.1
  17.9 0.0 collective-permute-done
  18.0 2.5 %all_gather.6.refs_2_.refs_0_.refs_1_ = f32[256,768]{1,0:T(8,128)S(1)} all-gather(f32[128,768]{1,0:T(8,128)S(1)} %pad_maximum_fusion), channel_id=1, replica_groups={{0,1},{2,3},{4,5},{6,7},{8,9},{10,11},{12,13},{14,15},{16,17},{18,19},{..., dimensions={0}, use_global_device_ids=true | all-gather | bytes 1179648 | tf_op jit(solution)/shard_map/all_gather | solution.py:270
  20.5 1.5 %shard_map.52 = (f32[256,256]{1,0:T(8,128)S(1)}, f32[256,256]{1,0:T(8,128)S(1)}, f32[256,256]{1,0:T(8,128)S(1)}) custom-call(f32[8,128]{1,0:T(8,128)S(1)} %get-tuple-element.31.refs_0_.wide_ref, f32[768,256]{1,0:T(8,128)S(1)} %copy-done.1, f32[256,768]{1,0:T(8,128)S(1)} %all_gather.6.refs_2_.refs_0_.refs_1_, f32[256,256]{1,0:T(8,128)S(1)} %copy-done.3, ...), custom_call_target="tpu_custom_call" | custom-call | flops 4000000000 | bytes 12000000 | tf_op jit(solution)/shard_map/pallas_call | solution.py:243
  22.0 3.9 %collective-permute-start.1 = (f32[256,256]{1,0:T(8,128)S(1)}, f32[256,256]{1,0:T(8,128)S(1)}, u32[]{:S(2)}, u32[]{:S(2)}) collective-permute-start(f32[256,256]{1,0:T(8,128)S(1)} %get-tuple-element.35), channel_id=1, source_target_pairs={{0,4},{4,0},{8,12},{12,8},{16,20},{20,16},{24,28},{28,24},{32,36},... | collective-permute-start | bytes 786440 | tf_op jit(solution)/shard_map/ppermute | solution.py:266
  25.9 1.6 %shard_map.53 = (f32[256,256]{1,0:T(8,128)S(1)}, f32[256,512]{1,0:T(8,128)S(1)}, f32[256,256]{1,0:T(8,128)S(1)}, f32[256,256]{1,0:T(8,128)S(1)}) custom-call(f32[256,768]{1,0:T(8,128)S(1)} %all_gather.6.refs_2_.refs_0_.refs_1_, f32[768,512]{1,0:T(8,128)S(1)} %copy-done, f32[256,512]{1,0:T(8,128)S(1)} %copy-done.2, f32[256,256]{1,0:T(8,128)S(1)} %get-tuple-element.37.refs_3_), custom_call_target="tpu_custom_call" | custom-call | flops 3000000000 | bytes 9000000 | tf_op jit(solution)/shard_map/pallas_call | solution.py:243
  27.6 1.9 %collective-permute-start.5 = (f32[256,256]{1,0:T(8,128)S(1)}, f32[256,256]{1,0:T(8,128)S(1)}, u32[]{:S(2)}, u32[]{:S(2)}) collective-permute-start(f32[256,256]{1,0:T(8,128)S(1)} %get-tuple-element.48), channel_id=1, source_target_pairs={{0,4},{4,0},{8,12},{12,8},{16,20},{20,16},{24,28},{28,24},{32,36},... | collective-permute-start | bytes 786440 | tf_op jit(solution)/shard_map/ppermute | solution.py:266
  29.5 3.9 %collective-permute-start.6 = (f32[256,256]{1,0:T(8,128)S(1)}, f32[256,256]{1,0:T(8,128)S(1)}, u32[]{:S(2)}, u32[]{:S(2)}) collective-permute-start(f32[256,256]{1,0:T(8,128)S(1)} %get-tuple-element.50), channel_id=1, source_target_pairs={{0,4},{4,0},{8,12},{12,8},{16,20},{20,16},{24,28},{28,24},{32,36},... | collective-permute-start | bytes 786440 | tf_op jit(solution)/shard_map/ppermute | solution.py:266
  33.4 0.0 collective-permute-done.1
  33.4 2.2 %all_gather.7.refs_4_.other_ref = f32[512,256]{1,0:T(8,128)S(1)} all-gather(f32[256,256]{1,0:T(8,128)S(1)} %collective-permute-done.1), channel_id=1, replica_groups={{0,1},{2,3},{4,5},{6,7},{8,9},{10,11},{12,13},{14,15},{16,17},{18,19},{..., dimensions={0}, use_global_device_ids=true | all-gather | bytes 786432 | tf_op jit(solution)/shard_map/all_gather | solution.py:270
  35.6 2.5 %shard_map.54 = (f32[256,256]{1,0:T(8,128)S(1)}, f32[256,256]{1,0:T(8,128)S(1)}, f32[256,256]{1,0:T(8,128)S(1)}, f32[384,128]{1,0:T(8,128)S(1)}) custom-call(f32[8,128]{1,0:T(8,128)S(1)} %get-tuple-element.31.refs_0_.wide_ref, f32[256,256]{1,0:T(8,128)S(1)} %copy-done.3, f32[256,256]{1,0:T(8,128)S(1)} %get-tuple-element.32.refs_4_.refs_2_, ...), custom_call_target="tpu_custom_call" | custom-call | flops 20000000000 | bytes 60000000 | tf_op jit(solution)/shard_map/pallas_call | solution.py:243
  38.2 3.5 %collective-permute-start.2 = (f32[384,128]{1,0:T(8,128)S(1)}, f32[384,128]{1,0:T(8,128)S(1)}, u32[]{:S(2)}, u32[]{:S(2)}) collective-permute-start(f32[384,128]{1,0:T(8,128)S(1)} %get-tuple-element.39.refs_0_), channel_id=1, source_target_pairs={{0,4},{4,0},{8,12},{12,8},{16,20},{20,16},{24,28},{28,24},{32,36},... | collective-permute-start | bytes 589832 | tf_op jit(solution)/shard_map/ppermute | solution.py:266
  41.7 0.0 collective-permute-done.5.other_v_ref
  41.7 0.0 collective-permute-done.4.other_y_ref
  41.7 0.6 shard_map.56
  42.3 1.9 %collective-permute-start.7 = (f32[256,256]{1,0:T(8,128)S(1)}, f32[256,256]{1,0:T(8,128)S(1)}, u32[]{:S(2)}, u32[]{:S(2)}) collective-permute-start(f32[256,256]{1,0:T(8,128)S(1)} %get-tuple-element.49.refs_4_), channel_id=1, source_target_pairs={{0,12},{4,8},{8,4},{12,0},{16,28},{20,24},{24,20},{28,16},{32,44},... | collective-permute-start | bytes 786440 | tf_op jit(solution)/shard_map/ppermute | solution.py:266
  44.3 0.0 collective-permute-done.6.other_v_ref
  44.3 0.8 %shard_map.57 = (f32[256,256]{1,0:T(8,128)S(1)}, f32[256,256]{1,0:T(8,128)S(1)}) custom-call(f32[8,128]{1,0:T(8,128)S(1)} %get-tuple-element.31.refs_0_.wide_ref, f32[256,256]{1,0:T(8,128)S(1)} %get-tuple-element.44.schur_ref, f32[256,256]{1,0:T(8,128)S(1)} %get-tuple-element.45.t_ref, f32[256,256]{1,0:T(8,128)S(1)} %get-tuple-element.46.et_ref.refs_3_, ...), custom_call_target="tpu_custom_call" | custom-call | flops 3000000000 | bytes 9000000 | tf_op jit(solution)/shard_map/pallas_call | solution.py:243
  45.1 5.1 %collective-permute-start.8 = (f32[256,256]{1,0:T(8,128)S(1)}, f32[256,256]{1,0:T(8,128)S(1)}, u32[]{:S(2)}, u32[]{:S(2)}) collective-permute-start(f32[256,256]{1,0:T(8,128)S(1)} %get-tuple-element.51.refs_5_), channel_id=1, source_target_pairs={{0,12},{4,8},{8,4},{12,0},{16,28},{20,24},{24,20},{28,16},{32,44},... | collective-permute-start | bytes 786440 | tf_op jit(solution)/shard_map/ppermute | solution.py:266
  50.3 0.0 collective-permute-done.2.refs_1_
  50.3 3.2 %shard_map.55 = (f32[256,256]{1,0:T(8,128)S(1)}, f32[256,256]{1,0:T(8,128)S(1)}, f32[8,128]{1,0:T(8,128)S(1)}, f32[384,128]{1,0:T(8,128)S(1)}) custom-call(f32[384,128]{1,0:T(8,128)S(1)} %get-tuple-element.39.refs_0_, f32[384,128]{1,0:T(8,128)S(1)} %collective-permute-done.2.refs_1_), custom_call_target="tpu_custom_call" | custom-call | flops 6000000000 | bytes 18000000 | tf_op jit(solution)/shard_map/pallas_call | solution.py:243
  53.5 1.9 %collective-permute-start.3 = (f32[384,128]{1,0:T(8,128)S(1)}, f32[384,128]{1,0:T(8,128)S(1)}, u32[]{:S(2)}, u32[]{:S(2)}) collective-permute-start(f32[384,128]{1,0:T(8,128)S(1)} %get-tuple-element.43), channel_id=1, source_target_pairs={{0,12},{4,8},{8,4},{12,0},{16,28},{20,24},{24,20},{28,16},{32,44},... | collective-permute-start | bytes 589832 | tf_op jit(solution)/shard_map/ppermute | solution.py:266
  55.4 1.4 %shard_map.58 = (f32[768,512]{1,0:T(8,128)S(1)}, bf16[768,256]{1,0:T(8,128)(2,1)S(1)}, bf16[768,256]{1,0:T(8,128)(2,1)S(1)}, f32[64,768]{1,0:T(8,128)}) custom-call(f32[768,256]{1,0:T(8,128)S(1)} %copy-done.1, f32[256,768]{1,0:T(8,128)S(1)} %all_gather.6.refs_2_.refs_0_.refs_1_, f32[768,512]{1,0:T(8,128)S(1)} %copy-done, ...), custom_call_target="tpu_custom_call" | custom-call | flops 4000000000 | bytes 12000000 | tf_op jit(solution)/shard_map/pallas_call | solution.py:243
  56.8 0.0 collective-permute-done.7.refs_6_
  56.8 3.0 %collective-permute-done.8.refs_7_ = f32[256,256]{1,0:T(8,128)S(1)} collective-permute-done((f32[256,256]{1,0:T(8,128)S(1)}, f32[256,256]{1,0:T(8,128)S(1)}, u32[]{:S(2)}, u32[]{:S(2)}) %collective-permute-start.8) | collective-permute-done | bytes 262176 | tf_op jit(solution)/shard_map/ppermute | solution.py:266
  59.8 3.6 %collective-permute-done.3.refs_3_ = f32[384,128]{1,0:T(8,128)S(1)} collective-permute-done((f32[384,128]{1,0:T(8,128)S(1)}, f32[384,128]{1,0:T(8,128)S(1)}, u32[]{:S(2)}, u32[]{:S(2)}) %collective-permute-start.3) | collective-permute-done | bytes 196640 | tf_op jit(solution)/shard_map/ppermute | solution.py:266
  63.4 3.7 %shard_map.59 = f32[768,512]{1,0:T(8,128)} custom-call(f32[8,128]{1,0:T(8,128)S(1)} %get-tuple-element.40.refs_0_, f32[256,256]{1,0:T(8,128)S(1)} %get-tuple-element.41.refs_1_, f32[256,256]{1,0:T(8,128)S(1)} %get-tuple-element.42.refs_2_, f32[384,128]{1,0:T(8,128)S(1)} %collective-permute-done.3.refs_3_, f32[256,256]{1,0:T(8,128)S(1)} %get-tuple-element.49.refs_4_, ...), custom_call_target="tpu_custom_call" | custom-call | flops 7000000000 | bytes 21000000 | tf_op jit(solution)/shard_map/pallas_call | solution.py:243
  (9 shorter events, 0.0 us)
Async XLA Ops:
  4.4 13.5 %collective-permute-start = (f32[64,768]{1,0:T(8,128)}, f32[64,768]{1,0:T(8,128)S(1)}, u32[]{:S(2)}, u32[]{:S(2)}) collective-permute-start(f32[64,768]{1,0:T(8,128)} %get-tuple-element.33), channel_id=1, source_target_pairs={{0,2},{1,3},{2,0},{3,1},{4,6},{5,7},{6,4},{7,5},{8,10},{9,11},{10,... | collective-permute-start | bytes 589832 | tf_op jit(solution)/shard_map/ppermute | solution.py:266
  12.0 29.7 %collective-permute-start.4 = (f32[256,512]{1,0:T(8,128)}, f32[256,512]{1,0:T(8,128)S(1)}, u32[]{:S(2)}, u32[]{:S(2)}) collective-permute-start(f32[256,512]{1,0:T(8,128)} %get-tuple-element.36.refs_2_.y_ref), channel_id=1, source_target_pairs={{0,4},{4,0},{8,12},{12,8},{16,20},{20,16},{24,28},{28,24},{32,36},... | collective-permute-start | bytes 1572872 | tf_op jit(solution)/shard_map/ppermute | solution.py:266
  13.9 1.0 %copy-start.3 = (f32[256,256]{1,0:T(8,128)S(1)}, f32[256,256]{1,0:T(8,128)}, u32[]{:S(2)}) copy-start(f32[256,256]{1,0:T(8,128)} %get-tuple-element.30.refs_0_.refs_3_.refs_1_) | copy-start | bytes 786436
  14.9 3.0 %copy-start.4 = (f32[64,768]{1,0:T(8,128)S(1)}, f32[64,768]{1,0:T(8,128)}, u32[]{:S(2)}) copy-start(f32[64,768]{1,0:T(8,128)} %get-tuple-element.33) | copy-start | bytes 589828
  17.9 2.6 %copy-start.1 = (f32[768,256]{1,0:T(8,128)S(1)}, f32[768,256]{1,0:T(8,128)}, u32[]{:S(2)}) copy-start(f32[768,256]{1,0:T(8,128)} %refs_0_.3) | copy-start | bytes 2359300
  20.5 5.5 %copy-start = (f32[768,512]{1,0:T(8,128)S(1)}, f32[768,512]{1,0:T(8,128)}, u32[]{:S(2)}) copy-start(f32[768,512]{1,0:T(8,128)} %refs_2_.3) | copy-start | bytes 4718596
  20.5 5.5 %copy-start.2 = (f32[256,512]{1,0:T(8,128)S(1)}, f32[256,512]{1,0:T(8,128)}, u32[]{:S(2)}) copy-start(f32[256,512]{1,0:T(8,128)} %get-tuple-element.36.refs_2_.y_ref) | copy-start | bytes 1572868
  22.0 11.4 %collective-permute-start.1 = (f32[256,256]{1,0:T(8,128)S(1)}, f32[256,256]{1,0:T(8,128)S(1)}, u32[]{:S(2)}, u32[]{:S(2)}) collective-permute-start(f32[256,256]{1,0:T(8,128)S(1)} %get-tuple-element.35), channel_id=1, source_target_pairs={{0,4},{4,0},{8,12},{12,8},{16,20},{20,16},{24,28},{28,24},{32,36},... | collective-permute-start | bytes 786440 | tf_op jit(solution)/shard_map/ppermute | solution.py:266
  27.6 14.1 %collective-permute-start.5 = (f32[256,256]{1,0:T(8,128)S(1)}, f32[256,256]{1,0:T(8,128)S(1)}, u32[]{:S(2)}, u32[]{:S(2)}) collective-permute-start(f32[256,256]{1,0:T(8,128)S(1)} %get-tuple-element.48), channel_id=1, source_target_pairs={{0,4},{4,0},{8,12},{12,8},{16,20},{20,16},{24,28},{28,24},{32,36},... | collective-permute-start | bytes 786440 | tf_op jit(solution)/shard_map/ppermute | solution.py:266
  29.5 14.8 %collective-permute-start.6 = (f32[256,256]{1,0:T(8,128)S(1)}, f32[256,256]{1,0:T(8,128)S(1)}, u32[]{:S(2)}, u32[]{:S(2)}) collective-permute-start(f32[256,256]{1,0:T(8,128)S(1)} %get-tuple-element.50), channel_id=1, source_target_pairs={{0,4},{4,0},{8,12},{12,8},{16,20},{20,16},{24,28},{28,24},{32,36},... | collective-permute-start | bytes 786440 | tf_op jit(solution)/shard_map/ppermute | solution.py:266
  38.2 12.1 %collective-permute-start.2 = (f32[384,128]{1,0:T(8,128)S(1)}, f32[384,128]{1,0:T(8,128)S(1)}, u32[]{:S(2)}, u32[]{:S(2)}) collective-permute-start(f32[384,128]{1,0:T(8,128)S(1)} %get-tuple-element.39.refs_0_), channel_id=1, source_target_pairs={{0,4},{4,0},{8,12},{12,8},{16,20},{20,16},{24,28},{28,24},{32,36},... | collective-permute-start | bytes 589832 | tf_op jit(solution)/shard_map/ppermute | solution.py:266
  42.3 14.5 %collective-permute-start.7 = (f32[256,256]{1,0:T(8,128)S(1)}, f32[256,256]{1,0:T(8,128)S(1)}, u32[]{:S(2)}, u32[]{:S(2)}) collective-permute-start(f32[256,256]{1,0:T(8,128)S(1)} %get-tuple-element.49.refs_4_), channel_id=1, source_target_pairs={{0,12},{4,8},{8,4},{12,0},{16,28},{20,24},{24,20},{28,16},{32,44},... | collective-permute-start | bytes 786440 | tf_op jit(solution)/shard_map/ppermute | solution.py:266
  45.1 14.6 %collective-permute-start.8 = (f32[256,256]{1,0:T(8,128)S(1)}, f32[256,256]{1,0:T(8,128)S(1)}, u32[]{:S(2)}, u32[]{:S(2)}) collective-permute-start(f32[256,256]{1,0:T(8,128)S(1)} %get-tuple-element.51.refs_5_), channel_id=1, source_target_pairs={{0,12},{4,8},{8,4},{12,0},{16,28},{20,24},{24,20},{28,16},{32,44},... | collective-permute-start | bytes 786440 | tf_op jit(solution)/shard_map/ppermute | solution.py:266
  53.5 9.9 %collective-permute-start.3 = (f32[384,128]{1,0:T(8,128)S(1)}, f32[384,128]{1,0:T(8,128)S(1)}, u32[]{:S(2)}, u32[]{:S(2)}) collective-permute-start(f32[384,128]{1,0:T(8,128)S(1)} %get-tuple-element.43), channel_id=1, source_target_pairs={{0,12},{4,8},{8,4},{12,0},{16,28},{20,24},{24,20},{28,16},{32,44},... | collective-permute-start | bytes 589832 | tf_op jit(solution)/shard_map/ppermute | solution.py:266
